TPU v7x, 256 devices: a whole 4x4x8 slice. The times are simulated.
256 devices in a mesh: bucket: 64 (over x, z, y_lo), replica: 4 (over y_hi, core).
Axes of the slice: x: 4, y: 4 (y_hi: 2, y_lo: 2; y = y_hi * 2 + y_lo), z: 8, core: 2. Of those that a mesh axis runs over, the one named last changes fastest.
Arguments:
- left_embed: float32 [4, 32768, 400], P('replica', 'bucket'), may hold values from -2.4 to 2.4
- right_embed: float32 [4, 32768, 400], P('replica', 'bucket'), may hold values from -2.4 to 2.4
- right_state: float32 [4, 32768], P('replica', 'bucket'), may hold values from 0.001 to 0.01
- relation_embed: float32 [2066, 400], replicated, may hold values from -3 to 3
- relation_state: float32 [2066], replicated, may hold values from 0.001 to 0.01
- source_rows: int32 [4, 64, 2, 1000], P('replica', 'bucket'), may hold values from 0 to 511
- target_rows: int32 [4, 64, 2, 1000], P('replica', 'bucket'), may hold values from 0 to 511
- relation_ids: int32 [4, 64, 2, 1000], P('replica', 'bucket'), may hold values from 0 to 2065
- negative_rows: int32 [4, 64, 2, 500], P('replica', 'bucket'), may hold values from 0 to 511
Outputs:
- right_out: float32 [4, 32768, 400], P('replica', 'bucket')
- state_out: float32 [4, 32768], P('replica', 'bucket')
- relation_out: float32 [2066, 400], replicated
- relation_state_out: float32 [2066], replicated
All inputs are finite; a program needn't handle non-finite values.
Results may differ from a plain program's by a relative error of at most 0.00045.
The roundings to bfloat16 on the way count: a program that leaves them out, or rounds other values in their place, can miss the bound.
Values may be sent and summed in bfloat16 or wider, within the bound.
No kernel may reach another device: no remote copies, remote signals or barrier semaphores. Data moves between devices by JAX's collectives and lax.ppermute only.
A program may use at most 64 MiB of HBM per device.

v0:
```python
import jax
import jax.numpy as jnp
from jax import lax
from jax.sharding import PartitionSpec as P


def passed_along(block, axis, distance):
    devices = range(lax.axis_size(axis))
    route = [((i - distance) % len(devices), i) for i in devices]
    return lax.ppermute(block, axis, route)


def one_hot(index, count):
    return (index[:, None] == jnp.arange(count, dtype=jnp.int32)[None, :]).astype(jnp.bfloat16)


def pick_rows(index, table_low):
    return jnp.dot(
        one_hot(index, table_low.shape[0]), table_low, preferred_element_type=jnp.float32
    ).astype(jnp.bfloat16)


def edge_terms(heads, slab, rel_low, dst, rel, neg):
    rows = slab.shape[0]
    half = slab.shape[1] // 2
    negatives = neg.shape[0]
    slab_low = slab.astype(jnp.bfloat16)
    pos_rows = pick_rows(dst, slab_low)
    neg_rows = pick_rows(neg, slab_low)
    rel_rows = pick_rows(rel, rel_low).astype(jnp.float32)
    head_vals = heads.astype(jnp.float32)
    real_part = head_vals[:, :half] * rel_rows[:, :half] - head_vals[:, half:] * rel_rows[:, half:]
    imag_part = head_vals[:, :half] * rel_rows[:, half:] + head_vals[:, half:] * rel_rows[:, :half]
    prod = jnp.concatenate([real_part, imag_part], 1).astype(jnp.bfloat16)
    pos = jnp.sum(prod.astype(jnp.float32) * pos_rows.astype(jnp.float32), 1)
    neg_scores = jnp.einsum("ed,nd->en", prod, neg_rows, preferred_element_type=jnp.float32)
    g_pos = -jax.nn.sigmoid(-pos)
    g_neg = (jax.nn.sigmoid(neg_scores) / negatives).astype(jnp.bfloat16)
    d_pos = (g_pos[:, None] * prod.astype(jnp.float32)).astype(jnp.bfloat16)
    d_neg = jnp.einsum("en,ed->nd", g_neg, prod, preferred_element_type=jnp.float32).astype(
        jnp.bfloat16
    )
    d_prod = g_pos[:, None] * pos_rows.astype(jnp.float32) + jnp.dot(
        g_neg, neg_rows, preferred_element_type=jnp.float32
    )
    d_real = d_prod[:, :half] * head_vals[:, :half] + d_prod[:, half:] * head_vals[:, half:]
    d_imag = d_prod[:, half:] * head_vals[:, :half] - d_prod[:, :half] * head_vals[:, half:]
    d_rel = jnp.concatenate([d_real, d_imag], 1).astype(jnp.bfloat16)
    grad = jnp.einsum("er,ed->rd", one_hot(dst, rows), d_pos, preferred_element_type=jnp.float32)
    grad = grad + jnp.einsum(
        "nr,nd->rd", one_hot(neg, rows), d_neg, preferred_element_type=jnp.float32
    )
    rel_grad = jnp.einsum(
        "ek,ed->kd", one_hot(rel, rel_low.shape[0]), d_rel, preferred_element_type=jnp.float32
    )
    return (grad, rel_grad)


def adagrad(table, state, grad, rate):
    new_state = state + jnp.mean(grad * grad, axis=-1)
    return (table - rate * grad / jnp.sqrt(new_state)[..., None], new_state)


def per_device(
    left_embed,
    right_embed,
    right_state,
    relation_embed,
    relation_state,
    source_rows,
    target_rows,
    relation_ids,
    negative_rows,
):
    left_low = left_embed[0].astype(jnp.bfloat16)
    slab = right_embed[0]
    state = right_state[0]
    rel_low = relation_embed.astype(jnp.bfloat16)
    src = source_rows[0, 0]
    dst = target_rows[0, 0]
    rel = relation_ids[0, 0]
    neg = negative_rows[0, 0]
    heads_first = pick_rows(src[0], left_low)
    grad, rel_first = edge_terms(heads_first, slab, rel_low, dst[0], rel[0], neg[0])
    slab, state = adagrad(slab, state, grad, 0.1)
    heads_second = pick_rows(src[1], left_low)
    moved, moved_state = passed_along((slab, state), "bucket", 1)
    grad, rel_second = edge_terms(heads_second, moved, rel_low, dst[1], rel[1], neg[1])
    moved, moved_state = adagrad(moved, moved_state, grad, 0.1)
    slab, state = passed_along((moved, moved_state), "bucket", -1)
    rel_total = lax.psum(rel_first + rel_second, ("bucket", "replica"))
    relation_out, relation_state_out = adagrad(relation_embed, relation_state, rel_total, 0.2)
    return (slab[None], state[None], relation_out, relation_state_out)


def solution(mesh):
    in_specs = (
        P("replica", "bucket", None),
        P("replica", "bucket", None),
        P("replica", "bucket"),
        P(),
        P(),
        P("replica", "bucket", None, None),
        P("replica", "bucket", None, None),
        P("replica", "bucket", None, None),
        P("replica", "bucket", None, None),
    )
    out_specs = (P("replica", "bucket", None), P("replica", "bucket"), P(), P())
    return jax.shard_map(
        per_device, mesh=mesh, in_specs=in_specs, out_specs=out_specs, check_vma=False
    )
```

profile of v0, /device:TPU:1, one launch (start us, length us, event | category | flops | bytes accessed | tf_op | source)
XLA Modules:
  0.0 345.8 jit_solution(8602083683917653313)
XLA Ops:
  7.2 0.8 fusion.73
  8.0 0.8 fusion.71
  8.8 0.8 fusion.70
  9.5 0.8 fusion.72
  10.3 1.8 convolution_convert_fusion.3
  12.2 1.9 fusion.24
  14.2 2.3 fusion.28
  16.9 0.7 copy-done.5
  17.6 1.7 fusion.16
  19.3 2.0 multiply_convert_fusion.1
  21.3 3.4 fusion.33
  24.8 2.0 multiply_reduce_fusion.2
  26.8 2.2 collective-permute-start.1
  29.2 1.8 collective-permute-start
  31.0 0.8 fusion.22
  32.9 1.6 copy-done.2
  34.4 2.3 fusion.30
  37.2 17.8 %collective-permute-done = f32[512,400]{0,1:T(8,128)S(1)} collective-permute-done((f32[512,400]{0,1:T(8,128)S(1)}, f32[512,400]{0,1:T(8,128)S(1)}, u32[]{:S(2)}, u32[]{:S(2)}) %collective-permute-start) | collective-permute-done | bytes 819232 | tf_op jit(solution)/shard_map/ppermute | solution.py:10
  54.9 0.8 fusion.19
  56.4 1.0 multiply_convert_fusion
  58.5 2.5 fusion
  61.0 4.3 %fusion.4 = f32[2066,400]{0,1:T(8,128)} fusion(f32[2066,400]{0,1:T(8,128)S(1)} %fusion, s32[1000]{0:T(1024)S(1)} %bitcast.56, bf16[1000,200]{0,1:T(8,128)(2,1)S(1)} %get-tuple-element.11, bf16[1000,200]{0,1:T(8,128)(2,1)S(1)} %get-tuple-element.10), kind=kOutput, calls=%fused_computation.6 | convolution fusion | flops 1657292416 | bytes 7415200 | tf_op jit(solution)/shard_map/ek,ed->kd/dot_general | solution.py:53
  65.4 2.3 fusion.34
  67.7 2.3 multiply_reduce_fusion.1
  70.0 1.3 divide_subtract_fusion.1
  71.4 1.2 collective-permute-start.2
  72.6 2.0 collective-permute-start.3
  74.6 17.2 %collective-permute-done.3 = f32[512]{0:T(512)S(1)} collective-permute-done((f32[512]{0:T(512)S(1)}, f32[512]{0:T(512)S(1)}, u32[]{:S(2)}, u32[]{:S(2)}) %collective-permute-start.3) | collective-permute-done | bytes 2080 | tf_op jit(solution)/shard_map/ppermute | solution.py:10
  91.8 239.2 %all-reduce.2.cloned.1.call-done = f32[2066,400]{0,1:T(8,128)} async-done(((f32[2066,400]{0,1:T(8,128)}), f32[2066,400]{0,1:T(8,128)}) %all-reduce.2.cloned.1.call-update) | async-done | bytes 3305616 | tf_op jit(solution)/shard_map/psum | solution.py:91
  331.0 2.4 multiply_reduce_fusion
  334.1 2.3 divide_subtract_fusion
  336.3 2.1 copy.16
  (44 shorter events, 5.0 us)
Async XLA Ops:
  7.2 323.9 %all-reduce.2.cloned.1.call-start = ((), (), s32[]{:S(2)}) async-start(), calls=%async_computation | async-start | bytes 6963200 | tf_op jit(solution)/shard_map/psum | solution.py:91
  10.3 3.8 %copy-start.1 = (f32[2066,400]{0,1:T(8,128)S(1)}, f32[2066,400]{0,1:T(8,128)}, u32[]{:S(2)}) copy-start(f32[2066,400]{0,1:T(8,128)} %param.12) | copy-start | bytes 9916804
  16.5 1.1 copy-start.5
  16.9 2.5 copy-start.11
  24.8 2.0 copy-start.13
  26.8 4.2 %copy-start.4 = (f32[1,512,400]{1,2,0:T(8,128)S(1)}, f32[1,512,400]{1,2,0:T(8,128)}, u32[]{:S(2)}) copy-start(f32[1,512,400]{1,2,0:T(8,128)} %param.9) | copy-start | bytes 2457604
  26.8 43.2 %collective-permute-start.1 = (f32[512]{0:T(512)S(1)}, f32[512]{0:T(512)S(1)}, u32[]{:S(2)}, u32[]{:S(2)}) collective-permute-start(f32[512]{0:T(512)S(1)} %get-tuple-element.9), channel_id=1, source_target_pairs={{252,0},{0,4},{4,8},{8,12},{12,16},{16,20},{20,24},{24,28},{28,32}... | collective-permute-start | bytes 6152 | tf_op jit(solution)/shard_map/ppermute | solution.py:10
  29.2 2.6 copy-start.7
  29.2 2.6 copy-start.8
  29.2 25.7 %collective-permute-start = (f32[512,400]{0,1:T(8,128)S(1)}, f32[512,400]{0,1:T(8,128)S(1)}, u32[]{:S(2)}, u32[]{:S(2)}) collective-permute-start(f32[512,400]{0,1:T(8,128)S(1)} %bitcast_subtract_fusion), channel_id=1, source_target_pairs={{252,0},{0,4},{4,8},{8,12},{12,16},{16,20},{20,24},{24,28},{28,32}... | collective-permute-start | bytes 2457608 | tf_op jit(solution)/shard_map/ppermute | solution.py:10
  32.4 2.0 copy-start.2
  37.1 28.2 %copy-start.9 = (bf16[1000,200]{0,1:T(8,128)(2,1)}, bf16[1000,200]{0,1:T(8,128)(2,1)S(1)}, u32[]{:S(2)}) copy-start(bf16[1000,200]{0,1:T(8,128)(2,1)S(1)} %get-tuple-element.14) | copy-start | bytes 1200004
  37.2 28.2 %copy-start.10 = (bf16[1000,200]{0,1:T(8,128)(2,1)}, bf16[1000,200]{0,1:T(8,128)(2,1)S(1)}, u32[]{:S(2)}) copy-start(bf16[1000,200]{0,1:T(8,128)(2,1)S(1)} %get-tuple-element.15) | copy-start | bytes 1200004
  54.9 0.9 copy-start.6
  67.7 266.3 %copy-start.3 = (f32[2066,400]{0,1:T(8,128)S(1)}, f32[2066,400]{0,1:T(8,128)}, u32[]{:S(2)}) copy-start(f32[2066,400]{0,1:T(8,128)} %param.12) | copy-start | bytes 9916804
  71.4 20.4 %collective-permute-start.2 = (f32[512,400]{0,1:T(8,128)S(1)}, f32[512,400]{0,1:T(8,128)}, u32[]{:S(2)}, u32[]{:S(2)}) collective-permute-start(f32[512,400]{0,1:T(8,128)S(1)} %divide_subtract_fusion.1), channel_id=1, source_target_pairs={{4,0},{8,4},{12,8},{16,12},{20,16},{24,20},{28,24},{32,28},{36,32}... | collective-permute-start | bytes 2457608 | tf_op jit(solution)/shard_map/ppermute | solution.py:10
  72.6 19.2 %collective-permute-start.3 = (f32[512]{0:T(512)S(1)}, f32[512]{0:T(512)S(1)}, u32[]{:S(2)}, u32[]{:S(2)}) collective-permute-start(f32[512]{0:T(512)S(1)} %get-tuple-element.7), channel_id=1, source_target_pairs={{4,0},{8,4},{12,8},{16,12},{20,16},{24,20},{28,24},{32,28},{36,32}... | collective-permute-start | bytes 6152 | tf_op jit(solution)/shard_map/ppermute | solution.py:10
  91.8 241.6 %copy-start.12 = (f32[2066]{0:T(1024)S(1)}, f32[2066]{0:T(1024)}, u32[]{:S(2)}) copy-start(f32[2066]{0:T(1024)} %param.13) | copy-start | bytes 24796
  331.0 3.0 copy-start
Sparse Core Ops, SparseCore 0:
  65.5 265.5 all-reduce.1
where the time goes:
time: 348 us; the launch traced here: 346 us
  waiting for transfers between devices  274 us (79%)
  matrix products  33.5 us (10%)
  between operations  14.3 us (4%)
  other arithmetic  8.43 us (2%)
  local copies, waits for them, and re-layouts  8.19 us (2%)
  starting transfers between devices  7.19 us (2%)
    psum x1, waiting for transfers between devices, per_device(): rel_total = lax.psum(rel_first + rel_second, ('bucket', 'replica'))  239 us
    ppermute x4, waiting for transfers between devices, passed_along(): return lax.ppermute(block, axis, route)  35 us
    dot_general x8, matrix products, pick_rows(): jnp.dot(one_hot(index, table_low.shape[0]), table_low, preferred_element_...  12.3 us
    ppermute x4, starting transfers between devices, passed_along(): return lax.ppermute(block, axis, route)  7.16 us
  transfers between devices with their start and end apart: 5, of which 3 were waited for; matrix products, arithmetic and copies ran while one was open for 6% of the time, Pallas kernels for 0%

commit v1 on v0

--- a/solution.py
+++ b/solution.py
@@ -4,10 +4,55 @@
 from jax.sharding import PartitionSpec as P
 
 
-def passed_along(block, axis, distance):
-    devices = range(lax.axis_size(axis))
-    route = [((i - distance) % len(devices), i) for i in devices]
-    return lax.ppermute(block, axis, route)
+BUCKET = ("x", "z", "y_lo")
+REPLICA = ("y_hi", "core")
+PLANE = ("x", "y_lo", "y_hi")
+HALF = 200
+WIDE = 256
+PART = 144
+LEVELS = 32000.0
+
+
+def from_next(block):
+    count = lax.axis_size(BUCKET)
+    return lax.ppermute(block, BUCKET, [((i + 1) % count, i) for i in range(count)])
+
+
+def swap_core(block):
+    return lax.ppermute(block, "core", [(0, 1), (1, 0)])
+
+
+def encode(block):
+    lane = lax.broadcasted_iota(jnp.int32, block.shape, block.ndim - 1)
+    top = jnp.max(jnp.abs(block), axis=-1, keepdims=True)
+    power = jnp.ceil(jnp.log2(jnp.maximum(top, 1e-30)))
+    code = jnp.round(block * (LEVELS * jnp.exp2(-power)))
+    return jnp.where(lane < HALF, code, power).astype(jnp.int16)
+
+
+def decode(code):
+    lane = lax.broadcasted_iota(jnp.int32, code.shape, code.ndim - 1)
+    wide = code.astype(jnp.float32)
+    step = jnp.exp2(wide[..., HALF : HALF + 1]) * (1.0 / LEVELS)
+    return jnp.where(lane < HALF, wide * step, 0.0)
+
+
+def to_all(block, axes):
+    count = lax.axis_size(axes)
+    copies = jnp.broadcast_to(block[None], (count, *block.shape))
+    return lax.all_to_all(copies, axes, 0, 0, tiled=True)
+
+
+def summed_over_devices(mine, other):
+    total = mine + swap_core(other)
+    parts = encode(total).reshape(16, PART, WIDE)
+    total = jnp.sum(decode(lax.all_to_all(parts, PLANE, 0, 0, tiled=True)), 0)
+    total = jnp.sum(decode(to_all(encode(total), "z")), 0)
+    ours = to_all(encode(total), PLANE).reshape(16 * PART, WIDE)
+    theirs = swap_core(ours)
+    first = lax.axis_index("core") == 0
+    real, imag = jnp.where(first, ours, theirs), jnp.where(first, theirs, ours)
+    return jnp.concatenate([decode(real)[:, :HALF], decode(imag)[:, :HALF]], 1)
 
 
 def one_hot(index, count):
@@ -61,6 +106,10 @@
     return (table - rate * grad / jnp.sqrt(new_state)[..., None], new_state)
 
 
+def padded(half):
+    return jnp.pad(half, ((0, 16 * PART - half.shape[0]), (0, WIDE - HALF)))
+
+
 def per_device(
     left_embed,
     right_embed,
@@ -73,39 +122,50 @@
     negative_rows,
 ):
     left_low = left_embed[0].astype(jnp.bfloat16)
+    blocks = jnp.concatenate(
+        [source_rows[0, 0], target_rows[0, 0], relation_ids[0, 0], negative_rows[0, 0]], 1
+    )
+    left_next = from_next(left_low)
+    block_next = from_next(blocks[1])
     slab = right_embed[0]
     state = right_state[0]
     rel_low = relation_embed.astype(jnp.bfloat16)
-    src = source_rows[0, 0]
-    dst = target_rows[0, 0]
-    rel = relation_ids[0, 0]
-    neg = negative_rows[0, 0]
-    heads_first = pick_rows(src[0], left_low)
-    grad, rel_first = edge_terms(heads_first, slab, rel_low, dst[0], rel[0], neg[0])
-    slab, state = adagrad(slab, state, grad, 0.1)
-    heads_second = pick_rows(src[1], left_low)
-    moved, moved_state = passed_along((slab, state), "bucket", 1)
-    grad, rel_second = edge_terms(heads_second, moved, rel_low, dst[1], rel[1], neg[1])
-    moved, moved_state = adagrad(moved, moved_state, grad, 0.1)
-    slab, state = passed_along((moved, moved_state), "bucket", -1)
-    rel_total = lax.psum(rel_first + rel_second, ("bucket", "replica"))
+    edges = source_rows.shape[-1]
+
+    def train(left, slab, state, block):
+        src, dst, rel = (block[i * edges : (i + 1) * edges] for i in range(3))
+        heads = pick_rows(src, left)
+        grad, rel_grad = edge_terms(heads, slab, rel_low, dst, rel, block[3 * edges :])
+        slab, state = adagrad(slab, state, grad, 0.1)
+        return slab, state, rel_grad
+
+    slab, state, rel_first = train(left_low, slab, state, blocks[0])
+    slab, state, rel_second = train(left_next, slab, state, block_next)
+    rel_sum = rel_first + rel_second
+    real, imag = padded(rel_sum[:, :HALF]), padded(rel_sum[:, HALF:])
+    first = lax.axis_index("core") == 0
+    mine, other = jnp.where(first, real, imag), jnp.where(first, imag, real)
+    rel_total = summed_over_devices(mine, other)[: relation_embed.shape[0]]
     relation_out, relation_state_out = adagrad(relation_embed, relation_state, rel_total, 0.2)
     return (slab[None], state[None], relation_out, relation_state_out)
 
 
 def solution(mesh):
+    split = jax.sharding.Mesh(
+        mesh.devices.reshape(4, 8, 2, 2, 2), ("x", "z", "y_lo", "y_hi", "core")
+    )
     in_specs = (
-        P("replica", "bucket", None),
-        P("replica", "bucket", None),
-        P("replica", "bucket"),
+        P(REPLICA, BUCKET, None),
+        P(REPLICA, BUCKET, None),
+        P(REPLICA, BUCKET),
         P(),
         P(),
-        P("replica", "bucket", None, None),
-        P("replica", "bucket", None, None),
-        P("replica", "bucket", None, None),
-        P("replica", "bucket", None, None),
+        P(REPLICA, BUCKET, None, None),
+        P(REPLICA, BUCKET, None, None),
+        P(REPLICA, BUCKET, None, None),
+        P(REPLICA, BUCKET, None, None),
     )
-    out_specs = (P("replica", "bucket", None), P("replica", "bucket"), P(), P())
+    out_specs = (P(REPLICA, BUCKET, None), P(REPLICA, BUCKET), P(), P())
     return jax.shard_map(
-        per_device, mesh=mesh, in_specs=in_specs, out_specs=out_specs, check_vma=False
+        per_device, mesh=split, in_specs=in_specs, out_specs=out_specs, check_vma=False
     )

time: 348 us -> 145 us (0.42)
  waiting for transfers between devices: 274 us -> 4.16 us
  blocking collectives: 0 us -> 60.1 us
  between operations: 14.3 us -> 1.09 us
  starting transfers between devices: 7.19 us -> 15.8 us
  other arithmetic: 8.43 us -> 15.5 us
  local copies, waits for them, and re-layouts: 8.19 us -> 12.5 us
    psum x1 -> x0, waiting for transfers between devices: 239 us -> none  [per_device(): rel_total = lax.psum(rel_first + rel_second, ('bucket', 'replica'))]
    all_to_all x0 -> x3, blocking collectives: none -> 60.1 us  [the longest x2 37.6 us: to_all(): return lax.all_to_all(copies, axes, 0, 0, tiled=True)]
    ppermute x4, waiting for transfers between devices: 35 us -> 4.16 us  [the longest x2 4.16 us: swap_core(): return lax.ppermute(block, 'core', [(0, 1), (1, 0)])]
    ppermute x4, starting transfers between devices: 7.16 us -> 15.8 us  [the longest x2 9.86 us: from_next(): lax.ppermute(block, BUCKET, [((i + 1) % count, i) for i in range(count)])]
    convert_element_type x0 -> x7, other arithmetic: none -> 4.46 us  [the longest x1 1.93 us: per_device(): left_low = left_embed[0].astype(jnp.bfloat16)]
  transfers between devices with their start and end apart: 5 -> 4, of which waited for: 3 -> 1; matrix products, arithmetic and copies ran while one was open for 6% -> 25% of each run, Pallas kernels for 0% -> 0%
where the time goes in v1:
time: 145 us
  blocking collectives  60.1 us (41%)
  matrix products  35.6 us (25%)
  starting transfers between devices  15.8 us (11%)
  other arithmetic  15.5 us (11%)
  local copies, waits for them, and re-layouts  12.5 us (9%)
  waiting for transfers between devices  4.16 us (3%)
    all_to_all x2, blocking collectives, to_all(): return lax.all_to_all(copies, axes, 0, 0, tiled=True)  37.6 us
    all_to_all x1, blocking collectives, summed_over_devices(): total = jnp.sum(decode(lax.all_to_all(parts, PLANE, 0, 0, tiled=True)), 0)  22.5 us
    dot_general x8, matrix products, pick_rows(): jnp.dot(one_hot(index, table_low.shape[0]), table_low, preferred_element_...  14 us
    ppermute x2, starting transfers between devices, from_next(): lax.ppermute(block, BUCKET, [((i + 1) % count, i) for i in range(count)])  9.86 us
    dot_general x2, matrix products, edge_terms(): jnp.einsum('ek,ed->kd', one_hot(rel, rel_low.shape[0]), d_rel, preferred_...  6.83 us
    dot_general x2, matrix products, edge_terms(): jnp.einsum('nr,nd->rd', one_hot(neg, rows), d_neg, preferred_element_type...  6.17 us
    ppermute x2, starting transfers between devices, swap_core(): return lax.ppermute(block, 'core', [(0, 1), (1, 0)])  5.91 us
    unnamed x24, local copies, waits for them, and re-layouts  4.5 us
  transfers between devices with their start and end apart: 4, of which 1 were waited for; matrix products, arithmetic and copies ran while one was open for 25% of the time, Pallas kernels for 0%

profile of v1, /device:TPU:1, one launch (start us, length us, event | category | flops | bytes accessed | tf_op | source)
XLA Modules:
  0.0 144.7 jit_solution(18135901110693965598)
XLA Ops:
  0.6 0.9 concatenate.23
  1.6 9.7 %collective-permute-start = (s32[3500]{0:T(1024)S(1)}, s32[3500]{0:T(1024)S(1)}, u32[]{:S(2)}, u32[]{:S(2)}) collective-permute-start(s32[3500]{0:T(1024)S(1)} %slice_reduce_fusion), channel_id=1, source_target_pairs={{4,0},{8,4},{12,8},{16,12},{20,16},{24,20},{28,24},{32,28},{36,32}... | collective-permute-start | bytes 42008 | tf_op jit(solution)/shard_map/ppermute | solution.py:18
  11.3 1.9 %convert_bitcast_fusion = bf16[512,400]{0,1:T(8,128)(2,1)} fusion(f32[1,512,400]{1,2,0:T(8,128)} %param.9), kind=kLoop, calls=%fused_computation.110 | loop fusion | flops 204800 | bytes 1228800 | tf_op jit(solution)/shard_map/convert_element_type | solution.py:124
  16.4 1.8 %fusion.27 = f32[1000,400]{0,1:T(8,128)S(1)} fusion(bf16[512,400]{0,1:T(8,128)(2,1)} %convert_bitcast_fusion, s32[1000]{0:T(1024)S(1)} %bitcast.70), kind=kOutput, calls=%fused_computation.52 | convolution fusion | flops 410912000 | bytes 2013600 | tf_op jit(solution)/shard_map/dot_general | solution.py:63
  18.8 2.3 %fusion.31 = f32[1000,400]{0,1:T(8,128)S(1)} fusion(s32[1000]{0:T(1024)S(1)} %bitcast.66, f32[2066,400]{0,1:T(8,128)S(1)} %copy-done), kind=kOutput, calls=%fused_computation.56 | convolution fusion | flops 1656492416 | bytes 4909600 | tf_op jit(solution)/shard_map/dot_general | solution.py:63
  21.5 1.7 %fusion.19 = (f32[1000]{0:T(1024)S(1)}, bf16[1000,400]{0,1:T(8,128)(2,1)}) fusion(bf16[1000,200]{0,1:T(8,128)(2,1)S(1)} %get-tuple-element.15, bf16[1000,200]{0,1:T(8,128)(2,1)S(1)} %get-tuple-element.14, s32[1000]{0:T(1024)S(1)} %bitcast.68, f32[1,512,400]{1,2,0:T(8,128)S(1)} %copy-done.2), kind=kOutput, calls=%fused_computation.44 | convolution fusion | flops 412911008 | bytes 2427200 | tf_op jit(solution)/shard_map/dot_general | solution.py:63
  23.2 2.0 %multiply_convert_fusion.1 = bf16[1000,500]{1,0:T(8,128)(2,1)} fusion(bf16[500,400]{0,1:T(8,128)(2,1)S(1)} %convolution_convert_fusion.3, bf16[1000,200]{0,1:T(8,128)(2,1)S(1)} %get-tuple-element.15, bf16[1000,200]{0,1:T(8,128)(2,1)S(1)} %get-tuple-element.14), kind=kOutput, calls=%fused_computation.29 | convolution fusion | flops 404100000 | bytes 2200000 | tf_op jit(solution)/shard_map/ed,nd->en/dot_general | solution.py:81
  25.2 3.0 %fusion.36 = f32[512,400]{0,1:T(8,128)} fusion(bf16[1000,500]{1,0:T(8,128)(2,1)} %multiply_convert_fusion.1, s32[500]{0:T(512)S(1)} %bitcast.63, bf16[1000,200]{0,1:T(8,128)(2,1)} %copy-done.6, bf16[1000,200]{0,1:T(8,128)(2,1)S(1)} %get-tuple-element.14), kind=kOutput, calls=%fused_computation.65 | convolution fusion | flops 606856000 | bytes 2621200 | tf_op jit(solution)/shard_map/nr,nd->rd/dot_general | solution.py:95
  28.2 2.1 %fusion.20 = f32[1000,400]{0,1:T(8,128)S(1)} fusion(bf16[1000,400]{0,1:T(8,128)(2,1)} %get-tuple-element.33, bf16[1000,500]{1,0:T(8,128)(2,1)} %multiply_convert_fusion.1, bf16[500,400]{0,1:T(8,128)(2,1)S(1)} %convolution_convert_fusion.3, f32[1000]{0:T(1024)S(1)} %divide_negate_fusion.1), kind=kOutput, calls=%fused_computation.45 | convolution fusion | flops 401200000 | bytes 3804000 | tf_op jit(solution)/shard_map/dot_general | solution.py:88
  32.3 4.2 %fusion.2 = f32[2066,400]{0,1:T(8,128)} fusion(s32[1000]{0:T(1024)S(1)} %bitcast.67, bf16[1000,200]{0,1:T(8,128)(2,1)S(1)} %get-tuple-element.11, bf16[1000,200]{0,1:T(8,128)(2,1)S(1)} %get-tuple-element.10), kind=kOutput, calls=%fused_computation.4 | convolution fusion | flops 1656466048 | bytes 4109600 | tf_op jit(solution)/shard_map/ek,ed->kd/dot_general | solution.py:98
  37.5 4.5 %fusion.33 = f32[1000,400]{0,1:T(8,128)S(1)} fusion(s32[1000]{0:T(1024)S(1)} %get-tuple-element.19, f32[2066,400]{0,1:T(8,128)} %param.12), kind=kOutput, calls=%fused_computation.58 | convolution fusion | flops 1656492416 | bytes 4909600 | tf_op jit(solution)/shard_map/dot_general | solution.py:63
  42.0 1.8 %fusion.25 = f32[1000,400]{0,1:T(8,128)S(1)} fusion(bf16[512,400]{0,1:T(8,128)(2,1)} %collective-permute-done.1, s32[1000]{0:T(1024)S(1)} %get-tuple-element.20), kind=kOutput, calls=%fused_computation.50 | convolution fusion | flops 410912000 | bytes 2013600 | tf_op jit(solution)/shard_map/dot_general | solution.py:63
  45.1 1.0 multiply_convert_fusion
  46.1 1.0 copy-done.3
  48.2 1.6 %copy-done.11 = f32[2066,400]{0,1:T(8,128)S(1)} copy-done((f32[2066,400]{0,1:T(8,128)S(1)}, f32[2066,400]{0,1:T(8,128)}, u32[]{:S(2)}) %copy-start.11) | copy-done | bytes 3305624
  49.7 2.6 %fusion.4 = f32[2066,400]{0,1:T(8,128)S(1)} fusion(f32[2066,400]{0,1:T(8,128)S(1)} %copy-done.11, s32[1000]{0:T(1024)S(1)} %get-tuple-element.19, bf16[1000,200]{0,1:T(8,128)(2,1)S(1)} %get-tuple-element.9, bf16[1000,200]{0,1:T(8,128)(2,1)S(1)} %get-tuple-element.8), kind=kOutput, calls=%fused_computation.6 | convolution fusion | flops 1657292416 | bytes 7415200 | tf_op jit(solution)/shard_map/ek,ed->kd/dot_general | solution.py:98
  52.8 1.3 collective-permute-start.2
  54.1 4.2 %collective-permute-done.2 = f32[2304,256]{0,1:T(8,128)S(1)} collective-permute-done((f32[2304,256]{0,1:T(8,128)S(1)}, f32[2304,256]{0,1:T(8,128)S(1)}, u32[]{:S(2)}, u32[]{:S(2)}) %collective-permute-start.2) | collective-permute-done | bytes 2359328 | tf_op jit(solution)/shard_map/ppermute | solution.py:22
  58.7 0.9 select_convert_fusion
  59.6 1.1 copy.29
  60.7 22.5 %all_to_all.15 = s16[16,144,256]{2,1,0:T(8,128)(2,1)S(1)} all-to-all(s16[16,144,256]{2,1,0:T(8,128)(2,1)S(1)} %bitcast.53), channel_id=1, replica_groups=mesh['x'=4,'z'=8,'y_lo'=2,'y_hi'=2,'core'=2] {'x','y_lo','y_hi'}, dimensions={0} | all-to-all | bytes 2359296 | tf_op jit(solution)/shard_map/all_to_all | solution.py:49
  83.6 1.0 fusion.40
  85.5 18.6 %all_to_all.16 = s16[8,144,256]{2,1,0:T(8,128)(2,1)S(1)} all-to-all(s16[8,144,256]{2,1,0:T(8,128)(2,1)S(1)} %broadcast_in_dim.35), channel_id=1, replica_groups=mesh['x'=4,'z'=8,'y_lo'=2,'y_hi'=2,'core'=2] {'z'}, dimensions={0} | all-to-all | bytes 1179648 | tf_op jit(solution)/shard_map/all_to_all | solution.py:43
  104.1 1.2 copy.30
  105.5 1.5 %select_reduce_fusion.1 = f32[144,256]{0,1:T(8,128)S(1)} fusion(f32[8,144]{1,0:T(8,128)S(1)} %fusion.73, pred[256]{0:T(512)(128)(4,1)S(1)} %iota_compare_fusion.48, s16[8,144,256]{1,0,2:T(8,128)(2,1)S(1)} %copy.30), kind=kLoop, calls=%fused_computation.20 | loop fusion | flops 1142784 | bytes 742144 | tf_op jit(solution)/shard_map/reduce_sum | solution.py:50
  107.4 19.0 %all_to_all.17 = s16[16,144,256]{2,1,0:T(8,128)(2,1)S(1)} all-to-all(s16[16,144,256]{2,1,0:T(8,128)(2,1)S(1)} %broadcast_in_dim.41), channel_id=1, replica_groups=mesh['x'=4,'z'=8,'y_lo'=2,'y_hi'=2,'core'=2] {'x','y_lo','y_hi'}, dimensions={0} | all-to-all | bytes 2359296 | tf_op jit(solution)/shard_map/all_to_all | solution.py:43
  126.4 1.2 copy.33
  127.7 4.6 %collective-permute-start.3 = (s16[2304,256]{0,1:T(8,128)(2,1)S(1)}, s16[2304,256]{0,1:T(8,128)(2,1)S(1)}, u32[]{:S(2)}, u32[]{:S(2)}) collective-permute-start(s16[2304,256]{0,1:T(8,128)(2,1)S(1)} %copy.33), channel_id=1, source_target_pairs={{0,1},{1,0},{2,3},{3,2},{4,5},{5,4},{6,7},{7,6},{8,9},{9,8},{10,11... | collective-permute-start | bytes 3538952 | tf_op jit(solution)/shard_map/ppermute | solution.py:22
  132.3 3.1 %fusion.37 = f32[512,400]{0,1:T(8,128)} fusion(bf16[1000,500]{1,0:T(8,128)(2,1)} %copy-done.3, s32[500]{0:T(512)S(1)} %slice.169, bf16[1000,200]{0,1:T(8,128)(2,1)} %copy-done.5, bf16[1000,200]{0,1:T(8,128)(2,1)} %copy-done.4), kind=kOutput, calls=%fused_computation.66 | convolution fusion | flops 606856000 | bytes 2621200 | tf_op jit(solution)/shard_map/nr,nd->rd/dot_general | solution.py:95
  135.4 2.1 %multiply_reduce_fusion.1 = (f32[512]{0:T(512)S(1)}, f32[512,400]{0,1:T(8,128)S(1)}) fusion(f32[512,400]{0,1:T(8,128)} %fusion.37, f32[1000]{0:T(1024)S(1)} %divide_negate_fusion, bf16[1000,200]{0,1:T(8,128)(2,1)} %copy-done.5, bf16[1000,200]{0,1:T(8,128)(2,1)} %copy-done.4, s32[1000]{0:T(1024)S(1)} %get-tuple-element.18), kind=kOutput, calls=%fused_computation.98 | convolution fusion | flops 413125888 | bytes 2448448 | tf_op jit(solution)/shard_map/er,ed->rd/dot_general | solution.py:94
  138.1 1.1 subtract_bitcast_fusion
  142.5 2.2 %divide_subtract_fusion = f32[2066,400]{0,1:T(8,128)} fusion(f32[2066,400]{0,1:T(8,128)S(1)} %copy-done.1, f32[2304,200]{0,1:T(8,128)S(1)} %get-tuple-element.31, f32[2304,200]{0,1:T(8,128)S(1)} %get-tuple-element.30, f32[2066]{0:T(1024)S(1)} %get-tuple-element.4), kind=kLoop, calls=%fused_computation.12 | loop fusion | flops 3305600 | bytes 10305864 | tf_op jit(solution)/shard_map/sub | solution.py:106
  (71 shorter events, 15.9 us)
Async XLA Ops:
  0.6 17.6 %copy-start.2 = (f32[1,512,400]{1,2,0:T(8,128)S(1)}, f32[1,512,400]{1,2,0:T(8,128)}, u32[]{:S(2)}) copy-start(f32[1,512,400]{1,2,0:T(8,128)} %param.10) | copy-start | bytes 2457604
  1.6 35.1 %collective-permute-start = (s32[3500]{0:T(1024)S(1)}, s32[3500]{0:T(1024)S(1)}, u32[]{:S(2)}, u32[]{:S(2)}) collective-permute-start(s32[3500]{0:T(1024)S(1)} %slice_reduce_fusion), channel_id=1, source_target_pairs={{4,0},{8,4},{12,8},{16,12},{20,16},{24,20},{28,24},{32,28},{36,32}... | collective-permute-start | bytes 42008 | tf_op jit(solution)/shard_map/ppermute | solution.py:18
  13.2 5.5 %copy-start = (f32[2066,400]{0,1:T(8,128)S(1)}, f32[2066,400]{0,1:T(8,128)}, u32[]{:S(2)}) copy-start(f32[2066,400]{0,1:T(8,128)} %param.12) | copy-start | bytes 9916804
  13.2 28.7 %collective-permute-start.1 = (bf16[512,400]{0,1:T(8,128)(2,1)}, bf16[512,400]{0,1:T(8,128)(2,1)}, u32[]{:S(2)}, u32[]{:S(2)}) collective-permute-start(bf16[512,400]{0,1:T(8,128)(2,1)} %convert_bitcast_fusion), channel_id=1, source_target_pairs={{4,0},{8,4},{12,8},{16,12},{20,16},{24,20},{28,24},{32,28},{36,32}... | collective-permute-start | bytes 1228808 | tf_op jit(solution)/shard_map/ppermute | solution.py:18
  21.5 1.7 %copy-start.6 = (bf16[1000,200]{0,1:T(8,128)(2,1)}, bf16[1000,200]{0,1:T(8,128)(2,1)S(1)}, u32[]{:S(2)}) copy-start(bf16[1000,200]{0,1:T(8,128)(2,1)S(1)} %get-tuple-element.15) | copy-start | bytes 1200004
  30.3 1.0 copy-start.7
  30.3 1.3 copy-start.10
  31.6 0.7 copy-start.8
  44.2 0.9 copy-start.4
  44.2 0.9 copy-start.5
  46.1 1.0 copy-start.3
  47.7 2.0 %copy-start.11 = (f32[2066,400]{0,1:T(8,128)S(1)}, f32[2066,400]{0,1:T(8,128)}, u32[]{:S(2)}) copy-start(f32[2066,400]{0,1:T(8,128)} %fusion.2) | copy-start | bytes 9916804
  52.8 5.5 %collective-permute-start.2 = (f32[2304,256]{0,1:T(8,128)S(1)}, f32[2304,256]{0,1:T(8,128)S(1)}, u32[]{:S(2)}, u32[]{:S(2)}) collective-permute-start(f32[2304,256]{0,1:T(8,128)S(1)} %pad_select_fusion), channel_id=1, source_target_pairs={{0,1},{1,0},{2,3},{3,2},{4,5},{5,4},{6,7},{7,6},{8,9},{9,8},{10,11... | collective-permute-start | bytes 7077896 | tf_op jit(solution)/shard_map/ppermute | solution.py:22
  127.7 11.6 %collective-permute-start.3 = (s16[2304,256]{0,1:T(8,128)(2,1)S(1)}, s16[2304,256]{0,1:T(8,128)(2,1)S(1)}, u32[]{:S(2)}, u32[]{:S(2)}) collective-permute-start(s16[2304,256]{0,1:T(8,128)(2,1)S(1)} %copy.33), channel_id=1, source_target_pairs={{0,1},{1,0},{2,3},{3,2},{4,5},{5,4},{6,7},{7,6},{8,9},{9,8},{10,11... | collective-permute-start | bytes 3538952 | tf_op jit(solution)/shard_map/ppermute | solution.py:22
  140.5 0.7 copy-start.9
  140.5 2.0 %copy-start.1 = (f32[2066,400]{0,1:T(8,128)S(1)}, f32[2066,400]{0,1:T(8,128)}, u32[]{:S(2)}) copy-start(f32[2066,400]{0,1:T(8,128)} %param.12) | copy-start | bytes 9916804

commit v2 on v0

v2 whole, which is shorter than its diff:
```python
import jax
import jax.numpy as jnp
from jax import lax
from jax.experimental import pallas as pl
from jax.experimental.pallas import tpu as pltpu
from jax.sharding import PartitionSpec as P

AXES = ("x", "z_hi", "z_lo", "y_lo", "y_hi", "core")
BUCKET = ("x", "z_hi", "z_lo", "y_lo")
REPLICA = ("y_hi", "core")
CUBE = ("x", "z_lo", "y_lo", "y_hi")
OWNERS = 32
D = 400
HALF = 200
WIDE = 256
FULL = 2 * WIDE
EDGES = 1000
EPAD = 1024
NEG = 500
NPAD = 512
ROWS = 512
NREL = 2066
PART = 72
RPAD = OWNERS * PART
LEVELS = 32000.0
F32 = jnp.float32
BF16 = jnp.bfloat16


def struct(shape, dtype):
    return jax.ShapeDtypeStruct(shape, dtype)


def call(kernel, out_shape, *args, scratch=(), name):
    return pl.pallas_call(
        kernel,
        out_shape=out_shape,
        scratch_shapes=scratch,
        compiler_params=pltpu.CompilerParams(vmem_limit_bytes=60 * 1024 * 1024),
        name=name,
    )(*args)


def from_next(block):
    count = lax.axis_size(BUCKET)
    return lax.ppermute(block, BUCKET, [((i + 1) % count, i) for i in range(count)])


def swap_core(block):
    return lax.ppermute(block, "core", [(0, 1), (1, 0)])


def dot(a, b, dims=((1,), (0,))):
    return lax.dot_general(a, b, (dims, ((), ())), preferred_element_type=F32)


def spread(rows):
    gap = jnp.zeros((rows.shape[0], WIDE - HALF), rows.dtype)
    return jnp.concatenate([rows[:, :HALF], gap, rows[:, HALF:], gap], 1)


def as_column(row):
    return jnp.transpose(jnp.broadcast_to(row, (8, row.shape[1])))[:, :1]


def picks(column, count):
    at = lax.broadcasted_iota(jnp.int32, (column.shape[0], count), 1)
    return jnp.where(at == column, 1.0, 0.0).astype(BF16)


def places(row, count, start=0):
    at = lax.broadcasted_iota(jnp.int32, (count, row.shape[1]), 0) + start
    return jnp.where(at == row, 1.0, 0.0).astype(BF16)


def edge_terms(left, slab, table, ids):
    cols = jnp.transpose(ids)
    src, dst, rel, neg = (cols[:, i : i + 1] for i in range(4))
    slab_low = slab.astype(BF16)
    heads = dot(picks(src, ROWS), left)
    rel_rows = dot(picks(rel, RPAD), table)
    h_re, h_im = heads[:, :WIDE], heads[:, WIDE:]
    r_re, r_im = rel_rows[:, :WIDE], rel_rows[:, WIDE:]
    prod = jnp.concatenate([h_re * r_re - h_im * r_im, h_re * r_im + h_im * r_re], 1).astype(BF16)
    prod_wide = prod.astype(F32)
    pos_rows = dot(picks(dst, ROWS), slab_low)
    neg_rows = dot(picks(neg[:NPAD], ROWS), slab_low).astype(BF16)
    pos = jnp.sum(prod_wide * pos_rows, 1, keepdims=True)
    g_pos = -jax.nn.sigmoid(-pos)
    g_neg = (jax.nn.sigmoid(dot(prod, neg_rows, ((1,), (1,)))) * (1.0 / NEG)).astype(BF16)
    d_pos = (g_pos * prod_wide).astype(BF16)
    d_prod = g_pos * pos_rows + dot(g_neg, neg_rows)
    p_re, p_im = d_prod[:, :WIDE], d_prod[:, WIDE:]
    d_rel = jnp.concatenate([p_re * h_re + p_im * h_im, p_im * h_re - p_re * h_im], 1)
    return prod, g_neg, d_pos, d_rel.astype(BF16)


def trained(slab, state, ids, prod, g_neg, d_pos):
    d_neg = dot(g_neg, prod, ((0,), (0,))).astype(BF16)
    grad = dot(places(ids[1:2], ROWS), d_pos) + dot(places(ids[3:4, :NPAD], ROWS), d_neg)
    state = state + jnp.sum(grad * grad, 1, keepdims=True) * (1.0 / D)
    return slab - grad * (0.1 * lax.rsqrt(state)), state


def prepare_kernel(left, src, dst, rel, neg, left_low, ids):
    left_low[...] = spread(left[...]).astype(BF16)
    ids[...] = jnp.full(ids.shape, -1, jnp.int32)
    for step in range(2):
        for place, source in enumerate((src, dst, rel, neg)):
            ids[step, place : place + 1, : source.shape[1]] = source[step : step + 1, :]


def first_kernel(left, slab, state, relation, ids, slab_out, state_out, d_rel_out, table_out):
    table_out[:NREL, :] = spread(relation[...]).astype(BF16)
    table_out[NREL:, :] = jnp.zeros((RPAD - NREL, FULL), BF16)
    slab_wide = spread(slab[...])
    prod, g_neg, d_pos, d_rel = edge_terms(left[...], slab_wide, table_out[...], ids[0])
    d_rel_out[...] = d_rel
    slab_out[...], state_out[...] = trained(
        slab_wide, as_column(state[...]), ids[0], prod, g_neg, d_pos
    )


def rel_half(core, ids, ids_next, d_rel, d_rel_next):
    at = pl.multiple_of(core * WIDE, WIDE)
    return dot(places(ids[0, 2:3], RPAD), d_rel[:, pl.ds(at, WIDE)]) + dot(
        places(ids_next[2:3], RPAD), d_rel_next[:, pl.ds(at, WIDE)]
    )


def second_kernel(core, left, slab, table, ids, ids_next, d_rel, prod, g_neg, d_pos, d_rel_next, other):
    prod[...], g_neg[...], d_pos[...], d_rel_next[...] = edge_terms(
        left[...], slab[...], table[...], ids_next[...]
    )
    other[...] = rel_half(1 - core[0], ids, ids_next, d_rel, d_rel_next)


def finish_kernel(core, slab, state, ids, ids_next, d_rel, prod, g_neg, d_pos, d_rel_next, mine, slab_out, state_out):
    mine[...] = rel_half(core[0], ids, ids_next, d_rel, d_rel_next)
    new_slab, new_state = trained(
        slab[...], state[...], ids_next[...], prod[...], g_neg[...], d_pos[...]
    )
    slab_out[:, :HALF] = new_slab[:, :HALF]
    slab_out[:, HALF:] = new_slab[:, WIDE : WIDE + HALF]
    state_out[...] = jnp.transpose(jnp.broadcast_to(new_state, (ROWS, 128)))[:1]


def encode(total):
    top = jnp.max(jnp.abs(total), axis=1, keepdims=True)
    power = jnp.ceil(jnp.log2(jnp.maximum(top, 1e-30)))
    codes = jnp.round(total * (LEVELS * jnp.exp2(-power)))
    lane = lax.broadcasted_iota(jnp.int32, total.shape, 1)
    codes = jnp.where(lane < HALF, codes, power)
    return jnp.concatenate([codes[:, :128], codes[:, 128:]], 0).astype(jnp.int32).astype(jnp.int16)


def decode(codes):
    wide = codes.astype(jnp.int32).astype(F32)
    low, high = wide[:PART], wide[PART:]
    step = jnp.exp2(high[:, 127:128]) * (1.0 / LEVELS)
    lane = lax.broadcasted_iota(jnp.int32, high.shape, 1)
    return low * step, jnp.where(lane < HALF - 128, high * step, 0.0)


def send_kernel(mine, theirs, codes):
    def one(i, _):
        at = pl.ds(pl.multiple_of(i * PART, 8), PART)
        codes[i] = encode(mine[at, :] + theirs[at, :])
        return 0

    lax.fori_loop(0, OWNERS, one, 0)


def gather_kernel(parts, codes):
    low, high = decode(parts[0])
    for i in range(1, OWNERS):
        more = decode(parts[i])
        low, high = low + more[0], high + more[1]
    codes[...] = encode(jnp.concatenate([low, high], 1))


def spread_kernel(a, b, c, d, copies):
    a, b, c, d = (decode(part[...]) for part in (a, b, c, d))
    low, high = ((a[i] + c[i]) + (b[i] + d[i]) for i in range(2))
    code = encode(jnp.concatenate([low, high], 1))
    for i in range(OWNERS):
        copies[i] = code


def update_kernel(core, ours, theirs, relation, state, relation_out, state_out):
    first = core[0] == 0
    ours, theirs = decode(ours[0]), decode(theirs[0])
    total = jnp.sum(sum(part * part for part in (*ours, *theirs)), 1, keepdims=True)
    new_state = state[0] + total * (1.0 / D)
    rate = 0.2 * lax.rsqrt(new_state)
    ours, theirs = (jnp.concatenate(pair, 1) * rate for pair in (ours, theirs))
    real, imag = jnp.where(first, ours, theirs), jnp.where(first, theirs, ours)
    relation_out[:, :HALF] = relation[:, :HALF] - real[:, :HALF]
    relation_out[:, HALF:] = relation[:, HALF:] - imag[:, :HALF]
    state_out[0] = new_state


def per_device(
    left_embed,
    right_embed,
    right_state,
    relation_embed,
    relation_state,
    source_rows,
    target_rows,
    relation_ids,
    negative_rows,
):
    core = lax.axis_index("core").astype(jnp.int32)[None]
    smem = pl.BlockSpec(memory_space=pltpu.SMEM)
    vmem = pl.BlockSpec(memory_space=pltpu.VMEM)

    def with_core(kernel, out_shape, *args, name):
        return pl.pallas_call(
            kernel,
            out_shape=out_shape,
            in_specs=[smem] + [vmem] * len(args),
            compiler_params=pltpu.CompilerParams(vmem_limit_bytes=60 * 1024 * 1024),
            name=name,
        )(core, *args)

    left_low, ids = call(
        prepare_kernel,
        (struct((ROWS, FULL), BF16), struct((2, 8, EPAD), jnp.int32)),
        left_embed[0],
        source_rows[0, 0],
        target_rows[0, 0],
        relation_ids[0, 0],
        negative_rows[0, 0],
        name="prepare",
    )
    left_next = from_next(left_low)
    ids_next = from_next(ids[1])
    edge_array = struct((EPAD, FULL), BF16)
    half_array = struct((RPAD, WIDE), F32)
    slab, state, d_rel, table = call(
        first_kernel,
        (struct((ROWS, FULL), F32), struct((ROWS, 1), F32), edge_array, struct((RPAD, FULL), BF16)),
        left_low,
        right_embed[0],
        right_state,
        relation_embed,
        ids,
        name="first",
    )
    prod, g_neg, d_pos, d_rel_next, other = with_core(
        second_kernel,
        (edge_array, struct((EPAD, NPAD), BF16), edge_array, edge_array, half_array),
        left_next,
        slab,
        table,
        ids,
        ids_next,
        d_rel,
        name="second",
    )
    theirs = swap_core(other)
    mine, slab_out, state_out = with_core(
        finish_kernel,
        (half_array, struct((ROWS, D), F32), struct((1, ROWS), F32)),
        slab,
        state,
        ids,
        ids_next,
        d_rel,
        prod,
        g_neg,
        d_pos,
        d_rel_next,
        name="finish",
    )
    part = struct((2 * PART, 128), jnp.int16)
    parts = struct((OWNERS, 2 * PART, 128), jnp.int16)
    sent = call(send_kernel, parts, mine, theirs, name="send")
    got = lax.all_to_all(sent, CUBE, 0, 0, tiled=True)
    code = call(gather_kernel, part, got, name="gather")
    count = lax.axis_size("z_hi")
    ring = [
        lax.ppermute(code, "z_hi", [((i + k) % count, i) for i in range(count)])
        for k in range(1, count)
    ]
    copies = call(spread_kernel, parts, code, *ring, name="spread")
    ours = lax.all_to_all(copies, CUBE, 0, 0, tiled=True)
    theirs = swap_core(ours)
    block = pl.BlockSpec((1, 2 * PART, 128), lambda i: (i, 0, 0))
    rows = pl.BlockSpec((PART, D), lambda i: (i, 0))
    column = pl.BlockSpec((1, PART, 1), lambda i: (i, 0, 0))
    state_in = jnp.pad(relation_state, (0, RPAD - NREL), constant_values=1.0)
    relation_out, relation_state_out = pl.pallas_call(
        update_kernel,
        grid=(pl.cdiv(NREL, PART),),
        in_specs=[smem, block, block, rows, column],
        out_specs=(rows, column),
        out_shape=(struct((NREL, D), F32), struct((OWNERS, PART, 1), F32)),
        compiler_params=pltpu.CompilerParams(vmem_limit_bytes=60 * 1024 * 1024),
        name="update",
    )(core, ours, theirs, relation_embed, state_in.reshape(OWNERS, PART, 1))
    relation_state_out = relation_state_out.reshape(RPAD)[:NREL]
    return (slab_out[None], state_out, relation_out, relation_state_out)


def solution(mesh):
    split = jax.sharding.Mesh(mesh.devices.reshape(4, 4, 2, 2, 2, 2), AXES)
    in_specs = (
        P(REPLICA, BUCKET, None),
        P(REPLICA, BUCKET, None),
        P(REPLICA, BUCKET),
        P(),
        P(),
        P(REPLICA, BUCKET, None, None),
        P(REPLICA, BUCKET, None, None),
        P(REPLICA, BUCKET, None, None),
        P(REPLICA, BUCKET, None, None),
    )
    out_specs = (P(REPLICA, BUCKET, None), P(REPLICA, BUCKET), P(), P())
    return jax.shard_map(
        per_device, mesh=split, in_specs=in_specs, out_specs=out_specs, check_vma=False
    )
```

time: 348 us -> 163 us (0.47)
  waiting for transfers between devices: 274 us -> 3.72 us
  Pallas kernels: 0 us -> 69.5 us
  blocking collectives: 0 us -> 44.7 us
  matrix products: 33.5 us -> 0 us
  local copies, waits for them, and re-layouts: 8.19 us -> 23.7 us
  between operations: 14.3 us -> 0.69 us
  starting transfers between devices: 7.19 us -> 19.4 us
  other arithmetic: 8.43 us -> 0.61 us
    psum x1 -> x0, waiting for transfers between devices: 239 us -> none  [per_device(): rel_total = lax.psum(rel_first + rel_second, ('bucket', 'replica'))]
    pallas_call x0 -> x8, Pallas kernels: none -> 69.5 us  [the longest x5 25.9 us: call(): pl.pallas_call(kernel, out_shape=out_shape, scratch_shapes=scratch, compi...]
    all_to_all x0 -> x2, blocking collectives: none -> 44.7 us  [the longest x1 24 us: per_device(): got = lax.all_to_all(sent, CUBE, 0, 0, tiled=True)]
    dot_general x18 -> x0, matrix products: 33.5 us -> none  [the longest x8 12.3 us: pick_rows(): jnp.dot(one_hot(index, table_low.shape[0]), table_low, preferred_element_...]
    ppermute x4 -> x7, waiting for transfers between devices: 35 us -> 3.72 us  [the longest x3 3.71 us: per_device(): lax.ppermute(code, 'z_hi', [((i + k) % count, i) for i in range(count)])]
    unnamed x30 -> x29, local copies, waits for them, and re-layouts: 5.07 us -> 20.2 us
    ppermute x4 -> x7, starting transfers between devices: 7.16 us -> 19.4 us  [the longest x2 9.78 us: from_next(): lax.ppermute(block, BUCKET, [((i + 1) % count, i) for i in range(count)])]
    sub x3 -> x0, other arithmetic: 3.79 us -> none  [adagrad(): return (table - rate * grad / jnp.sqrt(new_state)[..., None], new_state)]
  transfers between devices with their start and end apart: 5 -> 7, of which waited for: 3 -> 1; matrix products, arithmetic and copies ran while one was open for 6% -> 7% of each run, Pallas kernels for 0% -> 13%
where the time goes in v2:
time: 163 us; the launch traced here: 162 us
  Pallas kernels  69.5 us (43%)
  blocking collectives  44.7 us (27%)
  local copies, waits for them, and re-layouts  23.7 us (15%)
  starting transfers between devices  19.4 us (12%)
  waiting for transfers between devices  3.72 us (2%)
    pallas_call x5, Pallas kernels, call(): pl.pallas_call(kernel, out_shape=out_shape, scratch_shapes=scratch, compi...  25.9 us
    all_to_all x1, blocking collectives, per_device(): got = lax.all_to_all(sent, CUBE, 0, 0, tiled=True)  24 us
    pallas_call x1, Pallas kernels, per_device(): pl.pallas_call(update_kernel, grid=(pl.cdiv(NREL, PART),), in_specs=[smem...  21.9 us
    pallas_call x2, Pallas kernels, with_core(): pl.pallas_call(kernel, out_shape=out_shape, in_specs=[smem] + [vmem] * le...  21.7 us
    all_to_all x1, blocking collectives, per_device(): ours = lax.all_to_all(copies, CUBE, 0, 0, tiled=True)  20.6 us
    unnamed x29, local copies, waits for them, and re-layouts  20.2 us
    ppermute x2, starting transfers between devices, from_next(): lax.ppermute(block, BUCKET, [((i + 1) % count, i) for i in range(count)])  9.78 us
    ppermute x3, starting transfers between devices, per_device(): lax.ppermute(code, 'z_hi', [((i + k) % count, i) for i in range(count)])  4.89 us
  transfers between devices with their start and end apart: 7, of which 1 were waited for; matrix products, arithmetic and copies ran while one was open for 7% of the time, Pallas kernels for 13%

profile of v2, /device:TPU:1, one launch (start us, length us, event | category | flops | bytes accessed | tf_op | source)
XLA Modules:
  0.0 162.3 jit_solution(8336033523540247652)
XLA Ops:
  0.6 2.5 %copy.19 = f32[1,512,400]{2,1,0:T(8,128)} copy(f32[1,512,400]{1,2,0:T(8,128)} %param.9) | data formatting | bytes 1638400 | tf_op args[0]
  3.1 2.2 %prepare.1 = (bf16[512,512]{1,0:T(8,128)(2,1)}, s32[2,8,1024]{2,1,0:T(8,128)}) custom-call(f32[512,400]{1,0:T(8,128)} %bitcast.11, s32[2,1000]{1,0:T(2,128)} %bitcast.15, s32[2,1000]{1,0:T(2,128)} %bitcast.16, s32[2,1000]{1,0:T(2,128)} %bitcast.17, s32[2,500]{1,0:T(2,128)} %bitcast.18), custom_call_target="tpu_custom_call" | custom-call | tf_op jit(solution)/shard_map/prepare/pallas_call | solution.py:35
  5.3 9.6 %collective-permute-start.1 = (bf16[512,512]{1,0:T(8,128)(2,1)}, bf16[512,512]{1,0:T(8,128)(2,1)S(1)}, u32[]{:S(2)}, u32[]{:S(2)}) collective-permute-start(bf16[512,512]{1,0:T(8,128)(2,1)} %get-tuple-element.20.left), channel_id=1, source_target_pairs={{4,0},{8,4},{12,8},{16,12},{20,16},{24,20},{28,24},{32,28},{36,32}... | collective-permute-start | bytes 1572872 | tf_op jit(solution)/shard_map/ppermute | solution.py:46
  14.9 0.8 slice_bitcast_fusion
  15.9 5.3 %copy.21.relation = f32[2066,400]{1,0:T(8,128)} copy(f32[2066,400]{0,1:T(8,128)} %param.12) | data formatting | bytes 6611200 | tf_op args[3]
  21.1 1.3 copy.20
  22.5 11.9 %first.1 = (f32[512,512]{1,0:T(8,128)}, f32[512,1]{1,0:T(8,128)}, bf16[1024,512]{1,0:T(8,128)(2,1)}, bf16[2304,512]{1,0:T(8,128)(2,1)}) custom-call(bf16[512,512]{1,0:T(8,128)(2,1)} %get-tuple-element.20.left, f32[512,400]{1,0:T(8,128)} %bitcast.12, f32[1,512]{1,0:T(1,128)} %state.1, f32[2066,400]{1,0:T(8,128)} %copy.21.relation, ...), custom_call_target="tpu_custom_call" | custom-call | tf_op jit(solution)/shard_map/first/pallas_call | solution.py:35
  34.5 0.6 copy-done.7
  35.0 0.2 copy-done.6
  35.3 12.9 %second.1 = (bf16[1024,512]{1,0:T(8,128)(2,1)}, bf16[1024,512]{1,0:T(8,128)(2,1)}, bf16[1024,512]{1,0:T(8,128)(2,1)}, bf16[1024,512]{1,0:T(8,128)(2,1)}, f32[2304,256]{1,0:T(8,128)}) custom-call(s32[1]{0:T(128)} %bitcast.core, bf16[512,512]{1,0:T(8,128)(2,1)} %copy-done.6, f32[512,512]{1,0:T(8,128)} %get-tuple-element.22.slab, ...), custom_call_target="tpu_custom_call" | custom-call | tf_op jit(solution)/shard_map/second/pallas_call | solution.py:219
  48.2 1.3 collective-permute-start.2
  49.4 8.7 %finish.1 = (f32[2304,256]{1,0:T(8,128)}, f32[512,400]{1,0:T(8,128)}, f32[1,512]{1,0:T(1,128)}) custom-call(s32[1]{0:T(128)} %bitcast.core, f32[512,512]{1,0:T(8,128)} %get-tuple-element.22.slab, f32[512,1]{1,0:T(8,128)} %get-tuple-element.23.state, s32[2,8,1024]{2,1,0:T(8,128)} %get-tuple-element.21.ids, s32[8,1024]{1,0:T(8,128)} %copy-done.7, ...), custom_call_target="tpu_custom_call" | custom-call | tf_op jit(solution)/shard_map/finish/pallas_call | solution.py:219
  58.2 1.5 copy-done.1
  59.7 7.1 %send.1 = s16[32,144,128]{2,1,0:T(8,128)(2,1)} custom-call(f32[2304,256]{1,0:T(8,128)} %get-tuple-element.32.mine, f32[2304,256]{1,0:T(8,128)} %copy-done.1), custom_call_target="tpu_custom_call" | custom-call | tf_op jit(solution)/shard_map/send/pallas_call | solution.py:35
  66.8 24.0 %all_to_all.10.parts = s16[32,144,128]{2,1,0:T(8,128)(2,1)} all-to-all(s16[32,144,128]{2,1,0:T(8,128)(2,1)} %send.1), channel_id=1, replica_groups=mesh['x'=4,'z_hi'=4,'z_lo'=2,'y_lo'=2,'y_hi'=2,'core'=2] {'x','z_lo','y_..., dimensions={0} | all-to-all | bytes 2359296 | tf_op jit(solution)/shard_map/all_to_all | solution.py:280
  90.9 2.4 %gather.1.a = s16[144,128]{1,0:T(8,128)(2,1)} custom-call(s16[32,144,128]{2,1,0:T(8,128)(2,1)} %all_to_all.10.parts), custom_call_target="tpu_custom_call" | custom-call | tf_op jit(solution)/shard_map/gather/pallas_call | solution.py:35
  93.3 1.6 %collective-permute-start.3 = (s16[144,128]{1,0:T(8,128)(2,1)}, s16[144,128]{1,0:T(8,128)(2,1)S(1)}, u32[]{:S(2)}, u32[]{:S(2)}) collective-permute-start(s16[144,128]{1,0:T(8,128)(2,1)} %gather.1.a), channel_id=1, source_target_pairs={{16,0},{32,16},{48,32},{0,48},{17,1},{33,17},{49,33},{1,49},{18,2}... | collective-permute-start | bytes 110600 | tf_op jit(solution)/shard_map/ppermute | solution.py:284
  94.9 0.9 collective-permute-start.4
  95.8 2.4 %collective-permute-start.5 = (s16[144,128]{1,0:T(8,128)(2,1)}, s16[144,128]{1,0:T(8,128)(2,1)S(1)}, u32[]{:S(2)}, u32[]{:S(2)}) collective-permute-start(s16[144,128]{1,0:T(8,128)(2,1)} %gather.1.a), channel_id=1, source_target_pairs={{48,0},{0,16},{16,32},{32,48},{49,1},{1,17},{17,33},{33,49},{50,2}... | collective-permute-start | bytes 110600 | tf_op jit(solution)/shard_map/ppermute | solution.py:284
  98.2 3.7 %collective-permute-done.4.c = s16[144,128]{1,0:T(8,128)(2,1)S(1)} collective-permute-done((s16[144,128]{1,0:T(8,128)(2,1)}, s16[144,128]{1,0:T(8,128)(2,1)S(1)}, u32[]{:S(2)}, u32[]{:S(2)}) %collective-permute-start.4) | collective-permute-done | bytes 36896 | tf_op jit(solution)/shard_map/ppermute | solution.py:284
  101.9 0.6 copy-done.9
  102.5 0.6 copy-done.10
  103.1 2.2 %spread.1 = s16[32,144,128]{2,1,0:T(8,128)(2,1)} custom-call(s16[144,128]{1,0:T(8,128)(2,1)} %gather.1.a, s16[144,128]{1,0:T(8,128)(2,1)} %copy-done.8, s16[144,128]{1,0:T(8,128)(2,1)} %copy-done.9, s16[144,128]{1,0:T(8,128)(2,1)} %copy-done.10), custom_call_target="tpu_custom_call" | custom-call | tf_op jit(solution)/shard_map/spread/pallas_call | solution.py:35
  105.3 20.6 %all_to_all.11.ours = s16[32,144,128]{2,1,0:T(8,128)(2,1)S(1)} all-to-all(s16[32,144,128]{2,1,0:T(8,128)(2,1)} %spread.1), channel_id=1, replica_groups=mesh['x'=4,'z_hi'=4,'z_lo'=2,'y_lo'=2,'y_hi'=2,'core'=2] {'x','z_lo','y_..., dimensions={0} | all-to-all | bytes 2359296 | tf_op jit(solution)/shard_map/all_to_all | solution.py:288
  125.9 3.5 %collective-permute-start.6 = (s16[32,144,128]{2,1,0:T(8,128)(2,1)S(1)}, s16[32,144,128]{2,1,0:T(8,128)(2,1)S(1)}, u32[]{:S(2)}, u32[]{:S(2)}) collective-permute-start(s16[32,144,128]{2,1,0:T(8,128)(2,1)S(1)} %all_to_all.11.ours), channel_id=1, source_target_pairs={{0,1},{1,0},{2,3},{3,2},{4,5},{5,4},{6,7},{7,6},{8,9},{9,8},{10,11... | collective-permute-start | bytes 3538952 | tf_op jit(solution)/shard_map/ppermute | solution.py:50
  129.4 2.1 %reshape.16.state = f32[32,72,1]{2,1,0:T(8,128)} reshape(f32[2304]{0:T(1024)S(1)} %pad.4) | data formatting | bytes 18432 | tf_op jit(solution)/shard_map/reshape | solution.py:302
  131.5 1.2 copy.24
  132.7 1.0 copy-done.3
  133.7 21.9 %update.1 = (f32[2066,400]{1,0:T(8,128)}, f32[32,72,1]{2,1,0:T(8,128)}) custom-call(s32[1]{0:T(128)} %bitcast.core, s16[32,144,128]{2,1,0:T(8,128)(2,1)} %copy-done, s16[32,144,128]{2,1,0:T(8,128)(2,1)} %copy-done.3, f32[2066,400]{1,0:T(8,128)} %copy.21.relation, f32[32,72,1]{2,1,0:T(8,128)} %reshape.16.state), custom_call_target="tpu_custom_call" | custom-call | tf_op jit(solution)/shard_map/update/pallas_call | solution.py:294
  155.6 5.4 %copy.25 = f32[2066,400]{0,1:T(8,128)} copy(f32[2066,400]{1,0:T(8,128)} %get-tuple-element.42) | data formatting | bytes 6611200
  161.0 0.6 reduce
  161.6 0.7 reshape.15
  (26 shorter events, 0.2 us)
Async XLA Ops:
  5.3 29.1 %collective-permute-start.1 = (bf16[512,512]{1,0:T(8,128)(2,1)}, bf16[512,512]{1,0:T(8,128)(2,1)S(1)}, u32[]{:S(2)}, u32[]{:S(2)}) collective-permute-start(bf16[512,512]{1,0:T(8,128)(2,1)} %get-tuple-element.20.left), channel_id=1, source_target_pairs={{4,0},{8,4},{12,8},{16,12},{20,16},{24,20},{28,24},{32,28},{36,32}... | collective-permute-start | bytes 1572872 | tf_op jit(solution)/shard_map/ppermute | solution.py:46
  15.7 18.8 %collective-permute-start = (s32[8,1024]{1,0:T(8,128)S(1)}, s32[8,1024]{1,0:T(8,128)S(1)}, u32[]{:S(2)}, u32[]{:S(2)}) collective-permute-start(s32[8,1024]{1,0:T(8,128)S(1)} %slice_bitcast_fusion), channel_id=1, source_target_pairs={{4,0},{8,4},{12,8},{16,12},{20,16},{24,20},{28,24},{32,28},{36,32}... | collective-permute-start | bytes 98312 | tf_op jit(solution)/shard_map/ppermute | solution.py:46
  15.9 5.3 %copy-start.5 = (f32[1,512,400]{1,2,0:T(8,128)S(1)}, f32[1,512,400]{1,2,0:T(8,128)}, u32[]{:S(2)}) copy-start(f32[1,512,400]{1,2,0:T(8,128)} %param.10) | copy-start | bytes 2457604
  34.4 0.6 copy-start.7
  34.5 0.8 copy-start.6
  48.2 10.0 %collective-permute-start.2 = (f32[2304,256]{1,0:T(8,128)}, f32[2304,256]{1,0:T(8,128)S(1)}, u32[]{:S(2)}, u32[]{:S(2)}) collective-permute-start(f32[2304,256]{1,0:T(8,128)} %get-tuple-element.33), channel_id=1, source_target_pairs={{0,1},{1,0},{2,3},{3,2},{4,5},{5,4},{6,7},{7,6},{8,9},{9,8},{10,11... | collective-permute-start | bytes 7077896 | tf_op jit(solution)/shard_map/ppermute | solution.py:50
  58.2 1.5 copy-start.1
  90.9 38.6 %copy-start.11 = (f32[2066]{0:T(1024)S(1)}, f32[2066]{0:T(1024)}, u32[]{:S(2)}) copy-start(f32[2066]{0:T(1024)} %param.13) | copy-start | bytes 24796
  93.3 38.2 %copy-start.4 = (f32[512,400]{1,0:T(8,128)S(1)}, f32[512,400]{1,0:T(8,128)}, u32[]{:S(2)}) copy-start(f32[512,400]{1,0:T(8,128)} %get-tuple-element.30) | copy-start | bytes 2457604
  93.3 4.9 %collective-permute-start.3 = (s16[144,128]{1,0:T(8,128)(2,1)}, s16[144,128]{1,0:T(8,128)(2,1)S(1)}, u32[]{:S(2)}, u32[]{:S(2)}) collective-permute-start(s16[144,128]{1,0:T(8,128)(2,1)} %gather.1.a), channel_id=1, source_target_pairs={{16,0},{32,16},{48,32},{0,48},{17,1},{33,17},{49,33},{1,49},{18,2}... | collective-permute-start | bytes 110600 | tf_op jit(solution)/shard_map/ppermute | solution.py:284
  94.9 7.0 %collective-permute-start.4 = (s16[144,128]{1,0:T(8,128)(2,1)}, s16[144,128]{1,0:T(8,128)(2,1)S(1)}, u32[]{:S(2)}, u32[]{:S(2)}) collective-permute-start(s16[144,128]{1,0:T(8,128)(2,1)} %gather.1.a), channel_id=1, source_target_pairs={{32,0},{48,16},{0,32},{16,48},{33,1},{49,17},{1,33},{17,49},{34,2}... | collective-permute-start | bytes 110600 | tf_op jit(solution)/shard_map/ppermute | solution.py:284
  95.8 6.1 %collective-permute-start.5 = (s16[144,128]{1,0:T(8,128)(2,1)}, s16[144,128]{1,0:T(8,128)(2,1)S(1)}, u32[]{:S(2)}, u32[]{:S(2)}) collective-permute-start(s16[144,128]{1,0:T(8,128)(2,1)} %gather.1.a), channel_id=1, source_target_pairs={{48,0},{0,16},{16,32},{32,48},{49,1},{1,17},{17,33},{33,49},{50,2}... | collective-permute-start | bytes 110600 | tf_op jit(solution)/shard_map/ppermute | solution.py:284
  98.2 3.7 %copy-start.8 = (s16[144,128]{1,0:T(8,128)(2,1)}, s16[144,128]{1,0:T(8,128)(2,1)S(1)}, u32[]{:S(2)}) copy-start(s16[144,128]{1,0:T(8,128)(2,1)S(1)} %collective-permute-done.3.b) | copy-start | bytes 110596
  101.9 0.6 copy-start.9
  102.5 0.6 copy-start.10
  125.9 6.8 %copy-start = (s16[32,144,128]{2,1,0:T(8,128)(2,1)}, s16[32,144,128]{2,1,0:T(8,128)(2,1)S(1)}, u32[]{:S(2)}) copy-start(s16[32,144,128]{2,1,0:T(8,128)(2,1)S(1)} %all_to_all.11.ours) | copy-start | bytes 3538948
  125.9 6.8 %collective-permute-start.6 = (s16[32,144,128]{2,1,0:T(8,128)(2,1)S(1)}, s16[32,144,128]{2,1,0:T(8,128)(2,1)S(1)}, u32[]{:S(2)}, u32[]{:S(2)}) collective-permute-start(s16[32,144,128]{2,1,0:T(8,128)(2,1)S(1)} %all_to_all.11.ours), channel_id=1, source_target_pairs={{0,1},{1,0},{2,3},{3,2},{4,5},{5,4},{6,7},{7,6},{8,9},{9,8},{10,11... | collective-permute-start | bytes 3538952 | tf_op jit(solution)/shard_map/ppermute | solution.py:50
  132.7 1.0 copy-start.3
  155.6 5.4 %copy-start.2 = (f32[32,72,1]{2,1,0:T(8,128)S(1)}, f32[32,72,1]{2,1,0:T(8,128)}, u32[]{:S(2)}) copy-start(f32[32,72,1]{2,1,0:T(8,128)} %get-tuple-element.35) | copy-start | bytes 27652

commit v3 on v2

v3 whole, which is shorter than its diff:
```python
import jax
import jax.numpy as jnp
from jax import lax
from jax.experimental import pallas as pl
from jax.experimental.pallas import tpu as pltpu
from jax.sharding import PartitionSpec as P

AXES = ("x", "z_hi", "z_lo", "y_lo", "y_hi", "core")
BUCKET = ("x", "z_hi", "z_lo", "y_lo")
REPLICA = ("y_hi", "core")
CUBE = ("x", "z_lo", "y_lo", "y_hi")
OWNERS = 32
D = 400
HALF = 200
EPAD = 1024
NEG = 500
NPAD = 512
ROWS = 512
NREL = 2066
RMAIN = 2048
RPAD = 2176
CUT = 104
PART = 112
LEVELS = 32000.0
F32 = jnp.float32
BF16 = jnp.bfloat16


def struct(shape, dtype):
    return jax.ShapeDtypeStruct(shape, dtype)


def call(kernel, out_shape, *args, scratch=(), name):
    return pl.pallas_call(
        kernel,
        out_shape=out_shape,
        scratch_shapes=scratch,
        compiler_params=pltpu.CompilerParams(vmem_limit_bytes=60 * 1024 * 1024),
        name=name,
    )(*args)


def from_next(block):
    count = lax.axis_size(BUCKET)
    return lax.ppermute(block, BUCKET, [((i + 1) % count, i) for i in range(count)])


def swap_core(block):
    return lax.ppermute(block, "core", [(0, 1), (1, 0)])


def dot(a, b, dims=((1,), (0,))):
    return lax.dot_general(a, b, (dims, ((), ())), preferred_element_type=F32)


def places(row, count):
    at = lax.broadcasted_iota(jnp.int32, (count, row.shape[1]), 0)
    return jnp.where(at == row, 1.0, 0.0).astype(BF16)


def edge_terms(left, slab, table, ids):
    slab_low = slab.astype(BF16)
    heads = dot(left, places(ids[0:1], ROWS))
    rel_rows = dot(table, places(ids[2:3], RPAD))
    h_re, h_im = heads[:HALF], heads[HALF:]
    r_re, r_im = rel_rows[:HALF], rel_rows[HALF:]
    prod = jnp.concatenate([h_re * r_re - h_im * r_im, h_re * r_im + h_im * r_re], 0).astype(BF16)
    prod_wide = prod.astype(F32)
    pos_rows = dot(slab_low, places(ids[1:2], ROWS))
    neg_rows = dot(slab_low, places(ids[3:4, :NPAD], ROWS)).astype(BF16)
    pos = jnp.sum(prod_wide * pos_rows, 0, keepdims=True)
    g_pos = -jax.nn.sigmoid(-pos)
    g_neg = (jax.nn.sigmoid(dot(neg_rows, prod, ((0,), (0,)))) * (1.0 / NEG)).astype(BF16)
    d_pos = (g_pos * prod_wide).astype(BF16)
    d_prod = g_pos * pos_rows + dot(neg_rows, g_neg)
    p_re, p_im = d_prod[:HALF], d_prod[HALF:]
    d_rel = (p_re * h_re + p_im * h_im, p_im * h_re - p_re * h_im)
    return prod, g_neg, d_pos, [part.astype(BF16) for part in d_rel]


def trained(slab, state, ids, prod, g_neg, d_pos):
    along = ((1,), (1,))
    d_neg = dot(prod, g_neg, along).astype(BF16)
    grad = dot(d_pos, places(ids[1:2], ROWS), along)
    grad = grad + dot(d_neg, places(ids[3:4, :NPAD], ROWS), along)
    state = state + jnp.sum(grad * grad, 0, keepdims=True) * (1.0 / D)
    return slab - grad * (0.1 * lax.rsqrt(state)), state


def prepare_kernel(left, src, dst, rel, neg, left_low, ids):
    left_low[...] = left[...].astype(BF16)
    ids[...] = jnp.full(ids.shape, -1, jnp.int32)
    for step in range(2):
        for place, source in enumerate((src, dst, rel, neg)):
            ids[step, place : place + 1, : source.shape[1]] = source[step : step + 1, :]


def first_kernel(left, slab, state, relation, ids, slab_out, state_out, d_rel_out, table_out):
    table_out[:, :RMAIN] = relation[:, :RMAIN].astype(BF16)
    table_out[:, RMAIN:] = jnp.zeros((D, RPAD - RMAIN), BF16)
    table_out[:, RMAIN:NREL] = relation[:, RMAIN:].astype(BF16)
    prod, g_neg, d_pos, d_rel = edge_terms(left[...], slab[...], table_out[...], ids[0])
    for half in range(2):
        d_rel_out[half] = d_rel[half]
    slab_out[...], state_out[...] = trained(slab[...], state[...], ids[0], prod, g_neg, d_pos)


def rel_half(half, ids, ids_next, d_rel, d_rel_next):
    along = ((1,), (1,))
    return dot(d_rel[half], places(ids[0, 2:3], RPAD), along) + dot(
        d_rel_next[half], places(ids_next[2:3], RPAD), along
    )


def second_kernel(core, left, slab, table, ids, ids_next, d_rel, prod, g_neg, d_pos, d_rel_next, other):
    prod[...], g_neg[...], d_pos[...], parts = edge_terms(
        left[...], slab[...], table[...], ids_next[...]
    )
    for half in range(2):
        d_rel_next[half] = parts[half]
    other[...] = rel_half(1 - core[0], ids, ids_next, d_rel, d_rel_next)


def finish_kernel(core, slab, state, ids, ids_next, d_rel, prod, g_neg, d_pos, d_rel_next, mine, slab_out, state_out):
    mine[...] = rel_half(core[0], ids, ids_next, d_rel, d_rel_next)
    slab_out[...], state_out[...] = trained(
        slab[...], state[...], ids_next[...], prod[...], g_neg[...], d_pos[...]
    )


def power_of(block):
    top = jnp.max(jnp.abs(block), axis=0, keepdims=True)
    return jnp.ceil(jnp.log2(jnp.maximum(top, 1e-30)))


def encode(main, last):
    lane = lax.broadcasted_iota(jnp.int32, last.shape, 1)
    row = lax.broadcasted_iota(jnp.int32, last.shape, 0)
    last = jnp.where(row < 7, last, 0.0)
    main_power, last_power = power_of(main), power_of(last)
    main = jnp.round(main * (LEVELS * jnp.exp2(-main_power)))
    last = jnp.round(last * (LEVELS * jnp.exp2(-last_power)))
    last_power = pltpu.roll(jnp.broadcast_to(last_power, last.shape), 64, 1)
    last = jnp.where(lane < 64, last, last_power)
    last = jnp.where(row == 7, jnp.broadcast_to(main_power, last.shape), last)
    fill = [jnp.zeros((CUT - main.shape[0], 128), F32)] if main.shape[0] < CUT else []
    return jnp.concatenate([main, *fill, last], 0).astype(jnp.int32).astype(jnp.int16)


def decode(codes):
    wide = codes.astype(jnp.int32).astype(F32)
    main, last = wide[:CUT], wide[CUT:]
    lane = lax.broadcasted_iota(jnp.int32, last.shape, 1)
    row = lax.broadcasted_iota(jnp.int32, last.shape, 0)
    main = main * (jnp.exp2(last[7:8]) * (1.0 / LEVELS))
    last_step = jnp.exp2(pltpu.roll(last, 64, 1)) * (1.0 / LEVELS)
    valid = jnp.logical_and(lane < NREL - RMAIN, row < 7)
    return main, jnp.where(valid, last * last_step, 0.0)


def place_of(part):
    tile, low = divmod(part, 2)
    rows = slice(CUT, HALF) if low else slice(0, CUT)
    return rows, slice(128 * tile, 128 * tile + 128)


def send_kernel(mine, theirs, codes, last):
    last[HALF:] = jnp.zeros((last.shape[0] - HALF, 128), F32)
    last[:HALF] = mine[:, RMAIN:] + theirs[:, RMAIN:]
    for part in range(OWNERS):
        at = place_of(part)
        codes[part] = encode(mine[at] + theirs[at], last[7 * part : 7 * part + 8])


def gather_kernel(parts, codes):
    main, last = decode(parts[0])
    for part in range(1, OWNERS):
        more = decode(parts[part])
        main, last = main + more[0], last + more[1]
    codes[...] = encode(main, last)


def spread_kernel(a, b, c, d, copies):
    a, b, c, d = (decode(part[...]) for part in (a, b, c, d))
    code = encode(*((a[i] + c[i]) + (b[i] + d[i]) for i in range(2)))
    for part in range(OWNERS):
        copies[part] = code


def update_kernel(core, ours, theirs, relation, state, relation_out, state_out, grads, last):
    for half, codes in enumerate((ours, theirs)):
        for part in range(OWNERS):
            rows, lanes = place_of(part)
            main, tail = decode(codes[part])
            grads[half, rows, lanes] = main[: rows.stop - rows.start]
            last[7 * part : 7 * part + 8] = tail
        grads[half, :, RMAIN:] = last[:HALF]
    both = grads[0], grads[1]
    total = sum(jnp.sum(part * part, 0, keepdims=True) for part in both)[:, :NREL]
    new_state = state[...] + total * (1.0 / D)
    rate = 0.2 * lax.rsqrt(new_state)
    real, imag = grads[core[0]], grads[1 - core[0]]
    relation_out[:HALF] = relation[:HALF] - real[:, :NREL] * rate
    relation_out[HALF:] = relation[HALF:] - imag[:, :NREL] * rate
    state_out[...] = new_state


def per_device(
    left_embed,
    right_embed,
    right_state,
    relation_embed,
    relation_state,
    source_rows,
    target_rows,
    relation_ids,
    negative_rows,
):
    core = lax.axis_index("core").astype(jnp.int32)[None]
    smem = pl.BlockSpec(memory_space=pltpu.SMEM)
    vmem = pl.BlockSpec(memory_space=pltpu.VMEM)

    def with_core(kernel, out_shape, *args, scratch=(), name):
        return pl.pallas_call(
            kernel,
            out_shape=out_shape,
            scratch_shapes=scratch,
            in_specs=[smem] + [vmem] * len(args),
            compiler_params=pltpu.CompilerParams(vmem_limit_bytes=60 * 1024 * 1024),
            name=name,
        )(core, *args)

    left_low, ids = call(
        prepare_kernel,
        (struct((D, ROWS), BF16), struct((2, 8, EPAD), jnp.int32)),
        left_embed[0].T,
        source_rows[0, 0],
        target_rows[0, 0],
        relation_ids[0, 0],
        negative_rows[0, 0],
        name="prepare",
    )
    left_next = from_next(left_low)
    ids_next = from_next(ids[1])
    relation = relation_embed.T
    slab_array, state_array = struct((D, ROWS), F32), struct((1, ROWS), F32)
    edge_array = struct((D, EPAD), BF16)
    pair_array = struct((2, HALF, EPAD), BF16)
    half_array = struct((HALF, RPAD), F32)
    slab, state, d_rel, table = call(
        first_kernel,
        (slab_array, state_array, pair_array, struct((D, RPAD), BF16)),
        left_low,
        right_embed[0].T,
        right_state,
        relation,
        ids,
        name="first",
    )
    prod, g_neg, d_pos, d_rel_next, other = with_core(
        second_kernel,
        (edge_array, struct((NPAD, EPAD), BF16), edge_array, pair_array, half_array),
        left_next,
        slab,
        table,
        ids,
        ids_next,
        d_rel,
        name="second",
    )
    theirs = swap_core(other)
    mine, slab_out, state_out = with_core(
        finish_kernel,
        (half_array, slab_array, state_array),
        slab,
        state,
        ids,
        ids_next,
        d_rel,
        prod,
        g_neg,
        d_pos,
        d_rel_next,
        name="finish",
    )
    part = struct((PART, 128), jnp.int16)
    parts = struct((OWNERS, PART, 128), jnp.int16)
    last = pltpu.VMEM((232, 128), F32)
    sent = call(send_kernel, parts, mine, theirs, scratch=[last], name="send")
    got = lax.all_to_all(sent, CUBE, 0, 0, tiled=True)
    code = call(gather_kernel, part, got, name="gather")
    count = lax.axis_size("z_hi")
    ring = [
        lax.ppermute(code, "z_hi", [((i + k) % count, i) for i in range(count)])
        for k in range(1, count)
    ]
    copies = call(spread_kernel, parts, code, *ring, name="spread")
    ours = lax.all_to_all(copies, CUBE, 0, 0, tiled=True)
    theirs = swap_core(ours)
    relation_out, relation_state_out = with_core(
        update_kernel,
        (struct((D, NREL), F32), struct((1, NREL), F32)),
        ours,
        theirs,
        relation,
        relation_state[None],
        scratch=[pltpu.VMEM((2, HALF, RPAD), F32), last],
        name="update",
    )
    return (slab_out.T[None], state_out, relation_out.T, relation_state_out[0])


def solution(mesh):
    split = jax.sharding.Mesh(mesh.devices.reshape(4, 4, 2, 2, 2, 2), AXES)
    in_specs = (
        P(REPLICA, BUCKET, None),
        P(REPLICA, BUCKET, None),
        P(REPLICA, BUCKET),
        P(),
        P(),
        P(REPLICA, BUCKET, None, None),
        P(REPLICA, BUCKET, None, None),
        P(REPLICA, BUCKET, None, None),
        P(REPLICA, BUCKET, None, None),
    )
    out_specs = (P(REPLICA, BUCKET, None), P(REPLICA, BUCKET), P(), P())
    return jax.shard_map(
        per_device, mesh=split, in_specs=in_specs, out_specs=out_specs, check_vma=False
    )
```

time: 163 us -> 118 us (0.72)
  Pallas kernels: 69.5 us -> 42.6 us
  local copies, waits for them, and re-layouts: 23.7 us -> 5.53 us
  blocking collectives: 44.7 us -> 39.8 us
  waiting for transfers between devices: 3.72 us -> 6.56 us
    pallas_call x3, Pallas kernels: 43.6 us -> 24.1 us  [with_core(): pl.pallas_call(kernel, out_shape=out_shape, scratch_shapes=scratch, in_sp...]
    unnamed x29 -> x18, local copies, waits for them, and re-layouts: 20.2 us -> 4.16 us
    pallas_call x5, Pallas kernels: 25.9 us -> 18.5 us  [call(): pl.pallas_call(kernel, out_shape=out_shape, scratch_shapes=scratch, compi...]
    all_to_all x1, blocking collectives: 24 us -> 20.9 us  [per_device(): got = lax.all_to_all(sent, CUBE, 0, 0, tiled=True)]
    reshape x2 -> x0, local copies, waits for them, and re-layouts: 2.76 us -> none  [the longest x1 2.07 us: per_device(): state_in.reshape(OWNERS, PART, 1)]
    ppermute x3, starting transfers between devices: 4.89 us -> 7.26 us  [per_device(): lax.ppermute(code, 'z_hi', [((i + k) % count, i) for i in range(count)])]
    all_to_all x1, blocking collectives: 20.6 us -> 18.8 us  [per_device(): ours = lax.all_to_all(copies, CUBE, 0, 0, tiled=True)]
  transfers between devices with their start and end apart: 7 -> 7, of which waited for: 1 -> 2; matrix products, arithmetic and copies ran while one was open for 7% -> 1% of each run, Pallas kernels for 13% -> 14%
where the time goes in v3:
time: 118 us; the launch traced here: 117 us
  Pallas kernels  42.6 us (36%)
  blocking collectives  39.8 us (34%)
  starting transfers between devices  20.8 us (18%)
  waiting for transfers between devices  6.56 us (6%)
  local copies, waits for them, and re-layouts  5.53 us (5%)
  other arithmetic  1.32 us (1%)
    pallas_call x3, Pallas kernels, with_core(): pl.pallas_call(kernel, out_shape=out_shape, scratch_shapes=scratch, in_sp...  24.1 us
    all_to_all x1, blocking collectives, per_device(): got = lax.all_to_all(sent, CUBE, 0, 0, tiled=True)  20.9 us
    all_to_all x1, blocking collectives, per_device(): ours = lax.all_to_all(copies, CUBE, 0, 0, tiled=True)  18.8 us
    pallas_call x5, Pallas kernels, call(): pl.pallas_call(kernel, out_shape=out_shape, scratch_shapes=scratch, compi...  18.5 us
    ppermute x2, starting transfers between devices, from_next(): lax.ppermute(block, BUCKET, [((i + 1) % count, i) for i in range(count)])  9.78 us
    ppermute x3, starting transfers between devices, per_device(): lax.ppermute(code, 'z_hi', [((i + k) % count, i) for i in range(count)])  7.26 us
    ppermute x3, waiting for transfers between devices, per_device(): lax.ppermute(code, 'z_hi', [((i + k) % count, i) for i in range(count)])  5.06 us
    unnamed x18, local copies, waits for them, and re-layouts  4.16 us
  transfers between devices with their start and end apart: 7, of which 2 were waited for; matrix products, arithmetic and copies ran while one was open for 1% of the time, Pallas kernels for 14%

profile of v3, /device:TPU:1, one launch (start us, length us, event | category | flops | bytes accessed | tf_op | source)
XLA Modules:
  0.0 117.2 jit_solution(3399404401713676459)
XLA Ops:
  0.6 2.0 %prepare.1 = (bf16[400,512]{1,0:T(8,128)(2,1)}, s32[2,8,1024]{2,1,0:T(8,128)}) custom-call(f32[400,512]{1,0:T(8,128)} %bitcast.20, s32[2,1000]{1,0:T(2,128)} %bitcast.22, s32[2,1000]{1,0:T(2,128)} %bitcast.23, s32[2,1000]{1,0:T(2,128)} %bitcast.24, s32[2,500]{1,0:T(2,128)} %bitcast.25), custom_call_target="tpu_custom_call" | custom-call | tf_op jit(solution)/shard_map/prepare/pallas_call | solution.py:34
  2.6 9.6 %collective-permute-start.1 = (bf16[400,512]{1,0:T(8,128)(2,1)}, bf16[400,512]{1,0:T(8,128)(2,1)S(1)}, u32[]{:S(2)}, u32[]{:S(2)}) collective-permute-start(bf16[400,512]{1,0:T(8,128)(2,1)} %get-tuple-element.20.left), channel_id=1, source_target_pairs={{4,0},{8,4},{12,8},{16,12},{20,16},{24,20},{28,24},{32,28},{36,32}... | collective-permute-start | bytes 1228808 | tf_op jit(solution)/shard_map/ppermute | solution.py:45
  12.2 0.8 slice_bitcast_fusion
  13.0 0.2 collective-permute-start
  13.2 9.1 %first.1 = (f32[400,512]{1,0:T(8,128)}, f32[1,512]{1,0:T(1,128)}, bf16[2,200,1024]{2,1,0:T(8,128)(2,1)}, bf16[400,2176]{1,0:T(8,128)(2,1)}) custom-call(bf16[400,512]{1,0:T(8,128)(2,1)} %get-tuple-element.20.left, f32[400,512]{1,0:T(8,128)} %bitcast.21, f32[1,512]{1,0:T(1,128)} %state.1, f32[400,2066]{1,0:T(8,128)} %bitcast.18, ...), custom_call_target="tpu_custom_call" | custom-call | tf_op jit(solution)/shard_map/first/pallas_call | solution.py:34
  22.3 0.0 collective-permute-done.1.left
  22.3 0.0 copy-start.3
  22.3 0.6 copy-done.4
  22.9 0.2 copy-done.3
  23.0 11.0 %second.1 = (bf16[400,1024]{1,0:T(8,128)(2,1)}, bf16[512,1024]{1,0:T(8,128)(2,1)}, bf16[400,1024]{1,0:T(8,128)(2,1)}, bf16[2,200,1024]{2,1,0:T(8,128)(2,1)}, f32[200,2176]{1,0:T(8,128)}) custom-call(s32[1]{0:T(128)} %bitcast.core, bf16[400,512]{1,0:T(8,128)(2,1)} %copy-done.3, f32[400,512]{1,0:T(8,128)} %get-tuple-element.22.slab, ...), custom_call_target="tpu_custom_call" | custom-call | tf_op jit(solution)/shard_map/second/pallas_call | solution.py:224
  34.0 1.2 %collective-permute-start.2 = (f32[200,2176]{1,0:T(8,128)}, f32[200,2176]{1,0:T(8,128)S(1)}, u32[]{:S(2)}, u32[]{:S(2)}) collective-permute-start(f32[200,2176]{1,0:T(8,128)} %get-tuple-element.33), channel_id=1, source_target_pairs={{0,1},{1,0},{2,3},{3,2},{4,5},{5,4},{6,7},{7,6},{8,9},{9,8},{10,11... | collective-permute-start | bytes 5222408 | tf_op jit(solution)/shard_map/ppermute | solution.py:49
  35.3 7.4 %finish.1 = (f32[200,2176]{1,0:T(8,128)}, f32[400,512]{1,0:T(8,128)}, f32[1,512]{1,0:T(1,128)}) custom-call(s32[1]{0:T(128)} %bitcast.core, f32[400,512]{1,0:T(8,128)} %get-tuple-element.22.slab, f32[1,512]{1,0:T(1,128)} %get-tuple-element.23.state, s32[2,8,1024]{2,1,0:T(8,128)} %get-tuple-element.21.ids, s32[8,1024]{1,0:T(8,128)} %copy-done.4, ...), custom_call_target="tpu_custom_call" | custom-call | tf_op jit(solution)/shard_map/finish/pallas_call | solution.py:224
  42.7 1.2 %copy-done.1 = f32[200,2176]{1,0:T(8,128)} copy-done((f32[200,2176]{1,0:T(8,128)}, f32[200,2176]{1,0:T(8,128)S(1)}, u32[]{:S(2)}) %copy-start.1) | copy-done | bytes 1740824
  43.9 3.4 %send.1 = s16[32,112,128]{2,1,0:T(8,128)(2,1)} custom-call(f32[200,2176]{1,0:T(8,128)} %get-tuple-element.32.mine, f32[200,2176]{1,0:T(8,128)} %copy-done.1), custom_call_target="tpu_custom_call" | custom-call | tf_op jit(solution)/shard_map/send/pallas_call | solution.py:34
  47.3 20.9 %all_to_all.10.parts = s16[32,112,128]{2,1,0:T(8,128)(2,1)} all-to-all(s16[32,112,128]{2,1,0:T(8,128)(2,1)} %send.1), channel_id=1, replica_groups=mesh['x'=4,'z_hi'=4,'z_lo'=2,'y_lo'=2,'y_hi'=2,'core'=2] {'x','z_lo','y_..., dimensions={0} | all-to-all | bytes 1835008 | tf_op jit(solution)/shard_map/all_to_all | solution.py:290
  68.2 2.1 %gather.1.a = s16[112,128]{1,0:T(8,128)(2,1)} custom-call(s16[32,112,128]{2,1,0:T(8,128)(2,1)} %all_to_all.10.parts), custom_call_target="tpu_custom_call" | custom-call | tf_op jit(solution)/shard_map/gather/pallas_call | solution.py:34
  70.4 5.2 %collective-permute-start.3 = (s16[112,128]{1,0:T(8,128)(2,1)}, s16[112,128]{1,0:T(8,128)(2,1)S(1)}, u32[]{:S(2)}, u32[]{:S(2)}) collective-permute-start(s16[112,128]{1,0:T(8,128)(2,1)} %gather.1.a), channel_id=1, source_target_pairs={{16,0},{32,16},{48,32},{0,48},{17,1},{33,17},{49,33},{1,49},{18,2}... | collective-permute-start | bytes 86024 | tf_op jit(solution)/shard_map/ppermute | solution.py:294
  75.5 0.0 collective-permute-start.4
  75.6 2.1 %collective-permute-start.5 = (s16[112,128]{1,0:T(8,128)(2,1)}, s16[112,128]{1,0:T(8,128)(2,1)S(1)}, u32[]{:S(2)}, u32[]{:S(2)}) collective-permute-start(s16[112,128]{1,0:T(8,128)(2,1)} %gather.1.a), channel_id=1, source_target_pairs={{48,0},{0,16},{16,32},{32,48},{49,1},{1,17},{17,33},{33,49},{50,2}... | collective-permute-start | bytes 86024 | tf_op jit(solution)/shard_map/ppermute | solution.py:294
  77.6 0.0 collective-permute-done.3.b
  77.6 5.1 %collective-permute-done.4.c = s16[112,128]{1,0:T(8,128)(2,1)S(1)} collective-permute-done((s16[112,128]{1,0:T(8,128)(2,1)}, s16[112,128]{1,0:T(8,128)(2,1)S(1)}, u32[]{:S(2)}, u32[]{:S(2)}) %collective-permute-start.4) | collective-permute-done | bytes 28704 | tf_op jit(solution)/shard_map/ppermute | solution.py:294
  82.7 0.0 collective-permute-done.5.d
  82.7 0.6 copy-done.6
  83.3 0.6 copy-done.7
  83.9 1.9 %spread.1 = s16[32,112,128]{2,1,0:T(8,128)(2,1)} custom-call(s16[112,128]{1,0:T(8,128)(2,1)} %gather.1.a, s16[112,128]{1,0:T(8,128)(2,1)} %copy-done.5, s16[112,128]{1,0:T(8,128)(2,1)} %copy-done.6, s16[112,128]{1,0:T(8,128)(2,1)} %copy-done.7), custom_call_target="tpu_custom_call" | custom-call | tf_op jit(solution)/shard_map/spread/pallas_call | solution.py:34
  85.8 18.8 %all_to_all.11.ours = s16[32,112,128]{2,1,0:T(8,128)(2,1)S(1)} all-to-all(s16[32,112,128]{2,1,0:T(8,128)(2,1)} %spread.1), channel_id=1, replica_groups=mesh['x'=4,'z_hi'=4,'z_lo'=2,'y_lo'=2,'y_hi'=2,'core'=2] {'x','z_lo','y_..., dimensions={0} | all-to-all | bytes 1835008 | tf_op jit(solution)/shard_map/all_to_all | solution.py:298
  104.6 2.5 %collective-permute-start.6 = (s16[32,112,128]{2,1,0:T(8,128)(2,1)S(1)}, s16[32,112,128]{2,1,0:T(8,128)(2,1)S(1)}, u32[]{:S(2)}, u32[]{:S(2)}) collective-permute-start(s16[32,112,128]{2,1,0:T(8,128)(2,1)S(1)} %all_to_all.11.ours), channel_id=1, source_target_pairs={{0,1},{1,0},{2,3},{3,2},{4,5},{5,4},{6,7},{7,6},{8,9},{9,8},{10,11... | collective-permute-start | bytes 2752520 | tf_op jit(solution)/shard_map/ppermute | solution.py:49
  107.1 0.6 broadcast_in_dim.11.state
  107.7 1.5 %collective-permute-done.6.theirs = s16[32,112,128]{2,1,0:T(8,128)(2,1)S(1)} collective-permute-done((s16[32,112,128]{2,1,0:T(8,128)(2,1)S(1)}, s16[32,112,128]{2,1,0:T(8,128)(2,1)S(1)}, u32[]{:S(2)}, u32[]{:S(2)}) %collective-permute-start.6) | collective-permute-done | bytes 917536 | tf_op jit(solution)/shard_map/ppermute | solution.py:49
  109.2 1.0 copy-done.2
  110.2 5.7 %update.1 = (f32[400,2066]{1,0:T(8,128)}, f32[1,2066]{1,0:T(1,128)}) custom-call(s32[1]{0:T(128)} %bitcast.core, s16[32,112,128]{2,1,0:T(8,128)(2,1)} %copy-done, s16[32,112,128]{2,1,0:T(8,128)(2,1)} %copy-done.2, f32[400,2066]{1,0:T(8,128)} %bitcast.19, f32[1,2066]{1,0:T(1,128)} %broadcast_in_dim.11.state), custom_call_target="tpu_custom_call" | custom-call | tf_op jit(solution)/shard_map/update/pallas_call | solution.py:224
  115.9 1.3 %reduce = f32[2066]{0:T(1024)} reduce(f32[1,2066]{1,0:T(1,128)} %get-tuple-element.35, f32[]{:T(128)} %constant.11), dimensions={0}, to_apply=%get-tuple-element.35.reduce_sub_computation | reduce | bytes 16532 | tf_op jit(solution)/shard_map/update/pallas_call | solution.py:224
  (13 shorter events, 0.0 us)
Async XLA Ops:
  2.6 19.7 %collective-permute-start.1 = (bf16[400,512]{1,0:T(8,128)(2,1)}, bf16[400,512]{1,0:T(8,128)(2,1)S(1)}, u32[]{:S(2)}, u32[]{:S(2)}) collective-permute-start(bf16[400,512]{1,0:T(8,128)(2,1)} %get-tuple-element.20.left), channel_id=1, source_target_pairs={{4,0},{8,4},{12,8},{16,12},{20,16},{24,20},{28,24},{32,28},{36,32}... | collective-permute-start | bytes 1228808 | tf_op jit(solution)/shard_map/ppermute | solution.py:45
  13.0 9.3 %collective-permute-start = (s32[8,1024]{1,0:T(8,128)S(1)}, s32[8,1024]{1,0:T(8,128)S(1)}, u32[]{:S(2)}, u32[]{:S(2)}) collective-permute-start(s32[8,1024]{1,0:T(8,128)S(1)} %slice_bitcast_fusion), channel_id=1, source_target_pairs={{4,0},{8,4},{12,8},{16,12},{20,16},{24,20},{28,24},{32,28},{36,32}... | collective-permute-start | bytes 98312 | tf_op jit(solution)/shard_map/ppermute | solution.py:45
  22.3 0.6 copy-start.4
  22.3 0.8 copy-start.3
  34.0 8.7 %collective-permute-start.2 = (f32[200,2176]{1,0:T(8,128)}, f32[200,2176]{1,0:T(8,128)S(1)}, u32[]{:S(2)}, u32[]{:S(2)}) collective-permute-start(f32[200,2176]{1,0:T(8,128)} %get-tuple-element.33), channel_id=1, source_target_pairs={{0,1},{1,0},{2,3},{3,2},{4,5},{5,4},{6,7},{7,6},{8,9},{9,8},{10,11... | collective-permute-start | bytes 5222408 | tf_op jit(solution)/shard_map/ppermute | solution.py:49
  42.7 1.2 %copy-start.1 = (f32[200,2176]{1,0:T(8,128)}, f32[200,2176]{1,0:T(8,128)S(1)}, u32[]{:S(2)}) copy-start(f32[200,2176]{1,0:T(8,128)S(1)} %collective-permute-done.2.theirs) | copy-start | bytes 5222404
  68.2 38.9 %copy-start.8 = (f32[2066]{0:T(1024)S(1)}, f32[2066]{0:T(1024)}, u32[]{:S(2)}) copy-start(f32[2066]{0:T(1024)} %param.13) | copy-start | bytes 24796
  70.4 7.3 %collective-permute-start.3 = (s16[112,128]{1,0:T(8,128)(2,1)}, s16[112,128]{1,0:T(8,128)(2,1)S(1)}, u32[]{:S(2)}, u32[]{:S(2)}) collective-permute-start(s16[112,128]{1,0:T(8,128)(2,1)} %gather.1.a), channel_id=1, source_target_pairs={{16,0},{32,16},{48,32},{0,48},{17,1},{33,17},{49,33},{1,49},{18,2}... | collective-permute-start | bytes 86024 | tf_op jit(solution)/shard_map/ppermute | solution.py:294
  75.5 7.1 %collective-permute-start.4 = (s16[112,128]{1,0:T(8,128)(2,1)}, s16[112,128]{1,0:T(8,128)(2,1)S(1)}, u32[]{:S(2)}, u32[]{:S(2)}) collective-permute-start(s16[112,128]{1,0:T(8,128)(2,1)} %gather.1.a), channel_id=1, source_target_pairs={{32,0},{48,16},{0,32},{16,48},{33,1},{49,17},{1,33},{17,49},{34,2}... | collective-permute-start | bytes 86024 | tf_op jit(solution)/shard_map/ppermute | solution.py:294
  75.6 7.1 %collective-permute-start.5 = (s16[112,128]{1,0:T(8,128)(2,1)}, s16[112,128]{1,0:T(8,128)(2,1)S(1)}, u32[]{:S(2)}, u32[]{:S(2)}) collective-permute-start(s16[112,128]{1,0:T(8,128)(2,1)} %gather.1.a), channel_id=1, source_target_pairs={{48,0},{0,16},{16,32},{32,48},{49,1},{1,17},{17,33},{33,49},{50,2}... | collective-permute-start | bytes 86024 | tf_op jit(solution)/shard_map/ppermute | solution.py:294
  77.6 5.1 %copy-start.5 = (s16[112,128]{1,0:T(8,128)(2,1)}, s16[112,128]{1,0:T(8,128)(2,1)S(1)}, u32[]{:S(2)}) copy-start(s16[112,128]{1,0:T(8,128)(2,1)S(1)} %collective-permute-done.3.b) | copy-start | bytes 86020
  82.7 0.6 copy-start.6
  83.3 0.6 copy-start.7
  104.6 4.6 %copy-start = (s16[32,112,128]{2,1,0:T(8,128)(2,1)}, s16[32,112,128]{2,1,0:T(8,128)(2,1)S(1)}, u32[]{:S(2)}) copy-start(s16[32,112,128]{2,1,0:T(8,128)(2,1)S(1)} %all_to_all.11.ours) | copy-start | bytes 2752516
  104.6 4.6 %collective-permute-start.6 = (s16[32,112,128]{2,1,0:T(8,128)(2,1)S(1)}, s16[32,112,128]{2,1,0:T(8,128)(2,1)S(1)}, u32[]{:S(2)}, u32[]{:S(2)}) collective-permute-start(s16[32,112,128]{2,1,0:T(8,128)(2,1)S(1)} %all_to_all.11.ours), channel_id=1, source_target_pairs={{0,1},{1,0},{2,3},{3,2},{4,5},{5,4},{6,7},{7,6},{8,9},{9,8},{10,11... | collective-permute-start | bytes 2752520 | tf_op jit(solution)/shard_map/ppermute | solution.py:49
  109.2 1.0 copy-start.2

commit v4 on v3

--- a/solution.py
+++ b/solution.py
@@ -30,12 +30,31 @@
     return jax.ShapeDtypeStruct(shape, dtype)
 
 
-def call(kernel, out_shape, *args, scratch=(), name):
+def kept(shape, dtype):
+    return pltpu.VMEM(shape, dtype)
+
+
+def near(array):
+    return pltpu.with_memory_space_constraint(array, pltpu.VMEM)
+
+
+def call(kernel, out_shape, *args, core=None, scratch=(), far_out=(), name, limit=32):
+    vmem = pl.BlockSpec(memory_space=pltpu.VMEM)
+    far = pl.BlockSpec(memory_space=pl.ANY)
+    several = isinstance(out_shape, tuple)
+    outs = out_shape if several else (out_shape,)
+    specs = tuple(far if i in far_out else vmem for i in range(len(outs)))
+    in_specs = [vmem] * len(args)
+    args = [near(arg) for arg in args]
+    if core is not None:
+        in_specs, args = [pl.BlockSpec(memory_space=pltpu.SMEM)] + in_specs, [core] + args
     return pl.pallas_call(
         kernel,
         out_shape=out_shape,
+        in_specs=in_specs,
+        out_specs=specs if several else specs[0],
         scratch_shapes=scratch,
-        compiler_params=pltpu.CompilerParams(vmem_limit_bytes=60 * 1024 * 1024),
+        compiler_params=pltpu.CompilerParams(vmem_limit_bytes=limit * 1024 * 1024),
         name=name,
     )(*args)
 
@@ -54,8 +73,8 @@
 
 
 def places(row, count):
-    at = lax.broadcasted_iota(jnp.int32, (count, row.shape[1]), 0)
-    return jnp.where(at == row, 1.0, 0.0).astype(BF16)
+    at = lax.broadcasted_iota(jnp.int32, (count, row.shape[1]), 0).astype(jnp.int16)
+    return jnp.where(at == row.astype(jnp.int16), BF16(1), BF16(0))
 
 
 def edge_terms(left, slab, table, ids):
@@ -87,41 +106,58 @@
     return slab - grad * (0.1 * lax.rsqrt(state)), state
 
 
-def prepare_kernel(left, src, dst, rel, neg, left_low, ids):
-    left_low[...] = left[...].astype(BF16)
+def prepare_kernel(left, src, dst, rel, neg, ids, message, next_ids):
+    message[:D] = left[...].astype(BF16)
     ids[...] = jnp.full(ids.shape, -1, jnp.int32)
-    for step in range(2):
-        for place, source in enumerate((src, dst, rel, neg)):
-            ids[step, place : place + 1, : source.shape[1]] = source[step : step + 1, :]
+    next_ids[...] = jnp.full(next_ids.shape, -1, jnp.int32)
+    for place, source in enumerate((src, dst, rel, neg)):
+        ids[place : place + 1, : source.shape[1]] = source[0:1, :]
+        next_ids[place : place + 1, : source.shape[1]] = source[1:2, :]
+    high, low = (next_ids[...] >> 6).astype(F32), (next_ids[...] & 63).astype(F32)
+    halves = slice(0, ROWS), slice(ROWS, EPAD)
+    packed = [part[:4, half] for part in (high, low) for half in halves]
+    message[D:] = jnp.concatenate(packed, 0).astype(BF16)
+
+
+def unpacked_ids(message):
+    coded = message[D:].astype(F32)
+    halves = (coded[4 * i : 4 * i + 4] * 64.0 + coded[8 + 4 * i : 12 + 4 * i] for i in range(2))
+    rows = jnp.concatenate(list(halves), 1).astype(jnp.int32)
+    return jnp.concatenate([rows, rows], 0)
 
 
 def first_kernel(left, slab, state, relation, ids, slab_out, state_out, d_rel_out, table_out):
     table_out[:, :RMAIN] = relation[:, :RMAIN].astype(BF16)
     table_out[:, RMAIN:] = jnp.zeros((D, RPAD - RMAIN), BF16)
     table_out[:, RMAIN:NREL] = relation[:, RMAIN:].astype(BF16)
-    prod, g_neg, d_pos, d_rel = edge_terms(left[...], slab[...], table_out[...], ids[0])
+    prod, g_neg, d_pos, d_rel = edge_terms(left[:D], slab[...], table_out[...], ids[...])
     for half in range(2):
         d_rel_out[half] = d_rel[half]
-    slab_out[...], state_out[...] = trained(slab[...], state[...], ids[0], prod, g_neg, d_pos)
+    slab_out[...], state_out[...] = trained(slab[...], state[...], ids[...], prod, g_neg, d_pos)
 
 
 def rel_half(half, ids, ids_next, d_rel, d_rel_next):
     along = ((1,), (1,))
-    return dot(d_rel[half], places(ids[0, 2:3], RPAD), along) + dot(
+    return dot(d_rel[half], places(ids[2:3], RPAD), along) + dot(
         d_rel_next[half], places(ids_next[2:3], RPAD), along
     )
 
 
-def second_kernel(core, left, slab, table, ids, ids_next, d_rel, prod, g_neg, d_pos, d_rel_next, other):
+def second_kernel(
+    core, left, slab, table, ids, d_rel, ids_next, prod, g_neg, d_pos, d_rel_next, other
+):
+    ids_next[...] = unpacked_ids(left[...])
     prod[...], g_neg[...], d_pos[...], parts = edge_terms(
-        left[...], slab[...], table[...], ids_next[...]
+        left[:D], slab[...], table[...], ids_next[...]
     )
     for half in range(2):
         d_rel_next[half] = parts[half]
     other[...] = rel_half(1 - core[0], ids, ids_next, d_rel, d_rel_next)
 
 
-def finish_kernel(core, slab, state, ids, ids_next, d_rel, prod, g_neg, d_pos, d_rel_next, mine, slab_out, state_out):
+def finish_kernel(
+    core, slab, state, ids, ids_next, d_rel, prod, g_neg, d_pos, d_rel_next, mine, slab_out, state_out
+):
     mine[...] = rel_half(core[0], ids, ids_next, d_rel, d_rel_next)
     slab_out[...], state_out[...] = trained(
         slab[...], state[...], ids_next[...], prod[...], g_neg[...], d_pos[...]
@@ -177,17 +213,22 @@
     for part in range(1, OWNERS):
         more = decode(parts[part])
         main, last = main + more[0], last + more[1]
-    codes[...] = encode(main, last)
-
-
-def spread_kernel(a, b, c, d, copies):
-    a, b, c, d = (decode(part[...]) for part in (a, b, c, d))
-    code = encode(*((a[i] + c[i]) + (b[i] + d[i]) for i in range(2)))
-    for part in range(OWNERS):
-        copies[part] = code
-
-
-def update_kernel(core, ours, theirs, relation, state, relation_out, state_out, grads, last):
+    code = encode(main, last)
+    for copy in range(codes.shape[0]):
+        codes[copy] = code
+
+
+def spread_kernel(parts, copies):
+    main, last = decode(parts[0])
+    for part in range(1, parts.shape[0]):
+        more = decode(parts[part])
+        main, last = main + more[0], last + more[1]
+    code = encode(main, last)
+    for copy in range(OWNERS):
+        copies[copy] = code
+
+
+def update_kernel(core, ours, theirs, relation, state, relation_out, state_out, grads, last, wide, sems):
     for half, codes in enumerate((ours, theirs)):
         for part in range(OWNERS):
             rows, lanes = place_of(part)
@@ -199,10 +240,16 @@
     total = sum(jnp.sum(part * part, 0, keepdims=True) for part in both)[:, :NREL]
     new_state = state[...] + total * (1.0 / D)
     rate = 0.2 * lax.rsqrt(new_state)
-    real, imag = grads[core[0]], grads[1 - core[0]]
-    relation_out[:HALF] = relation[:HALF] - real[:, :NREL] * rate
-    relation_out[HALF:] = relation[HALF:] - imag[:, :NREL] * rate
     state_out[...] = new_state
+    copies = []
+    for half in range(2):
+        rows = slice(half * HALF, half * HALF + HALF)
+        grad = grads[core[0] if half == 0 else 1 - core[0]]
+        wide[half] = relation[rows] - grad[:, :NREL] * rate
+        copies.append(pltpu.make_async_copy(wide.at[half], relation_out.at[rows], sems.at[half]))
+        copies[half].start()
+    for copy in copies:
+        copy.wait()
 
 
 def per_device(
@@ -217,61 +264,55 @@
     negative_rows,
 ):
     core = lax.axis_index("core").astype(jnp.int32)[None]
-    smem = pl.BlockSpec(memory_space=pltpu.SMEM)
-    vmem = pl.BlockSpec(memory_space=pltpu.VMEM)
-
-    def with_core(kernel, out_shape, *args, scratch=(), name):
-        return pl.pallas_call(
-            kernel,
-            out_shape=out_shape,
-            scratch_shapes=scratch,
-            in_specs=[smem] + [vmem] * len(args),
-            compiler_params=pltpu.CompilerParams(vmem_limit_bytes=60 * 1024 * 1024),
-            name=name,
-        )(core, *args)
-
-    left_low, ids = call(
+    ids, message = call(
         prepare_kernel,
-        (struct((D, ROWS), BF16), struct((2, 8, EPAD), jnp.int32)),
+        (kept((8, EPAD), jnp.int32), kept((D + 16, ROWS), BF16)),
         left_embed[0].T,
         source_rows[0, 0],
         target_rows[0, 0],
         relation_ids[0, 0],
         negative_rows[0, 0],
+        scratch=[pltpu.VMEM((8, EPAD), jnp.int32)],
         name="prepare",
     )
-    left_next = from_next(left_low)
-    ids_next = from_next(ids[1])
+    message_next = from_next(message)
     relation = relation_embed.T
-    slab_array, state_array = struct((D, ROWS), F32), struct((1, ROWS), F32)
-    edge_array = struct((D, EPAD), BF16)
-    pair_array = struct((2, HALF, EPAD), BF16)
-    half_array = struct((HALF, RPAD), F32)
+    slab_array, state_array = (D, ROWS), (1, ROWS)
+    edge_array = kept((D, EPAD), BF16)
+    pair_array = kept((2, HALF, EPAD), BF16)
+    half_array = kept((HALF, RPAD), F32)
     slab, state, d_rel, table = call(
         first_kernel,
-        (slab_array, state_array, pair_array, struct((D, RPAD), BF16)),
-        left_low,
+        (kept(slab_array, F32), kept(state_array, F32), pair_array, kept((D, RPAD), BF16)),
+        message,
         right_embed[0].T,
         right_state,
         relation,
         ids,
         name="first",
     )
-    prod, g_neg, d_pos, d_rel_next, other = with_core(
+    ids_next, prod, g_neg, d_pos, d_rel_next, other = call(
         second_kernel,
-        (edge_array, struct((NPAD, EPAD), BF16), edge_array, pair_array, half_array),
-        left_next,
+        (
+            kept((8, EPAD), jnp.int32),
+            edge_array,
+            kept((NPAD, EPAD), BF16),
+            edge_array,
+            pair_array,
+            half_array,
+        ),
+        message_next,
         slab,
         table,
         ids,
-        ids_next,
         d_rel,
+        core=core,
         name="second",
     )
     theirs = swap_core(other)
-    mine, slab_out, state_out = with_core(
+    mine, slab_out, state_out = call(
         finish_kernel,
-        (half_array, slab_array, state_array),
+        (half_array, struct(slab_array, F32), struct(state_array, F32)),
         slab,
         state,
         ids,
@@ -281,30 +322,35 @@
         g_neg,
         d_pos,
         d_rel_next,
+        core=core,
         name="finish",
     )
-    part = struct((PART, 128), jnp.int16)
-    parts = struct((OWNERS, PART, 128), jnp.int16)
+    part = (PART, 128)
     last = pltpu.VMEM((232, 128), F32)
+    parts = kept((OWNERS, *part), jnp.int16)
     sent = call(send_kernel, parts, mine, theirs, scratch=[last], name="send")
     got = lax.all_to_all(sent, CUBE, 0, 0, tiled=True)
-    code = call(gather_kernel, part, got, name="gather")
     count = lax.axis_size("z_hi")
-    ring = [
-        lax.ppermute(code, "z_hi", [((i + k) % count, i) for i in range(count)])
-        for k in range(1, count)
-    ]
-    copies = call(spread_kernel, parts, code, *ring, name="spread")
+    codes = call(gather_kernel, kept((count, *part), jnp.int16), got, name="gather")
+    codes = lax.all_to_all(codes, "z_hi", 0, 0, tiled=True)
+    copies = call(spread_kernel, parts, codes, name="spread")
     ours = lax.all_to_all(copies, CUBE, 0, 0, tiled=True)
     theirs = swap_core(ours)
-    relation_out, relation_state_out = with_core(
+    relation_out, relation_state_out = call(
         update_kernel,
         (struct((D, NREL), F32), struct((1, NREL), F32)),
         ours,
         theirs,
         relation,
         relation_state[None],
-        scratch=[pltpu.VMEM((2, HALF, RPAD), F32), last],
+        core=core,
+        far_out=(0,),
+        scratch=[
+            pltpu.VMEM((2, HALF, RPAD), F32),
+            last,
+            pltpu.VMEM((2, HALF, NREL), F32),
+            pltpu.SemaphoreType.DMA((2,)),
+        ],
         name="update",
     )
     return (slab_out.T[None], state_out, relation_out.T, relation_state_out[0])

time: 118 us -> 99.7 us (0.84)
  Pallas kernels: 42.6 us -> 22.2 us
  blocking collectives: 39.8 us -> 52.6 us
  starting transfers between devices: 20.8 us -> 13.2 us
  waiting for transfers between devices: 6.56 us -> 2.09 us
  local copies, waits for them, and re-layouts: 5.53 us -> 7.74 us
    pallas_call x8, Pallas kernels: 42.6 us -> 22.2 us  [call(): pl.pallas_call(kernel, out_shape=out_shape, in_specs=in_specs, out_specs=...]
    all_to_all x0 -> x1, blocking collectives: none -> 14.2 us  [per_device(): codes = lax.all_to_all(codes, 'z_hi', 0, 0, tiled=True)]
    ppermute x3 -> x0, starting transfers between devices: 7.26 us -> none  [per_device(): lax.ppermute(code, 'z_hi', [((i + k) % count, i) for i in range(count)])]
    ppermute x3 -> x0, waiting for transfers between devices: 5.06 us -> none  [per_device(): lax.ppermute(code, 'z_hi', [((i + k) % count, i) for i in range(count)])]
    unnamed x18 -> x20, local copies, waits for them, and re-layouts: 4.16 us -> 7.73 us
    ppermute x2 -> x1, starting transfers between devices: 9.78 us -> 9.69 us  [from_next(): lax.ppermute(block, BUCKET, [((i + 1) % count, i) for i in range(count)])]
  transfers between devices with their start and end apart: 7 -> 3, of which waited for: 2 -> 1; matrix products, arithmetic and copies ran while one was open for 1% -> 0% of each run, Pallas kernels for 14% -> 11%
where the time goes in v4:
time: 99.7 us; the launch traced here: 99.2 us
  blocking collectives  52.6 us (53%)
  Pallas kernels  22.2 us (22%)
  starting transfers between devices  13.2 us (13%)
  local copies, waits for them, and re-layouts  7.74 us (8%)
  waiting for transfers between devices  2.09 us (2%)
    pallas_call x8, Pallas kernels, call(): pl.pallas_call(kernel, out_shape=out_shape, in_specs=in_specs, out_specs=...  22.2 us
    all_to_all x1, blocking collectives, per_device(): got = lax.all_to_all(sent, CUBE, 0, 0, tiled=True)  20.3 us
    all_to_all x1, blocking collectives, per_device(): ours = lax.all_to_all(copies, CUBE, 0, 0, tiled=True)  18.2 us
    all_to_all x1, blocking collectives, per_device(): codes = lax.all_to_all(codes, 'z_hi', 0, 0, tiled=True)  14.2 us
    ppermute x1, starting transfers between devices, from_next(): lax.ppermute(block, BUCKET, [((i + 1) % count, i) for i in range(count)])  9.69 us
    unnamed x20, local copies, waits for them, and re-layouts  7.73 us
    ppermute x2, starting transfers between devices, swap_core(): return lax.ppermute(block, 'core', [(0, 1), (1, 0)])  3.51 us
    ppermute x2, waiting for transfers between devices, swap_core(): return lax.ppermute(block, 'core', [(0, 1), (1, 0)])  2.09 us
  transfers between devices with their start and end apart: 3, of which 1 were waited for; matrix products, arithmetic and copies ran while one was open for 0% of the time, Pallas kernels for 11%

profile of v4, /device:TPU:1, one launch (start us, length us, event | category | flops | bytes accessed | tf_op | source)
XLA Modules:
  0.0 99.2 jit_solution(11476710593755463813)
XLA Ops:
  0.6 0.0 copy-start.2
  0.6 1.1 %copy-done.2 = f32[1,512,400]{1,2,0:T(8,128)S(1)} copy-done((f32[1,512,400]{1,2,0:T(8,128)S(1)}, f32[1,512,400]{1,2,0:T(8,128)}, u32[]{:S(2)}) %copy-start.2) | copy-done | bytes 819224
  1.8 0.0 copy-start.4
  1.8 0.7 copy-done.4
  2.5 0.0 copy-start.5
  2.5 0.7 copy-done.5
  3.2 0.7 copy-done.6
  3.9 0.7 copy-done.7
  4.6 0.1 prepare.1
  4.6 9.7 %collective-permute-start = (bf16[416,512]{1,0:T(8,128)(2,1)S(1)}, bf16[416,512]{1,0:T(8,128)(2,1)S(1)}, u32[]{:S(2)}, u32[]{:S(2)}) collective-permute-start(bf16[416,512]{1,0:T(8,128)(2,1)S(1)} %get-tuple-element.21.left), channel_id=1, source_target_pairs={{4,0},{8,4},{12,8},{16,12},{20,16},{24,20},{28,24},{32,28},{36,32}... | collective-permute-start | bytes 1277960 | tf_op jit(solution)/shard_map/ppermute | solution.py:64
  14.3 2.0 %copy-done = f32[2066,400]{0,1:T(8,128)S(1)} copy-done((f32[2066,400]{0,1:T(8,128)S(1)}, f32[2066,400]{0,1:T(8,128)}, u32[]{:S(2)}) %copy-start) | copy-done | bytes 3305624
  16.3 1.1 %copy-done.3 = f32[1,512,400]{1,2,0:T(8,128)S(1)} copy-done((f32[1,512,400]{1,2,0:T(8,128)S(1)}, f32[1,512,400]{1,2,0:T(8,128)}, u32[]{:S(2)}) %copy-start.3) | copy-done | bytes 819224
  17.4 0.7 copy-done.8
  18.1 5.7 %first.1 = (f32[400,512]{1,0:T(8,128)S(1)}, f32[1,512]{1,0:T(1,128)S(1)}, bf16[2,200,1024]{2,1,0:T(8,128)(2,1)S(1)}, bf16[400,2176]{1,0:T(8,128)(2,1)S(1)}) custom-call(bf16[416,512]{1,0:T(8,128)(2,1)S(1)} %get-tuple-element.21.left, f32[400,512]{1,0:T(8,128)S(1)} %bitcast.19, f32[1,512]{1,0:T(1,128)S(1)} %copy-done.8, f32[400,2066]{1,0:T(8,128)S(1)} %bitcast.16, ...), custom_call_target="tpu_custom_call" | custom-call | tf_op jit(solution)/shard_map/first/pallas_call | solution.py:51
  23.8 0.0 collective-permute-done.left
  23.8 7.6 %second.1 = (s32[8,1024]{1,0:T(8,128)S(1)}, bf16[400,1024]{1,0:T(8,128)(2,1)S(1)}, bf16[512,1024]{1,0:T(8,128)(2,1)S(1)}, bf16[400,1024]{1,0:T(8,128)(2,1)S(1)},...) custom-call(s32[1]{0:T(128)} %bitcast.core, bf16[416,512]{1,0:T(8,128)(2,1)S(1)} %collective-permute-done.left, ...), custom_call_target="tpu_custom_call" | custom-call | tf_op jit(solution)/shard_map/second/pallas_call | solution.py:51
  31.5 1.2 %collective-permute-start.1 = (f32[200,2176]{1,0:T(8,128)S(1)}, f32[200,2176]{1,0:T(8,128)S(1)}, u32[]{:S(2)}, u32[]{:S(2)}) collective-permute-start(f32[200,2176]{1,0:T(8,128)S(1)} %get-tuple-element.35), channel_id=1, source_target_pairs={{0,1},{1,0},{2,3},{3,2},{4,5},{5,4},{6,7},{7,6},{8,9},{9,8},{10,11... | collective-permute-start | bytes 5222408 | tf_op jit(solution)/shard_map/ppermute | solution.py:68
  32.7 4.9 %finish.1 = (f32[200,2176]{1,0:T(8,128)S(1)}, f32[400,512]{1,0:T(8,128)}, f32[1,512]{1,0:T(1,128)}) custom-call(s32[1]{0:T(128)} %bitcast.core, f32[400,512]{1,0:T(8,128)S(1)} %get-tuple-element.23.slab, f32[1,512]{1,0:T(1,128)S(1)} %get-tuple-element.24.state, s32[8,1024]{1,0:T(8,128)S(1)} %get-tuple-element.22.ids, ...), custom_call_target="tpu_custom_call" | custom-call | tf_op jit(solution)/shard_map/finish/pallas_call | solution.py:51
  37.6 0.0 collective-permute-done.1.theirs
  37.6 0.5 send.1
  38.1 20.3 %all_to_all.15.parts = s16[32,112,128]{2,1,0:T(8,128)(2,1)S(1)} all-to-all(s16[32,112,128]{2,1,0:T(8,128)(2,1)S(1)} %send.1), channel_id=1, replica_groups=mesh['x'=4,'z_hi'=4,'z_lo'=2,'y_lo'=2,'y_hi'=2,'core'=2] {'x','z_lo','y_..., dimensions={0} | all-to-all | bytes 1835008 | tf_op jit(solution)/shard_map/all_to_all | solution.py:332
  58.4 0.3 gather.1
  58.7 0.0 copy-start.9
  58.8 14.2 %all_to_all.16.parts = s16[4,112,128]{2,1,0:T(8,128)(2,1)S(1)} all-to-all(s16[4,112,128]{2,1,0:T(8,128)(2,1)S(1)} %gather.1), channel_id=1, replica_groups=mesh['x'=4,'z_hi'=4,'z_lo'=2,'y_lo'=2,'y_hi'=2,'core'=2] {'z_hi'}, dimensions={0} | all-to-all | bytes 229376 | tf_op jit(solution)/shard_map/all_to_all | solution.py:335
  72.9 0.2 spread.1
  73.1 18.2 %all_to_all.17.ours = s16[32,112,128]{2,1,0:T(8,128)(2,1)S(1)} all-to-all(s16[32,112,128]{2,1,0:T(8,128)(2,1)S(1)} %spread.1), channel_id=1, replica_groups=mesh['x'=4,'z_hi'=4,'z_lo'=2,'y_lo'=2,'y_hi'=2,'core'=2] {'x','z_lo','y_..., dimensions={0} | all-to-all | bytes 1835008 | tf_op jit(solution)/shard_map/all_to_all | solution.py:337
  91.3 2.3 %collective-permute-start.2 = (s16[32,112,128]{2,1,0:T(8,128)(2,1)S(1)}, s16[32,112,128]{2,1,0:T(8,128)(2,1)S(1)}, u32[]{:S(2)}, u32[]{:S(2)}) collective-permute-start(s16[32,112,128]{2,1,0:T(8,128)(2,1)S(1)} %all_to_all.17.ours), channel_id=1, source_target_pairs={{0,1},{1,0},{2,3},{3,2},{4,5},{5,4},{6,7},{7,6},{8,9},{9,8},{10,11... | collective-permute-start | bytes 2752520 | tf_op jit(solution)/shard_map/ppermute | solution.py:68
  93.6 0.0 copy-done.9
  93.6 2.1 %collective-permute-done.2.theirs = s16[32,112,128]{2,1,0:T(8,128)(2,1)S(1)} collective-permute-done((s16[32,112,128]{2,1,0:T(8,128)(2,1)S(1)}, s16[32,112,128]{2,1,0:T(8,128)(2,1)S(1)}, u32[]{:S(2)}, u32[]{:S(2)}) %collective-permute-start.2) | collective-permute-done | bytes 917536 | tf_op jit(solution)/shard_map/ppermute | solution.py:68
  95.7 0.0 copy-done.1
  95.7 2.9 %update.1 = (f32[400,2066]{1,0:T(8,128)}, f32[1,2066]{1,0:T(1,128)S(1)}) custom-call(s32[1]{0:T(128)} %bitcast.core, s16[32,112,128]{2,1,0:T(8,128)(2,1)S(1)} %all_to_all.17.ours, s16[32,112,128]{2,1,0:T(8,128)(2,1)S(1)} %collective-permute-done.2.theirs, f32[400,2066]{1,0:T(8,128)S(1)} %bitcast.17, f32[1,2066]{1,0:T(1,128)S(1)} %broadcast_in_dim.11.state), custom_call_target="tpu_custom_call" | custom-call | tf_op jit(solution)/shard_map/update/pallas_call | solution.py:51
  98.6 0.6 reduce
  (7 shorter events, 0.0 us)
Async XLA Ops:
  0.6 1.1 %copy-start.2 = (f32[1,512,400]{1,2,0:T(8,128)S(1)}, f32[1,512,400]{1,2,0:T(8,128)}, u32[]{:S(2)}) copy-start(f32[1,512,400]{1,2,0:T(8,128)} %param.9) | copy-start | bytes 2457604
  1.8 0.7 copy-start.4
  2.5 0.7 copy-start.5
  3.2 0.7 copy-start.6
  3.9 0.7 copy-start.7
  4.6 19.2 %collective-permute-start = (bf16[416,512]{1,0:T(8,128)(2,1)S(1)}, bf16[416,512]{1,0:T(8,128)(2,1)S(1)}, u32[]{:S(2)}, u32[]{:S(2)}) collective-permute-start(bf16[416,512]{1,0:T(8,128)(2,1)S(1)} %get-tuple-element.21.left), channel_id=1, source_target_pairs={{4,0},{8,4},{12,8},{16,12},{20,16},{24,20},{28,24},{32,28},{36,32}... | collective-permute-start | bytes 1277960 | tf_op jit(solution)/shard_map/ppermute | solution.py:64
  14.3 2.0 %copy-start = (f32[2066,400]{0,1:T(8,128)S(1)}, f32[2066,400]{0,1:T(8,128)}, u32[]{:S(2)}) copy-start(f32[2066,400]{0,1:T(8,128)} %param.12) | copy-start | bytes 9916804
  16.3 1.1 %copy-start.3 = (f32[1,512,400]{1,2,0:T(8,128)S(1)}, f32[1,512,400]{1,2,0:T(8,128)}, u32[]{:S(2)}) copy-start(f32[1,512,400]{1,2,0:T(8,128)} %param.10) | copy-start | bytes 2457604
  17.4 0.7 copy-start.8
  31.5 6.1 %collective-permute-start.1 = (f32[200,2176]{1,0:T(8,128)S(1)}, f32[200,2176]{1,0:T(8,128)S(1)}, u32[]{:S(2)}, u32[]{:S(2)}) collective-permute-start(f32[200,2176]{1,0:T(8,128)S(1)} %get-tuple-element.35), channel_id=1, source_target_pairs={{0,1},{1,0},{2,3},{3,2},{4,5},{5,4},{6,7},{7,6},{8,9},{9,8},{10,11... | collective-permute-start | bytes 5222408 | tf_op jit(solution)/shard_map/ppermute | solution.py:68
  58.4 37.3 %copy-start.1 = (f32[2066,400]{0,1:T(8,128)S(1)}, f32[2066,400]{0,1:T(8,128)}, u32[]{:S(2)}) copy-start(f32[2066,400]{0,1:T(8,128)} %param.12) | copy-start | bytes 9916804
  58.7 34.8 %copy-start.9 = (f32[2066]{0:T(1024)S(1)}, f32[2066]{0:T(1024)}, u32[]{:S(2)}) copy-start(f32[2066]{0:T(1024)} %param.13) | copy-start | bytes 24796
  91.3 4.4 %collective-permute-start.2 = (s16[32,112,128]{2,1,0:T(8,128)(2,1)S(1)}, s16[32,112,128]{2,1,0:T(8,128)(2,1)S(1)}, u32[]{:S(2)}, u32[]{:S(2)}) collective-permute-start(s16[32,112,128]{2,1,0:T(8,128)(2,1)S(1)} %all_to_all.17.ours), channel_id=1, source_target_pairs={{0,1},{1,0},{2,3},{3,2},{4,5},{5,4},{6,7},{7,6},{8,9},{9,8},{10,11... | collective-permute-start | bytes 2752520 | tf_op jit(solution)/shard_map/ppermute | solution.py:68

commit v5 on v4

--- a/solution.py
+++ b/solution.py
@@ -38,14 +38,18 @@
     return pltpu.with_memory_space_constraint(array, pltpu.VMEM)
 
 
-def call(kernel, out_shape, *args, core=None, scratch=(), far_out=(), name, limit=32):
+def away(array):
+    return pltpu.with_memory_space_constraint(array, pltpu.HBM)
+
+
+def call(kernel, out_shape, *args, core=None, scratch=(), far_in=(), far_out=(), name, limit=32):
     vmem = pl.BlockSpec(memory_space=pltpu.VMEM)
-    far = pl.BlockSpec(memory_space=pl.ANY)
+    far = pl.BlockSpec(memory_space=pltpu.HBM)
     several = isinstance(out_shape, tuple)
     outs = out_shape if several else (out_shape,)
     specs = tuple(far if i in far_out else vmem for i in range(len(outs)))
-    in_specs = [vmem] * len(args)
-    args = [near(arg) for arg in args]
+    in_specs = [far if i in far_in else vmem for i in range(len(args))]
+    args = [away(arg) if i in far_in else near(arg) for i, arg in enumerate(args)]
     if core is not None:
         in_specs, args = [pl.BlockSpec(memory_space=pltpu.SMEM)] + in_specs, [core] + args
     return pl.pallas_call(
@@ -77,16 +81,20 @@
     return jnp.where(at == row.astype(jnp.int16), BF16(1), BF16(0))
 
 
-def edge_terms(left, slab, table, ids):
-    slab_low = slab.astype(BF16)
-    heads = dot(left, places(ids[0:1], ROWS))
-    rel_rows = dot(table, places(ids[2:3], RPAD))
+def target_rows_of(slab_low, ids):
+    pos_rows = dot(slab_low, places(ids[1:2], ROWS))
+    return pos_rows, dot(slab_low, places(ids[3:4, :NPAD], ROWS)).astype(BF16)
+
+
+def relation_rows_of(table, ids):
+    return dot(table, places(ids[2:3], RPAD))
+
+
+def edge_terms(heads, pos_rows, neg_rows, rel_rows):
     h_re, h_im = heads[:HALF], heads[HALF:]
     r_re, r_im = rel_rows[:HALF], rel_rows[HALF:]
     prod = jnp.concatenate([h_re * r_re - h_im * r_im, h_re * r_im + h_im * r_re], 0).astype(BF16)
     prod_wide = prod.astype(F32)
-    pos_rows = dot(slab_low, places(ids[1:2], ROWS))
-    neg_rows = dot(slab_low, places(ids[3:4, :NPAD], ROWS)).astype(BF16)
     pos = jnp.sum(prod_wide * pos_rows, 0, keepdims=True)
     g_pos = -jax.nn.sigmoid(-pos)
     g_neg = (jax.nn.sigmoid(dot(neg_rows, prod, ((0,), (0,)))) * (1.0 / NEG)).astype(BF16)
@@ -106,61 +114,83 @@
     return slab - grad * (0.1 * lax.rsqrt(state)), state
 
 
-def prepare_kernel(left, src, dst, rel, neg, ids, message, next_ids):
-    message[:D] = left[...].astype(BF16)
-    ids[...] = jnp.full(ids.shape, -1, jnp.int32)
-    next_ids[...] = jnp.full(next_ids.shape, -1, jnp.int32)
-    for place, source in enumerate((src, dst, rel, neg)):
-        ids[place : place + 1, : source.shape[1]] = source[0:1, :]
-        next_ids[place : place + 1, : source.shape[1]] = source[1:2, :]
-    high, low = (next_ids[...] >> 6).astype(F32), (next_ids[...] & 63).astype(F32)
-    halves = slice(0, ROWS), slice(ROWS, EPAD)
-    packed = [part[:4, half] for part in (high, low) for half in halves]
-    message[D:] = jnp.concatenate(packed, 0).astype(BF16)
-
-
-def unpacked_ids(message):
-    coded = message[D:].astype(F32)
-    halves = (coded[4 * i : 4 * i + 4] * 64.0 + coded[8 + 4 * i : 12 + 4 * i] for i in range(2))
-    rows = jnp.concatenate(list(halves), 1).astype(jnp.int32)
-    return jnp.concatenate([rows, rows], 0)
-
-
-def first_kernel(left, slab, state, relation, ids, slab_out, state_out, d_rel_out, table_out):
-    table_out[:, :RMAIN] = relation[:, :RMAIN].astype(BF16)
-    table_out[:, RMAIN:] = jnp.zeros((D, RPAD - RMAIN), BF16)
-    table_out[:, RMAIN:NREL] = relation[:, RMAIN:].astype(BF16)
-    prod, g_neg, d_pos, d_rel = edge_terms(left[:D], slab[...], table_out[...], ids[...])
+def prepare_kernel(left, src, dst, rel, neg, ids, next_ids, left_low, wide, places_in, sems):
+    sources = (src, dst, rel, neg)
+    copies = [pltpu.make_async_copy(left, wide, sems.at[4])]
+    copies += [pltpu.make_async_copy(r, places_in[i], sems.at[i]) for i, r in enumerate(sources)]
+    for copy in copies:
+        copy.start()
+    for step_ids in (ids, next_ids):
+        step_ids[...] = jnp.full(step_ids.shape, -1, jnp.int32)
+    for copy in copies[1:]:
+        copy.wait()
+    for place, source in enumerate(places_in):
+        for step, step_ids in enumerate((ids, next_ids)):
+            step_ids[place : place + 1, : source.shape[1]] = source[step : step + 1, :]
+    copies[0].wait()
+    left_low[...] = wide[...].astype(BF16)
+
+
+CHUNKS = ((0, 104), (104, 200), (200, 304), (304, 400))
+
+
+def first_kernel(
+    left, ids, slab_far, state_far, relation_far, slab_out, state_out, d_rel_out, table, slab, state, relation, sems
+):
+    copies = [
+        pltpu.make_async_copy(slab_far, slab, sems.at[0]),
+        pltpu.make_async_copy(state_far, state, sems.at[1]),
+    ]
+    for i, (start, stop) in enumerate(CHUNKS):
+        rows = slice(start, stop)
+        copies.append(pltpu.make_async_copy(relation_far.at[rows], relation.at[rows], sems.at[2 + i]))
+    for copy in copies:
+        copy.start()
+    heads = dot(left[...], places(ids[0:1], ROWS))
+    for copy in copies[:2]:
+        copy.wait()
+    pos_rows, neg_rows = target_rows_of(slab[...].astype(BF16), ids)
+    for copy in copies[2:]:
+        copy.wait()
+    table[:, :RMAIN] = relation[:, :RMAIN].astype(BF16)
+    table[:, RMAIN:] = jnp.zeros((D, RPAD - RMAIN), BF16)
+    table[:, RMAIN:NREL] = relation[:, RMAIN:].astype(BF16)
+    rel_rows = relation_rows_of(table[...], ids)
+    prod, g_neg, d_pos, d_rel = edge_terms(heads, pos_rows, neg_rows, rel_rows)
+    d_rel_out[:HALF], d_rel_out[HALF:] = d_rel
+    slab_out[...], state_out[...] = trained(slab[...], state[...], ids[...], prod, g_neg, d_pos)
+
+
+def between_kernel(slab, table, ids, ids_next, d_rel, pos_rows, neg_rows, rel_rows, rel_grad):
+    pos_rows[...], neg_rows[...] = target_rows_of(slab[...].astype(BF16), ids_next)
+    rel_rows[...] = relation_rows_of(table[...], ids_next)
+    whole = dot(d_rel[...], places(ids[2:3], RPAD), ((1,), (1,)))
     for half in range(2):
-        d_rel_out[half] = d_rel[half]
-    slab_out[...], state_out[...] = trained(slab[...], state[...], ids[...], prod, g_neg, d_pos)
-
-
-def rel_half(half, ids, ids_next, d_rel, d_rel_next):
-    along = ((1,), (1,))
-    return dot(d_rel[half], places(ids[2:3], RPAD), along) + dot(
-        d_rel_next[half], places(ids_next[2:3], RPAD), along
-    )
+        rel_grad[half] = whole[half * HALF : half * HALF + HALF]
+
+
+def rel_half(half, ids, d_rel, rel_grad):
+    return rel_grad[half] + dot(d_rel[half], places(ids[2:3], RPAD), ((1,), (1,)))
 
 
 def second_kernel(
-    core, left, slab, table, ids, d_rel, ids_next, prod, g_neg, d_pos, d_rel_next, other
+    core, left, ids, pos_rows, neg_rows, rel_rows, rel_grad, prod, g_neg, d_pos, d_rel, other
 ):
-    ids_next[...] = unpacked_ids(left[...])
+    heads = dot(left[...], places(ids[0:1], ROWS))
     prod[...], g_neg[...], d_pos[...], parts = edge_terms(
-        left[:D], slab[...], table[...], ids_next[...]
+        heads, pos_rows[...], neg_rows[...], rel_rows[...]
     )
     for half in range(2):
-        d_rel_next[half] = parts[half]
-    other[...] = rel_half(1 - core[0], ids, ids_next, d_rel, d_rel_next)
+        d_rel[half] = parts[half]
+    other[...] = rel_half(1 - core[0], ids, d_rel, rel_grad)
 
 
 def finish_kernel(
-    core, slab, state, ids, ids_next, d_rel, prod, g_neg, d_pos, d_rel_next, mine, slab_out, state_out
+    core, slab, state, ids, rel_grad, prod, g_neg, d_pos, d_rel, mine, slab_out, state_out
 ):
-    mine[...] = rel_half(core[0], ids, ids_next, d_rel, d_rel_next)
+    mine[...] = rel_half(core[0], ids, d_rel, rel_grad)
     slab_out[...], state_out[...] = trained(
-        slab[...], state[...], ids_next[...], prod[...], g_neg[...], d_pos[...]
+        slab[...], state[...], ids[...], prod[...], g_neg[...], d_pos[...]
     )
 
 
@@ -228,26 +258,34 @@
         copies[copy] = code
 
 
-def update_kernel(core, ours, theirs, relation, state, relation_out, state_out, grads, last, wide, sems):
-    for half, codes in enumerate((ours, theirs)):
-        for part in range(OWNERS):
-            rows, lanes = place_of(part)
-            main, tail = decode(codes[part])
-            grads[half, rows, lanes] = main[: rows.stop - rows.start]
-            last[7 * part : 7 * part + 8] = tail
-        grads[half, :, RMAIN:] = last[:HALF]
-    both = grads[0], grads[1]
-    total = sum(jnp.sum(part * part, 0, keepdims=True) for part in both)[:, :NREL]
-    new_state = state[...] + total * (1.0 / D)
+def decoded_into(codes, grads, last):
+    for part in range(OWNERS):
+        rows, lanes = place_of(part)
+        main, tail = decode(codes[part])
+        grads[rows, lanes] = main[: rows.stop - rows.start]
+        last[7 * part : 7 * part + 8] = tail
+    grads[:, RMAIN:] = last[:HALF]
+    return jnp.sum(grads[...] * grads[...], 0, keepdims=True)
+
+
+def ours_kernel(codes, grads, squares, last):
+    squares[...] = decoded_into(codes, grads, last)
+
+
+def update_kernel(
+    core, ours, squares, codes, relation, state, relation_out, state_out, theirs, last, wide, sems
+):
+    total = squares[...] + decoded_into(codes, theirs, last)
+    new_state = state[...].reshape(1, NREL) + total[:, :NREL] * (1.0 / D)
     rate = 0.2 * lax.rsqrt(new_state)
-    state_out[...] = new_state
+    state_out[...] = new_state.reshape(NREL)
+    starts = core[0] * HALF, (1 - core[0]) * HALF
     copies = []
-    for half in range(2):
-        rows = slice(half * HALF, half * HALF + HALF)
-        grad = grads[core[0] if half == 0 else 1 - core[0]]
-        wide[half] = relation[rows] - grad[:, :NREL] * rate
-        copies.append(pltpu.make_async_copy(wide.at[half], relation_out.at[rows], sems.at[half]))
-        copies[half].start()
+    for place, (grad, start) in enumerate(zip((ours, theirs), starts)):
+        rows = pl.ds(pl.multiple_of(start, 8), HALF)
+        wide[rows] = relation[rows] - grad[:, :NREL] * rate
+        copies.append(pltpu.make_async_copy(wide.at[rows], relation_out.at[rows], sems.at[place]))
+        copies[place].start()
     for copy in copies:
         copy.wait()
 
@@ -264,48 +302,73 @@
     negative_rows,
 ):
     core = lax.axis_index("core").astype(jnp.int32)[None]
-    ids, message = call(
+    id_array = kept((8, EPAD), jnp.int32)
+    index_arrays = [
+        array[0, 0] for array in (source_rows, target_rows, relation_ids, negative_rows)
+    ]
+    dma = pltpu.SemaphoreType.DMA
+    ids, ids_next, left_low = call(
         prepare_kernel,
-        (kept((8, EPAD), jnp.int32), kept((D + 16, ROWS), BF16)),
+        (id_array, id_array, kept((D, ROWS), BF16)),
         left_embed[0].T,
-        source_rows[0, 0],
-        target_rows[0, 0],
-        relation_ids[0, 0],
-        negative_rows[0, 0],
-        scratch=[pltpu.VMEM((8, EPAD), jnp.int32)],
+        *index_arrays,
+        far_in=range(5),
+        scratch=[
+            pltpu.VMEM((D, ROWS), F32),
+            [pltpu.VMEM(array.shape, jnp.int32) for array in index_arrays],
+            dma((5,)),
+        ],
         name="prepare",
     )
-    message_next = from_next(message)
+    ids_next = from_next(ids_next)
+    left_next = from_next(left_low)
     relation = relation_embed.T
     slab_array, state_array = (D, ROWS), (1, ROWS)
     edge_array = kept((D, EPAD), BF16)
-    pair_array = kept((2, HALF, EPAD), BF16)
     half_array = kept((HALF, RPAD), F32)
     slab, state, d_rel, table = call(
         first_kernel,
-        (kept(slab_array, F32), kept(state_array, F32), pair_array, kept((D, RPAD), BF16)),
-        message,
+        (kept(slab_array, F32), kept(state_array, F32), edge_array, kept((D, RPAD), BF16)),
+        left_low,
+        ids,
         right_embed[0].T,
         right_state,
         relation,
+        far_in=(2, 3, 4),
+        scratch=[
+            pltpu.VMEM(slab_array, F32),
+            pltpu.VMEM(state_array, F32),
+            pltpu.VMEM((D, NREL), F32),
+            dma((6,)),
+        ],
+        name="first",
+    )
+    wide_array = kept((D, EPAD), F32)
+    pos_rows, neg_rows, rel_rows, rel_grad = call(
+        between_kernel,
+        (wide_array, kept((D, NPAD), BF16), wide_array, kept((2, HALF, RPAD), F32)),
+        slab,
+        table,
         ids,
-        name="first",
-    )
-    ids_next, prod, g_neg, d_pos, d_rel_next, other = call(
+        ids_next,
+        d_rel,
+        name="between",
+    )
+    prod, g_neg, d_pos, d_rel, other = call(
         second_kernel,
         (
-            kept((8, EPAD), jnp.int32),
             edge_array,
             kept((NPAD, EPAD), BF16),
             edge_array,
-            pair_array,
+            kept((2, HALF, EPAD), BF16),
             half_array,
         ),
-        message_next,
-        slab,
-        table,
-        ids,
-        d_rel,
+        left_next,
+        ids_next,
+        pos_rows,
+        neg_rows,
+        rel_rows,
+        rel_grad,
         core=core,
         name="second",
     )
@@ -315,13 +378,12 @@
         (half_array, struct(slab_array, F32), struct(state_array, F32)),
         slab,
         state,
-        ids,
         ids_next,
-        d_rel,
+        rel_grad,
         prod,
         g_neg,
         d_pos,
-        d_rel_next,
+        d_rel,
         core=core,
         name="finish",
     )
@@ -336,24 +398,28 @@
     copies = call(spread_kernel, parts, codes, name="spread")
     ours = lax.all_to_all(copies, CUBE, 0, 0, tiled=True)
     theirs = swap_core(ours)
+    grads, squares = call(
+        ours_kernel, (half_array, kept((1, RPAD), F32)), ours, scratch=[last], name="ours"
+    )
     relation_out, relation_state_out = call(
         update_kernel,
-        (struct((D, NREL), F32), struct((1, NREL), F32)),
-        ours,
+        (struct((D, NREL), F32), struct((NREL,), F32)),
+        grads,
+        squares,
         theirs,
         relation,
-        relation_state[None],
+        relation_state,
         core=core,
         far_out=(0,),
         scratch=[
-            pltpu.VMEM((2, HALF, RPAD), F32),
+            pltpu.VMEM((HALF, RPAD), F32),
             last,
-            pltpu.VMEM((2, HALF, NREL), F32),
-            pltpu.SemaphoreType.DMA((2,)),
+            pltpu.VMEM((D, NREL), F32),
+            dma((2,)),
         ],
         name="update",
     )
-    return (slab_out.T[None], state_out, relation_out.T, relation_state_out[0])
+    return (slab_out.T[None], state_out, relation_out.T, relation_state_out)
 
 
 def solution(mesh):

time: 99.7 us -> 97 us (0.973)
  local copies, waits for them, and re-layouts: 7.74 us -> 0.01 us
  Pallas kernels: 22.2 us -> 25.5 us
    unnamed x20 -> x4, local copies, waits for them, and re-layouts: 7.73 us -> 0.01 us
    pallas_call x8 -> x10, Pallas kernels: 22.2 us -> 25.5 us  [call(): pl.pallas_call(kernel, out_shape=out_shape, in_specs=in_specs, out_specs=...]
    ppermute x1 -> x2, waiting for transfers between devices: 0.01 us -> 1.3 us  [from_next(): lax.ppermute(block, BUCKET, [((i + 1) % count, i) for i in range(count)])]
    ppermute x1 -> x2, starting transfers between devices: 9.69 us -> 9.86 us  [from_next(): lax.ppermute(block, BUCKET, [((i + 1) % count, i) for i in range(count)])]
  transfers between devices with their start and end apart: 3 -> 4, of which waited for: 1 -> 2; matrix products, arithmetic and copies ran while one was open for 0% -> 0% of each run, Pallas kernels for 11% -> 17%
where the time goes in v5:
time: 97 us; the launch traced here: 96.7 us
  blocking collectives  53.3 us (55%)
  Pallas kernels  25.5 us (26%)
  starting transfers between devices  14 us (14%)
  waiting for transfers between devices  3.05 us (3%)
    pallas_call x10, Pallas kernels, call(): pl.pallas_call(kernel, out_shape=out_shape, in_specs=in_specs, out_specs=...  25.5 us
    all_to_all x1, blocking collectives, per_device(): got = lax.all_to_all(sent, CUBE, 0, 0, tiled=True)  20.3 us
    all_to_all x1, blocking collectives, per_device(): ours = lax.all_to_all(copies, CUBE, 0, 0, tiled=True)  18.5 us
    all_to_all x1, blocking collectives, per_device(): codes = lax.all_to_all(codes, 'z_hi', 0, 0, tiled=True)  14.5 us
    ppermute x2, starting transfers between devices, from_next(): lax.ppermute(block, BUCKET, [((i + 1) % count, i) for i in range(count)])  9.86 us
    ppermute x2, starting transfers between devices, swap_core(): return lax.ppermute(block, 'core', [(0, 1), (1, 0)])  4.11 us
  transfers between devices with their start and end apart: 4, of which 2 were waited for; matrix products, arithmetic and copies ran while one was open for 0% of the time, Pallas kernels for 17%

profile of v5, /device:TPU:1, one launch (start us, length us, event | category | flops | bytes accessed | tf_op | source)
XLA Modules:
  0.0 96.7 jit_solution(5967991497091967825)
XLA Ops:
  0.6 1.2 %prepare.1 = (s32[8,1024]{1,0:T(8,128)S(1)}, s32[8,1024]{1,0:T(8,128)S(1)}, bf16[400,512]{1,0:T(8,128)(2,1)S(1)}) custom-call(f32[400,512]{1,0:T(8,128)} %bitcast.18, s32[2,1000]{1,0:T(2,128)} %bitcast.20, s32[2,1000]{1,0:T(2,128)} %bitcast.21, s32[2,1000]{1,0:T(2,128)} %bitcast.22, s32[2,500]{1,0:T(2,128)} %bitcast.23), custom_call_target="tpu_custom_call" | custom-call | tf_op jit(solution)/shard_map/prepare/pallas_call | solution.py:55
  1.9 9.7 %collective-permute-start.1 = (bf16[400,512]{1,0:T(8,128)(2,1)S(1)}, bf16[400,512]{1,0:T(8,128)(2,1)S(1)}, u32[]{:S(2)}, u32[]{:S(2)}) collective-permute-start(bf16[400,512]{1,0:T(8,128)(2,1)S(1)} %get-tuple-element.27.left), channel_id=1, source_target_pairs={{4,0},{8,4},{12,8},{16,12},{20,16},{24,20},{28,24},{32,28},{36,32}... | collective-permute-start | bytes 1228808 | tf_op jit(solution)/shard_map/ppermute | solution.py:68
  11.6 0.2 collective-permute-start
  11.7 7.4 %first.1 = (f32[400,512]{1,0:T(8,128)S(1)}, f32[1,512]{1,0:T(1,128)S(1)}, bf16[400,1024]{1,0:T(8,128)(2,1)S(1)}, bf16[400,2176]{1,0:T(8,128)(2,1)S(1)}) custom-call(bf16[400,512]{1,0:T(8,128)(2,1)S(1)} %get-tuple-element.27.left, s32[8,1024]{1,0:T(8,128)S(1)} %get-tuple-element.28.ids, f32[400,512]{1,0:T(8,128)} %bitcast.19, f32[1,512]{1,0:T(1,128)} %state_far.1, ...), custom_call_target="tpu_custom_call" | custom-call | tf_op jit(solution)/shard_map/first/pallas_call | solution.py:55
  19.1 1.3 %collective-permute-done.ids_next.ids = s32[8,1024]{1,0:T(8,128)S(1)} collective-permute-done((s32[8,1024]{1,0:T(8,128)S(1)}, s32[8,1024]{1,0:T(8,128)S(1)}, u32[]{:S(2)}, u32[]{:S(2)}) %collective-permute-start) | collective-permute-done | bytes 32800 | tf_op jit(solution)/shard_map/ppermute | solution.py:68
  20.4 4.6 %between.1 = (f32[400,1024]{1,0:T(8,128)S(1)}, bf16[400,512]{1,0:T(8,128)(2,1)S(1)}, f32[400,1024]{1,0:T(8,128)S(1)}, f32[2,200,2176]{2,1,0:T(8,128)S(1)}) custom-call(f32[400,512]{1,0:T(8,128)S(1)} %get-tuple-element.29.slab, bf16[400,2176]{1,0:T(8,128)(2,1)S(1)} %get-tuple-element.32.table, s32[8,1024]{1,0:T(8,128)S(1)} %get-tuple-element.28.ids, ...), custom_call_target="tpu_custom_call" | custom-call | tf_op jit(solution)/shard_map/between/pallas_call | solution.py:55
  25.0 0.0 collective-permute-done.1.left
  25.0 4.0 %second.1 = (bf16[400,1024]{1,0:T(8,128)(2,1)S(1)}, bf16[512,1024]{1,0:T(8,128)(2,1)S(1)}, bf16[400,1024]{1,0:T(8,128)(2,1)S(1)}, bf16[2,200,1024]{2,1,0:T(8,128)(2,1)S(1)}, f32[200,2176]{1,0:T(8,128)S(1)}) custom-call(s32[1]{0:T(128)} %bitcast.core, bf16[400,512]{1,0:T(8,128)(2,1)S(1)} %collective-permute-done.1.left, ...), custom_call_target="tpu_custom_call" | custom-call | tf_op jit(solution)/shard_map/second/pallas_call | solution.py:55
  29.0 1.8 %collective-permute-start.2 = (f32[200,2176]{1,0:T(8,128)S(1)}, f32[200,2176]{1,0:T(8,128)S(1)}, u32[]{:S(2)}, u32[]{:S(2)}) collective-permute-start(f32[200,2176]{1,0:T(8,128)S(1)} %get-tuple-element.45), channel_id=1, source_target_pairs={{0,1},{1,0},{2,3},{3,2},{4,5},{5,4},{6,7},{7,6},{8,9},{9,8},{10,11... | collective-permute-start | bytes 5222408 | tf_op jit(solution)/shard_map/ppermute | solution.py:72
  30.8 3.8 %finish.1 = (f32[200,2176]{1,0:T(8,128)S(1)}, f32[400,512]{1,0:T(8,128)}, f32[1,512]{1,0:T(1,128)}) custom-call(s32[1]{0:T(128)} %bitcast.core, f32[400,512]{1,0:T(8,128)S(1)} %get-tuple-element.29.slab, f32[1,512]{1,0:T(1,128)S(1)} %get-tuple-element.30.state, s32[8,1024]{1,0:T(8,128)S(1)} %collective-permute-done.ids_next.ids, ...), custom_call_target="tpu_custom_call" | custom-call | tf_op jit(solution)/shard_map/finish/pallas_call | solution.py:55
  34.6 0.0 collective-permute-done.2.theirs
  34.6 0.5 send.1
  35.2 20.3 %all_to_all.15.parts = s16[32,112,128]{2,1,0:T(8,128)(2,1)S(1)} all-to-all(s16[32,112,128]{2,1,0:T(8,128)(2,1)S(1)} %send.1), channel_id=1, replica_groups=mesh['x'=4,'z_hi'=4,'z_lo'=2,'y_lo'=2,'y_hi'=2,'core'=2] {'x','z_lo','y_..., dimensions={0} | all-to-all | bytes 1835008 | tf_op jit(solution)/shard_map/all_to_all | solution.py:394
  55.5 0.3 gather.1
  55.8 14.5 %all_to_all.16.parts = s16[4,112,128]{2,1,0:T(8,128)(2,1)S(1)} all-to-all(s16[4,112,128]{2,1,0:T(8,128)(2,1)S(1)} %gather.1), channel_id=1, replica_groups=mesh['x'=4,'z_hi'=4,'z_lo'=2,'y_lo'=2,'y_hi'=2,'core'=2] {'z_hi'}, dimensions={0} | all-to-all | bytes 229376 | tf_op jit(solution)/shard_map/all_to_all | solution.py:397
  70.3 0.0 copy-start
  70.3 0.0 copy-start.1
  70.3 0.2 spread.1
  70.5 18.5 %all_to_all.17.codes = s16[32,112,128]{2,1,0:T(8,128)(2,1)S(1)} all-to-all(s16[32,112,128]{2,1,0:T(8,128)(2,1)S(1)} %spread.1), channel_id=1, replica_groups=mesh['x'=4,'z_hi'=4,'z_lo'=2,'y_lo'=2,'y_hi'=2,'core'=2] {'x','z_lo','y_..., dimensions={0} | all-to-all | bytes 1835008 | tf_op jit(solution)/shard_map/all_to_all | solution.py:399
  89.0 2.3 %collective-permute-start.3 = (s16[32,112,128]{2,1,0:T(8,128)(2,1)S(1)}, s16[32,112,128]{2,1,0:T(8,128)(2,1)S(1)}, u32[]{:S(2)}, u32[]{:S(2)}) collective-permute-start(s16[32,112,128]{2,1,0:T(8,128)(2,1)S(1)} %all_to_all.17.codes), channel_id=1, source_target_pairs={{0,1},{1,0},{2,3},{3,2},{4,5},{5,4},{6,7},{7,6},{8,9},{9,8},{10,11... | collective-permute-start | bytes 2752520 | tf_op jit(solution)/shard_map/ppermute | solution.py:72
  91.3 0.4 ours.1
  91.7 1.7 %collective-permute-done.3.codes = s16[32,112,128]{2,1,0:T(8,128)(2,1)S(1)} collective-permute-done((s16[32,112,128]{2,1,0:T(8,128)(2,1)S(1)}, s16[32,112,128]{2,1,0:T(8,128)(2,1)S(1)}, u32[]{:S(2)}, u32[]{:S(2)}) %collective-permute-start.3) | collective-permute-done | bytes 917536 | tf_op jit(solution)/shard_map/ppermute | solution.py:72
  93.4 0.0 copy-done
  93.4 0.0 copy-done.1
  93.4 3.1 %update.1 = (f32[400,2066]{1,0:T(8,128)}, f32[2066]{0:T(1024)}) custom-call(s32[1]{0:T(128)} %bitcast.core, f32[200,2176]{1,0:T(8,128)S(1)} %get-tuple-element.46.ours, f32[1,2176]{1,0:T(1,128)S(1)} %get-tuple-element.47.squares, s16[32,112,128]{2,1,0:T(8,128)(2,1)S(1)} %collective-permute-done.3.codes, f32[400,2066]{1,0:T(8,128)S(1)} %bitcast.17, ...), custom_call_target="tpu_custom_call" | custom-call | tf_op jit(solution)/shard_map/update/pallas_call | solution.py:55
Async XLA Ops:
  1.9 23.2 %collective-permute-start.1 = (bf16[400,512]{1,0:T(8,128)(2,1)S(1)}, bf16[400,512]{1,0:T(8,128)(2,1)S(1)}, u32[]{:S(2)}, u32[]{:S(2)}) collective-permute-start(bf16[400,512]{1,0:T(8,128)(2,1)S(1)} %get-tuple-element.27.left), channel_id=1, source_target_pairs={{4,0},{8,4},{12,8},{16,12},{20,16},{24,20},{28,24},{32,28},{36,32}... | collective-permute-start | bytes 1228808 | tf_op jit(solution)/shard_map/ppermute | solution.py:68
  11.6 8.8 %collective-permute-start = (s32[8,1024]{1,0:T(8,128)S(1)}, s32[8,1024]{1,0:T(8,128)S(1)}, u32[]{:S(2)}, u32[]{:S(2)}) collective-permute-start(s32[8,1024]{1,0:T(8,128)S(1)} %get-tuple-element.31), channel_id=1, source_target_pairs={{4,0},{8,4},{12,8},{16,12},{20,16},{24,20},{28,24},{32,28},{36,32}... | collective-permute-start | bytes 98312 | tf_op jit(solution)/shard_map/ppermute | solution.py:68
  29.0 5.6 %collective-permute-start.2 = (f32[200,2176]{1,0:T(8,128)S(1)}, f32[200,2176]{1,0:T(8,128)S(1)}, u32[]{:S(2)}, u32[]{:S(2)}) collective-permute-start(f32[200,2176]{1,0:T(8,128)S(1)} %get-tuple-element.45), channel_id=1, source_target_pairs={{0,1},{1,0},{2,3},{3,2},{4,5},{5,4},{6,7},{7,6},{8,9},{9,8},{10,11... | collective-permute-start | bytes 5222408 | tf_op jit(solution)/shard_map/ppermute | solution.py:72
  70.3 23.1 %copy-start = (f32[2066,400]{0,1:T(8,128)S(1)}, f32[2066,400]{0,1:T(8,128)}, u32[]{:S(2)}) copy-start(f32[2066,400]{0,1:T(8,128)} %param.12) | copy-start | bytes 9916804
  70.3 23.1 %copy-start.1 = (f32[2066]{0:T(1024)S(1)}, f32[2066]{0:T(1024)}, u32[]{:S(2)}) copy-start(f32[2066]{0:T(1024)} %state.1) | copy-start | bytes 24796
  89.0 4.4 %collective-permute-start.3 = (s16[32,112,128]{2,1,0:T(8,128)(2,1)S(1)}, s16[32,112,128]{2,1,0:T(8,128)(2,1)S(1)}, u32[]{:S(2)}, u32[]{:S(2)}) collective-permute-start(s16[32,112,128]{2,1,0:T(8,128)(2,1)S(1)} %all_to_all.17.codes), channel_id=1, source_target_pairs={{0,1},{1,0},{2,3},{3,2},{4,5},{5,4},{6,7},{7,6},{8,9},{9,8},{10,11... | collective-permute-start | bytes 2752520 | tf_op jit(solution)/shard_map/ppermute | solution.py:72

commit v6 on v5

--- a/solution.py
+++ b/solution.py
@@ -5,11 +5,11 @@
 from jax.experimental.pallas import tpu as pltpu
 from jax.sharding import PartitionSpec as P
 
-AXES = ("x", "z_hi", "z_lo", "y_lo", "y_hi", "core")
-BUCKET = ("x", "z_hi", "z_lo", "y_lo")
+AXES = ("x", "z", "y_lo", "y_hi", "core")
+BUCKET = ("x", "z", "y_lo")
 REPLICA = ("y_hi", "core")
-CUBE = ("x", "z_lo", "y_lo", "y_hi")
-OWNERS = 32
+PLANE = ("x", "y_lo", "y_hi")
+OWNERS = 16
 D = 400
 HALF = 200
 EPAD = 1024
@@ -19,8 +19,9 @@
 NREL = 2066
 RMAIN = 2048
 RPAD = 2176
-CUT = 104
-PART = 112
+SHARE = 13
+TAIL = 24
+PART = HALF + TAIL
 LEVELS = 32000.0
 F32 = jnp.float32
 BF16 = jnp.bfloat16
@@ -102,7 +103,7 @@
     d_prod = g_pos * pos_rows + dot(neg_rows, g_neg)
     p_re, p_im = d_prod[:HALF], d_prod[HALF:]
     d_rel = (p_re * h_re + p_im * h_im, p_im * h_re - p_re * h_im)
-    return prod, g_neg, d_pos, [part.astype(BF16) for part in d_rel]
+    return prod, g_neg, d_pos, d_rel
 
 
 def trained(slab, state, ids, prod, g_neg, d_pos):
@@ -114,7 +115,7 @@
     return slab - grad * (0.1 * lax.rsqrt(state)), state
 
 
-def prepare_kernel(left, src, dst, rel, neg, ids, next_ids, left_low, wide, places_in, sems):
+def prepare_kernel(left, src, dst, rel, neg, ids, message, wide, next_ids, places_in, sems):
     sources = (src, dst, rel, neg)
     copies = [pltpu.make_async_copy(left, wide, sems.at[4])]
     copies += [pltpu.make_async_copy(r, places_in[i], sems.at[i]) for i, r in enumerate(sources)]
@@ -127,15 +128,26 @@
     for place, source in enumerate(places_in):
         for step, step_ids in enumerate((ids, next_ids)):
             step_ids[place : place + 1, : source.shape[1]] = source[step : step + 1, :]
+    high, low = (next_ids[...] >> 6).astype(F32), (next_ids[...] & 63).astype(F32)
+    halves = slice(0, ROWS), slice(ROWS, EPAD)
+    packed = [part[:4, half] for part in (high, low) for half in halves]
+    message[D:] = jnp.concatenate(packed, 0).astype(BF16)
     copies[0].wait()
-    left_low[...] = wide[...].astype(BF16)
+    message[:D] = wide[...].astype(BF16)
+
+
+def unpacked_ids(message):
+    coded = message[D:].astype(F32)
+    halves = (coded[4 * i : 4 * i + 4] * 64.0 + coded[8 + 4 * i : 12 + 4 * i] for i in range(2))
+    rows = jnp.concatenate(list(halves), 1).astype(jnp.int32)
+    return jnp.concatenate([rows, rows], 0)
 
 
 CHUNKS = ((0, 104), (104, 200), (200, 304), (304, 400))
 
 
 def first_kernel(
-    left, ids, slab_far, state_far, relation_far, slab_out, state_out, d_rel_out, table, slab, state, relation, sems
+    left, ids, slab_far, state_far, relation_far, slab_out, state_out, rel_grad, table, slab, state, relation, sems
 ):
     copies = [
         pltpu.make_async_copy(slab_far, slab, sems.at[0]),
@@ -146,7 +158,7 @@
         copies.append(pltpu.make_async_copy(relation_far.at[rows], relation.at[rows], sems.at[2 + i]))
     for copy in copies:
         copy.start()
-    heads = dot(left[...], places(ids[0:1], ROWS))
+    heads = dot(left[:D], places(ids[0:1], ROWS))
     for copy in copies[:2]:
         copy.wait()
     pos_rows, neg_rows = target_rows_of(slab[...].astype(BF16), ids)
@@ -157,14 +169,8 @@
     table[:, RMAIN:NREL] = relation[:, RMAIN:].astype(BF16)
     rel_rows = relation_rows_of(table[...], ids)
     prod, g_neg, d_pos, d_rel = edge_terms(heads, pos_rows, neg_rows, rel_rows)
-    d_rel_out[:HALF], d_rel_out[HALF:] = d_rel
     slab_out[...], state_out[...] = trained(slab[...], state[...], ids[...], prod, g_neg, d_pos)
-
-
-def between_kernel(slab, table, ids, ids_next, d_rel, pos_rows, neg_rows, rel_rows, rel_grad):
-    pos_rows[...], neg_rows[...] = target_rows_of(slab[...].astype(BF16), ids_next)
-    rel_rows[...] = relation_rows_of(table[...], ids_next)
-    whole = dot(d_rel[...], places(ids[2:3], RPAD), ((1,), (1,)))
+    whole = dot(jnp.concatenate(d_rel, 0).astype(BF16), places(ids[2:3], RPAD), ((1,), (1,)))
     for half in range(2):
         rel_grad[half] = whole[half * HALF : half * HALF + HALF]
 
@@ -174,14 +180,15 @@
 
 
 def second_kernel(
-    core, left, ids, pos_rows, neg_rows, rel_rows, rel_grad, prod, g_neg, d_pos, d_rel, other
+    core, message, slab, table, rel_grad, ids, prod, g_neg, d_pos, d_rel, other
 ):
-    heads = dot(left[...], places(ids[0:1], ROWS))
-    prod[...], g_neg[...], d_pos[...], parts = edge_terms(
-        heads, pos_rows[...], neg_rows[...], rel_rows[...]
-    )
+    ids[...] = unpacked_ids(message[...])
+    heads = dot(message[:D], places(ids[0:1], ROWS))
+    rel_rows = relation_rows_of(table[...], ids)
+    pos_rows, neg_rows = target_rows_of(slab[...].astype(BF16), ids)
+    prod[...], g_neg[...], d_pos[...], parts = edge_terms(heads, pos_rows, neg_rows, rel_rows)
     for half in range(2):
-        d_rel[half] = parts[half]
+        d_rel[half] = parts[half].astype(BF16)
     other[...] = rel_half(1 - core[0], ids, d_rel, rel_grad)
 
 
@@ -202,40 +209,33 @@
 def encode(main, last):
     lane = lax.broadcasted_iota(jnp.int32, last.shape, 1)
     row = lax.broadcasted_iota(jnp.int32, last.shape, 0)
-    last = jnp.where(row < 7, last, 0.0)
+    last = jnp.where(row < SHARE, last, 0.0)
     main_power, last_power = power_of(main), power_of(last)
     main = jnp.round(main * (LEVELS * jnp.exp2(-main_power)))
     last = jnp.round(last * (LEVELS * jnp.exp2(-last_power)))
     last_power = pltpu.roll(jnp.broadcast_to(last_power, last.shape), 64, 1)
     last = jnp.where(lane < 64, last, last_power)
-    last = jnp.where(row == 7, jnp.broadcast_to(main_power, last.shape), last)
-    fill = [jnp.zeros((CUT - main.shape[0], 128), F32)] if main.shape[0] < CUT else []
-    return jnp.concatenate([main, *fill, last], 0).astype(jnp.int32).astype(jnp.int16)
+    last = jnp.where(row == TAIL - 1, jnp.broadcast_to(main_power, last.shape), last)
+    return jnp.concatenate([main, last], 0).astype(jnp.int32).astype(jnp.int16)
 
 
 def decode(codes):
     wide = codes.astype(jnp.int32).astype(F32)
-    main, last = wide[:CUT], wide[CUT:]
+    main, last = wide[:HALF], wide[HALF:]
     lane = lax.broadcasted_iota(jnp.int32, last.shape, 1)
     row = lax.broadcasted_iota(jnp.int32, last.shape, 0)
-    main = main * (jnp.exp2(last[7:8]) * (1.0 / LEVELS))
+    main = main * (jnp.exp2(last[TAIL - 1 :]) * (1.0 / LEVELS))
     last_step = jnp.exp2(pltpu.roll(last, 64, 1)) * (1.0 / LEVELS)
-    valid = jnp.logical_and(lane < NREL - RMAIN, row < 7)
+    valid = jnp.logical_and(lane < NREL - RMAIN, row < SHARE)
     return main, jnp.where(valid, last * last_step, 0.0)
-
-
-def place_of(part):
-    tile, low = divmod(part, 2)
-    rows = slice(CUT, HALF) if low else slice(0, CUT)
-    return rows, slice(128 * tile, 128 * tile + 128)
 
 
 def send_kernel(mine, theirs, codes, last):
     last[HALF:] = jnp.zeros((last.shape[0] - HALF, 128), F32)
     last[:HALF] = mine[:, RMAIN:] + theirs[:, RMAIN:]
     for part in range(OWNERS):
-        at = place_of(part)
-        codes[part] = encode(mine[at] + theirs[at], last[7 * part : 7 * part + 8])
+        at = slice(None), slice(128 * part, 128 * part + 128)
+        codes[part] = encode(mine[at] + theirs[at], last[SHARE * part : SHARE * part + TAIL])
 
 
 def gather_kernel(parts, codes):
@@ -260,10 +260,9 @@
 
 def decoded_into(codes, grads, last):
     for part in range(OWNERS):
-        rows, lanes = place_of(part)
         main, tail = decode(codes[part])
-        grads[rows, lanes] = main[: rows.stop - rows.start]
-        last[7 * part : 7 * part + 8] = tail
+        grads[:, 128 * part : 128 * part + 128] = main
+        last[SHARE * part : SHARE * part + TAIL] = tail
     grads[:, RMAIN:] = last[:HALF]
     return jnp.sum(grads[...] * grads[...], 0, keepdims=True)
 
@@ -307,29 +306,34 @@
         array[0, 0] for array in (source_rows, target_rows, relation_ids, negative_rows)
     ]
     dma = pltpu.SemaphoreType.DMA
-    ids, ids_next, left_low = call(
+    ids, message = call(
         prepare_kernel,
-        (id_array, id_array, kept((D, ROWS), BF16)),
+        (id_array, kept((D + 16, ROWS), BF16)),
         left_embed[0].T,
         *index_arrays,
         far_in=range(5),
         scratch=[
             pltpu.VMEM((D, ROWS), F32),
+            id_array,
             [pltpu.VMEM(array.shape, jnp.int32) for array in index_arrays],
             dma((5,)),
         ],
         name="prepare",
     )
-    ids_next = from_next(ids_next)
-    left_next = from_next(left_low)
+    message_next = from_next(message)
     relation = relation_embed.T
     slab_array, state_array = (D, ROWS), (1, ROWS)
     edge_array = kept((D, EPAD), BF16)
     half_array = kept((HALF, RPAD), F32)
-    slab, state, d_rel, table = call(
+    slab, state, rel_grad, table = call(
         first_kernel,
-        (kept(slab_array, F32), kept(state_array, F32), edge_array, kept((D, RPAD), BF16)),
-        left_low,
+        (
+            kept(slab_array, F32),
+            kept(state_array, F32),
+            kept((2, HALF, RPAD), F32),
+            kept((D, RPAD), BF16),
+        ),
+        message,
         ids,
         right_embed[0].T,
         right_state,
@@ -343,31 +347,19 @@
         ],
         name="first",
     )
-    wide_array = kept((D, EPAD), F32)
-    pos_rows, neg_rows, rel_rows, rel_grad = call(
-        between_kernel,
-        (wide_array, kept((D, NPAD), BF16), wide_array, kept((2, HALF, RPAD), F32)),
-        slab,
-        table,
-        ids,
-        ids_next,
-        d_rel,
-        name="between",
-    )
-    prod, g_neg, d_pos, d_rel, other = call(
+    ids_next, prod, g_neg, d_pos, d_rel, other = call(
         second_kernel,
         (
+            id_array,
             edge_array,
             kept((NPAD, EPAD), BF16),
             edge_array,
             kept((2, HALF, EPAD), BF16),
             half_array,
         ),
-        left_next,
-        ids_next,
-        pos_rows,
-        neg_rows,
-        rel_rows,
+        message_next,
+        slab,
+        table,
         rel_grad,
         core=core,
         name="second",
@@ -391,12 +383,12 @@
     last = pltpu.VMEM((232, 128), F32)
     parts = kept((OWNERS, *part), jnp.int16)
     sent = call(send_kernel, parts, mine, theirs, scratch=[last], name="send")
-    got = lax.all_to_all(sent, CUBE, 0, 0, tiled=True)
-    count = lax.axis_size("z_hi")
+    got = lax.all_to_all(sent, PLANE, 0, 0, tiled=True)
+    count = lax.axis_size("z")
     codes = call(gather_kernel, kept((count, *part), jnp.int16), got, name="gather")
-    codes = lax.all_to_all(codes, "z_hi", 0, 0, tiled=True)
+    codes = lax.all_to_all(codes, "z", 0, 0, tiled=True)
     copies = call(spread_kernel, parts, codes, name="spread")
-    ours = lax.all_to_all(copies, CUBE, 0, 0, tiled=True)
+    ours = lax.all_to_all(copies, PLANE, 0, 0, tiled=True)
     theirs = swap_core(ours)
     grads, squares = call(
         ours_kernel, (half_array, kept((1, RPAD), F32)), ours, scratch=[last], name="ours"
@@ -423,7 +415,7 @@
 
 
 def solution(mesh):
-    split = jax.sharding.Mesh(mesh.devices.reshape(4, 4, 2, 2, 2, 2), AXES)
+    split = jax.sharding.Mesh(mesh.devices.reshape(4, 8, 2, 2, 2), AXES)
     in_specs = (
         P(REPLICA, BUCKET, None),
         P(REPLICA, BUCKET, None),

time: 97 us -> 99 us (1.021)
  blocking collectives: 53.3 us -> 56.2 us
  waiting for transfers between devices: 3.05 us -> 1.72 us
    all_to_all x3, blocking collectives: 53.3 us -> 56.2 us  [the longest x1 20.2 us: per_device(): codes = lax.all_to_all(codes, 'z', 0, 0, tiled=True)]
    ppermute x2 -> x1, waiting for transfers between devices: 1.3 us -> 0.01 us  [from_next(): lax.ppermute(block, BUCKET, [((i + 1) % count, i) for i in range(count)])]
    pallas_call x10 -> x9, Pallas kernels: 25.5 us -> 25.3 us  [call(): pl.pallas_call(kernel, out_shape=out_shape, in_specs=in_specs, out_specs=...]
    ppermute x2 -> x1, starting transfers between devices: 9.86 us -> 9.69 us  [from_next(): lax.ppermute(block, BUCKET, [((i + 1) % count, i) for i in range(count)])]
  transfers between devices with their start and end apart: 4 -> 3, of which waited for: 2 -> 1; matrix products, arithmetic and copies ran while one was open for 0% -> 0% of each run, Pallas kernels for 17% -> 14%
where the time goes in v6:
time: 99 us; the launch traced here: 98.8 us
  blocking collectives  56.2 us (57%)
  Pallas kernels  25.3 us (26%)
  starting transfers between devices  14.7 us (15%)
  waiting for transfers between devices  1.72 us (2%)
    pallas_call x9, Pallas kernels, call(): pl.pallas_call(kernel, out_shape=out_shape, in_specs=in_specs, out_specs=...  25.3 us
    all_to_all x1, blocking collectives, per_device(): codes = lax.all_to_all(codes, 'z', 0, 0, tiled=True)  20.2 us
    all_to_all x1, blocking collectives, per_device(): got = lax.all_to_all(sent, PLANE, 0, 0, tiled=True)  19.4 us
    all_to_all x1, blocking collectives, per_device(): ours = lax.all_to_all(copies, PLANE, 0, 0, tiled=True)  16.6 us
    ppermute x1, starting transfers between devices, from_next(): lax.ppermute(block, BUCKET, [((i + 1) % count, i) for i in range(count)])  9.69 us
    ppermute x2, starting transfers between devices, swap_core(): return lax.ppermute(block, 'core', [(0, 1), (1, 0)])  5.05 us
  transfers between devices with their start and end apart: 3, of which 1 were waited for; matrix products, arithmetic and copies ran while one was open for 0% of the time, Pallas kernels for 14%

profile of v6, /device:TPU:1, one launch (start us, length us, event | category | flops | bytes accessed | tf_op | source)
XLA Modules:
  0.0 98.8 jit_solution(2661443468932773122)
XLA Ops:
  0.6 1.2 %prepare.1 = (s32[8,1024]{1,0:T(8,128)S(1)}, bf16[416,512]{1,0:T(8,128)(2,1)S(1)}) custom-call(f32[400,512]{1,0:T(8,128)} %bitcast.18, s32[2,1000]{1,0:T(2,128)} %bitcast.20, s32[2,1000]{1,0:T(2,128)} %bitcast.21, s32[2,1000]{1,0:T(2,128)} %bitcast.22, s32[2,500]{1,0:T(2,128)} %bitcast.23), custom_call_target="tpu_custom_call" | custom-call | tf_op jit(solution)/shard_map/prepare/pallas_call | solution.py:56
  1.9 9.7 %collective-permute-start = (bf16[416,512]{1,0:T(8,128)(2,1)S(1)}, bf16[416,512]{1,0:T(8,128)(2,1)S(1)}, u32[]{:S(2)}, u32[]{:S(2)}) collective-permute-start(bf16[416,512]{1,0:T(8,128)(2,1)S(1)} %get-tuple-element.23.left), channel_id=1, source_target_pairs={{4,0},{8,4},{12,8},{16,12},{20,16},{24,20},{28,24},{32,28},{36,32}... | collective-permute-start | bytes 1277960 | tf_op jit(solution)/shard_map/ppermute | solution.py:69
  11.6 9.4 %first.1 = (f32[400,512]{1,0:T(8,128)S(1)}, f32[1,512]{1,0:T(1,128)S(1)}, f32[2,200,2176]{2,1,0:T(8,128)S(1)}, bf16[400,2176]{1,0:T(8,128)(2,1)S(1)}) custom-call(bf16[416,512]{1,0:T(8,128)(2,1)S(1)} %get-tuple-element.23.left, s32[8,1024]{1,0:T(8,128)S(1)} %get-tuple-element.24.ids, f32[400,512]{1,0:T(8,128)} %bitcast.19, f32[1,512]{1,0:T(1,128)} %state_far.1, ...), custom_call_target="tpu_custom_call" | custom-call | tf_op jit(solution)/shard_map/first/pallas_call | solution.py:56
  20.9 0.0 collective-permute-done.message
  20.9 6.2 %second.1 = (s32[8,1024]{1,0:T(8,128)S(1)}, bf16[400,1024]{1,0:T(8,128)(2,1)S(1)}, bf16[512,1024]{1,0:T(8,128)(2,1)S(1)}, bf16[400,1024]{1,0:T(8,128)(2,1)S(1)},...) custom-call(s32[1]{0:T(128)} %bitcast.core, bf16[416,512]{1,0:T(8,128)(2,1)S(1)} %collective-permute-done.message, ...), custom_call_target="tpu_custom_call" | custom-call | tf_op jit(solution)/shard_map/second/pallas_call | solution.py:56
  27.1 1.2 %collective-permute-start.1 = (f32[200,2176]{1,0:T(8,128)S(1)}, f32[200,2176]{1,0:T(8,128)S(1)}, u32[]{:S(2)}, u32[]{:S(2)}) collective-permute-start(f32[200,2176]{1,0:T(8,128)S(1)} %get-tuple-element.37), channel_id=1, source_target_pairs={{0,1},{1,0},{2,3},{3,2},{4,5},{5,4},{6,7},{7,6},{8,9},{9,8},{10,11... | collective-permute-start | bytes 5222408 | tf_op jit(solution)/shard_map/ppermute | solution.py:73
  28.3 3.8 %finish.1 = (f32[200,2176]{1,0:T(8,128)S(1)}, f32[400,512]{1,0:T(8,128)}, f32[1,512]{1,0:T(1,128)}) custom-call(s32[1]{0:T(128)} %bitcast.core, f32[400,512]{1,0:T(8,128)S(1)} %get-tuple-element.25.slab, f32[1,512]{1,0:T(1,128)S(1)} %get-tuple-element.26.state, s32[8,1024]{1,0:T(8,128)S(1)} %get-tuple-element.29.ids, ...), custom_call_target="tpu_custom_call" | custom-call | tf_op jit(solution)/shard_map/finish/pallas_call | solution.py:56
  32.1 0.0 collective-permute-done.1.theirs
  32.1 0.5 send.1
  32.6 19.4 %all_to_all.15.parts = s16[16,224,128]{2,1,0:T(8,128)(2,1)S(1)} all-to-all(s16[16,224,128]{2,1,0:T(8,128)(2,1)S(1)} %send.1), channel_id=1, replica_groups=mesh['x'=4,'z'=8,'y_lo'=2,'y_hi'=2,'core'=2] {'x','y_lo','y_hi'}, dimensions={0} | all-to-all | bytes 1835008 | tf_op jit(solution)/shard_map/all_to_all | solution.py:386
  52.0 0.4 gather.1
  52.4 20.2 %all_to_all.16.parts = s16[8,224,128]{2,1,0:T(8,128)(2,1)S(1)} all-to-all(s16[8,224,128]{2,1,0:T(8,128)(2,1)S(1)} %gather.1), channel_id=1, replica_groups=mesh['x'=4,'z'=8,'y_lo'=2,'y_hi'=2,'core'=2] {'z'}, dimensions={0} | all-to-all | bytes 917504 | tf_op jit(solution)/shard_map/all_to_all | solution.py:389
  72.6 0.0 copy-start
  72.6 0.0 copy-start.1
  72.6 0.3 spread.1
  72.9 16.6 %all_to_all.17.codes = s16[16,224,128]{2,1,0:T(8,128)(2,1)S(1)} all-to-all(s16[16,224,128]{2,1,0:T(8,128)(2,1)S(1)} %spread.1), channel_id=1, replica_groups=mesh['x'=4,'z'=8,'y_lo'=2,'y_hi'=2,'core'=2] {'x','y_lo','y_hi'}, dimensions={0} | all-to-all | bytes 1835008 | tf_op jit(solution)/shard_map/all_to_all | solution.py:391
  89.5 3.8 %collective-permute-start.2 = (s16[16,224,128]{2,1,0:T(8,128)(2,1)S(1)}, s16[16,224,128]{2,1,0:T(8,128)(2,1)S(1)}, u32[]{:S(2)}, u32[]{:S(2)}) collective-permute-start(s16[16,224,128]{2,1,0:T(8,128)(2,1)S(1)} %all_to_all.17.codes), channel_id=1, source_target_pairs={{0,1},{1,0},{2,3},{3,2},{4,5},{5,4},{6,7},{7,6},{8,9},{9,8},{10,11... | collective-permute-start | bytes 2752520 | tf_op jit(solution)/shard_map/ppermute | solution.py:73
  93.4 0.4 ours.1
  93.7 1.7 %collective-permute-done.2.codes = s16[16,224,128]{2,1,0:T(8,128)(2,1)S(1)} collective-permute-done((s16[16,224,128]{2,1,0:T(8,128)(2,1)S(1)}, s16[16,224,128]{2,1,0:T(8,128)(2,1)S(1)}, u32[]{:S(2)}, u32[]{:S(2)}) %collective-permute-start.2) | collective-permute-done | bytes 917536 | tf_op jit(solution)/shard_map/ppermute | solution.py:73
  95.5 0.0 copy-done
  95.5 0.0 copy-done.1
  95.5 3.2 %update.1 = (f32[400,2066]{1,0:T(8,128)}, f32[2066]{0:T(1024)}) custom-call(s32[1]{0:T(128)} %bitcast.core, f32[200,2176]{1,0:T(8,128)S(1)} %get-tuple-element.38.ours, f32[1,2176]{1,0:T(1,128)S(1)} %get-tuple-element.39.squares, s16[16,224,128]{2,1,0:T(8,128)(2,1)S(1)} %collective-permute-done.2.codes, f32[400,2066]{1,0:T(8,128)S(1)} %bitcast.17, ...), custom_call_target="tpu_custom_call" | custom-call | tf_op jit(solution)/shard_map/update/pallas_call | solution.py:56
Async XLA Ops:
  1.9 19.1 %collective-permute-start = (bf16[416,512]{1,0:T(8,128)(2,1)S(1)}, bf16[416,512]{1,0:T(8,128)(2,1)S(1)}, u32[]{:S(2)}, u32[]{:S(2)}) collective-permute-start(bf16[416,512]{1,0:T(8,128)(2,1)S(1)} %get-tuple-element.23.left), channel_id=1, source_target_pairs={{4,0},{8,4},{12,8},{16,12},{20,16},{24,20},{28,24},{32,28},{36,32}... | collective-permute-start | bytes 1277960 | tf_op jit(solution)/shard_map/ppermute | solution.py:69
  27.1 5.0 %collective-permute-start.1 = (f32[200,2176]{1,0:T(8,128)S(1)}, f32[200,2176]{1,0:T(8,128)S(1)}, u32[]{:S(2)}, u32[]{:S(2)}) collective-permute-start(f32[200,2176]{1,0:T(8,128)S(1)} %get-tuple-element.37), channel_id=1, source_target_pairs={{0,1},{1,0},{2,3},{3,2},{4,5},{5,4},{6,7},{7,6},{8,9},{9,8},{10,11... | collective-permute-start | bytes 5222408 | tf_op jit(solution)/shard_map/ppermute | solution.py:73
  72.6 22.8 %copy-start = (f32[2066,400]{0,1:T(8,128)S(1)}, f32[2066,400]{0,1:T(8,128)}, u32[]{:S(2)}) copy-start(f32[2066,400]{0,1:T(8,128)} %param.12) | copy-start | bytes 9916804
  72.6 22.8 %copy-start.1 = (f32[2066]{0:T(1024)S(1)}, f32[2066]{0:T(1024)}, u32[]{:S(2)}) copy-start(f32[2066]{0:T(1024)} %state.1) | copy-start | bytes 24796
  89.5 5.9 %collective-permute-start.2 = (s16[16,224,128]{2,1,0:T(8,128)(2,1)S(1)}, s16[16,224,128]{2,1,0:T(8,128)(2,1)S(1)}, u32[]{:S(2)}, u32[]{:S(2)}) collective-permute-start(s16[16,224,128]{2,1,0:T(8,128)(2,1)S(1)} %all_to_all.17.codes), channel_id=1, source_target_pairs={{0,1},{1,0},{2,3},{3,2},{4,5},{5,4},{6,7},{7,6},{8,9},{9,8},{10,11... | collective-permute-start | bytes 2752520 | tf_op jit(solution)/shard_map/ppermute | solution.py:73

commit v7 on v5

--- a/solution.py
+++ b/solution.py
@@ -42,7 +42,7 @@
     return pltpu.with_memory_space_constraint(array, pltpu.HBM)
 
 
-def call(kernel, out_shape, *args, core=None, scratch=(), far_in=(), far_out=(), name, limit=32):
+def call(kernel, out_shape, *args, core=None, scratch=(), far_in=(), far_out=(), name, flops=None):
     vmem = pl.BlockSpec(memory_space=pltpu.VMEM)
     far = pl.BlockSpec(memory_space=pltpu.HBM)
     several = isinstance(out_shape, tuple)
@@ -58,7 +58,8 @@
         in_specs=in_specs,
         out_specs=specs if several else specs[0],
         scratch_shapes=scratch,
-        compiler_params=pltpu.CompilerParams(vmem_limit_bytes=limit * 1024 * 1024),
+        compiler_params=pltpu.CompilerParams(vmem_limit_bytes=32 * 1024 * 1024),
+        cost_estimate=flops and pl.CostEstimate(flops=flops, bytes_accessed=0, transcendentals=0),
         name=name,
     )(*args)
 
@@ -279,13 +280,15 @@
     new_state = state[...].reshape(1, NREL) + total[:, :NREL] * (1.0 / D)
     rate = 0.2 * lax.rsqrt(new_state)
     state_out[...] = new_state.reshape(NREL)
-    starts = core[0] * HALF, (1 - core[0]) * HALF
     copies = []
-    for place, (grad, start) in enumerate(zip((ours, theirs), starts)):
-        rows = pl.ds(pl.multiple_of(start, 8), HALF)
-        wide[rows] = relation[rows] - grad[:, :NREL] * rate
-        copies.append(pltpu.make_async_copy(wide.at[rows], relation_out.at[rows], sems.at[place]))
-        copies[place].start()
+    for grad, half in ((ours, core[0]), (theirs, 1 - core[0])):
+        for start, stop in ((0, 56), (56, 104), (104, 152), (152, 200)):
+            rows = pl.ds(pl.multiple_of(half * HALF + start, 8), stop - start)
+            wide[rows] = relation[rows] - grad[start:stop, :NREL] * rate
+            copies.append(
+                pltpu.make_async_copy(wide.at[rows], relation_out.at[rows], sems.at[len(copies)])
+            )
+            copies[-1].start()
     for copy in copies:
         copy.wait()
 
@@ -341,6 +344,7 @@
             pltpu.VMEM((D, NREL), F32),
             dma((6,)),
         ],
+        flops=1000,
         name="first",
     )
     wide_array = kept((D, EPAD), F32)
@@ -352,6 +356,7 @@
         ids,
         ids_next,
         d_rel,
+        flops=2 * 10**10,
         name="between",
     )
     prod, g_neg, d_pos, d_rel, other = call(
@@ -415,7 +420,7 @@
             pltpu.VMEM((HALF, RPAD), F32),
             last,
             pltpu.VMEM((D, NREL), F32),
-            dma((2,)),
+            dma((8,)),
         ],
         name="update",
     )

time: 97 us -> 93.8 us (0.967)
  blocking collectives: 53.3 us -> 50 us
  local copies, waits for them, and re-layouts: 0.01 us -> 2.04 us
  waiting for transfers between devices: 3.05 us -> 1.76 us
    all_to_all x1, blocking collectives: 14.5 us -> 10.8 us  [per_device(): codes = lax.all_to_all(codes, 'z_hi', 0, 0, tiled=True)]
    unnamed x4 -> x8, local copies, waits for them, and re-layouts: 0.01 us -> 2.04 us
    ppermute x2, waiting for transfers between devices: 1.3 us -> 0.01 us  [from_next(): lax.ppermute(block, BUCKET, [((i + 1) % count, i) for i in range(count)])]
  transfers between devices with their start and end apart: 4 -> 4, of which waited for: 2 -> 1; matrix products, arithmetic and copies ran while one was open for 0% -> 0% of each run, Pallas kernels for 17% -> 17%
where the time goes in v7:
time: 93.8 us; the launch traced here: 93.6 us
  blocking collectives  50 us (53%)
  Pallas kernels  25.3 us (27%)
  starting transfers between devices  13.6 us (14%)
  local copies, waits for them, and re-layouts  2.04 us (2%)
  waiting for transfers between devices  1.76 us (2%)
    pallas_call x10, Pallas kernels, call(): pl.pallas_call(kernel, out_shape=out_shape, in_specs=in_specs, out_specs=...  25.3 us
    all_to_all x1, blocking collectives, per_device(): got = lax.all_to_all(sent, CUBE, 0, 0, tiled=True)  20.6 us
    all_to_all x1, blocking collectives, per_device(): ours = lax.all_to_all(copies, CUBE, 0, 0, tiled=True)  18.5 us
    all_to_all x1, blocking collectives, per_device(): codes = lax.all_to_all(codes, 'z_hi', 0, 0, tiled=True)  10.8 us
    ppermute x2, starting transfers between devices, from_next(): lax.ppermute(block, BUCKET, [((i + 1) % count, i) for i in range(count)])  9.86 us
    ppermute x2, starting transfers between devices, swap_core(): return lax.ppermute(block, 'core', [(0, 1), (1, 0)])  3.79 us
    unnamed x8, local copies, waits for them, and re-layouts  2.04 us
  transfers between devices with their start and end apart: 4, of which 1 were waited for; matrix products, arithmetic and copies ran while one was open for 0% of the time, Pallas kernels for 17%

profile of v7, /device:TPU:1, one launch (start us, length us, event | category | flops | bytes accessed | tf_op | source)
XLA Modules:
  0.0 93.6 jit_solution(2286530738524838437)
XLA Ops:
  0.6 1.2 %prepare.1 = (s32[8,1024]{1,0:T(8,128)S(1)}, s32[8,1024]{1,0:T(8,128)S(1)}, bf16[400,512]{1,0:T(8,128)(2,1)S(1)}) custom-call(f32[400,512]{1,0:T(8,128)} %bitcast.18, s32[2,1000]{1,0:T(2,128)} %bitcast.20, s32[2,1000]{1,0:T(2,128)} %bitcast.21, s32[2,1000]{1,0:T(2,128)} %bitcast.22, s32[2,500]{1,0:T(2,128)} %bitcast.23), custom_call_target="tpu_custom_call" | custom-call | tf_op jit(solution)/shard_map/prepare/pallas_call | solution.py:55
  1.9 9.7 %collective-permute-start = (s32[8,1024]{1,0:T(8,128)S(1)}, s32[8,1024]{1,0:T(8,128)S(1)}, u32[]{:S(2)}, u32[]{:S(2)}) collective-permute-start(s32[8,1024]{1,0:T(8,128)S(1)} %get-tuple-element.31), channel_id=1, source_target_pairs={{4,0},{8,4},{12,8},{16,12},{20,16},{24,20},{28,24},{32,28},{36,32}... | collective-permute-start | bytes 98312 | tf_op jit(solution)/shard_map/ppermute | solution.py:69
  11.6 0.2 collective-permute-start.1
  11.7 7.4 %first.1 = (f32[400,512]{1,0:T(8,128)S(1)}, f32[1,512]{1,0:T(1,128)S(1)}, bf16[400,1024]{1,0:T(8,128)(2,1)S(1)}, bf16[400,2176]{1,0:T(8,128)(2,1)S(1)}) custom-call(bf16[400,512]{1,0:T(8,128)(2,1)S(1)} %get-tuple-element.27.left, s32[8,1024]{1,0:T(8,128)S(1)} %get-tuple-element.28.ids, f32[400,512]{1,0:T(8,128)} %bitcast.19, f32[1,512]{1,0:T(1,128)} %state_far.1, ...), custom_call_target="tpu_custom_call" | custom-call | flops 1000 | tf_op jit(solution)/shard_map/first/pallas_call | solution.py:55
  19.1 0.0 copy-start.2
  19.1 0.9 copy-done.2
  20.0 0.0 collective-permute-done.ids_next.ids
  20.0 0.0 copy-start.3
  20.0 1.1 %copy-done.3 = bf16[400,1024]{1,0:T(8,128)(2,1)S(1)} copy-done((bf16[400,1024]{1,0:T(8,128)(2,1)S(1)}, bf16[400,1024]{1,0:T(8,128)(2,1)}, u32[]{:S(2)}) %copy-start.3) | copy-done | bytes 819224
  21.1 4.6 %between.1 = (f32[400,1024]{1,0:T(8,128)S(1)}, bf16[400,512]{1,0:T(8,128)(2,1)S(1)}, f32[400,1024]{1,0:T(8,128)S(1)}, f32[2,200,2176]{2,1,0:T(8,128)S(1)}) custom-call(f32[400,512]{1,0:T(8,128)S(1)} %get-tuple-element.29.slab, bf16[400,2176]{1,0:T(8,128)(2,1)S(1)} %get-tuple-element.32.table, s32[8,1024]{1,0:T(8,128)S(1)} %get-tuple-element.28.ids, ...), custom_call_target="tpu_custom_call" | custom-call | flops 20000000000 | tf_op jit(solution)/shard_map/between/pallas_call | solution.py:55
  25.8 0.0 collective-permute-done.1.left
  25.8 4.0 %second.1 = (bf16[400,1024]{1,0:T(8,128)(2,1)S(1)}, bf16[512,1024]{1,0:T(8,128)(2,1)S(1)}, bf16[400,1024]{1,0:T(8,128)(2,1)S(1)}, bf16[2,200,1024]{2,1,0:T(8,128)(2,1)S(1)}, f32[200,2176]{1,0:T(8,128)S(1)}) custom-call(s32[1]{0:T(128)} %bitcast.core, bf16[400,512]{1,0:T(8,128)(2,1)S(1)} %collective-permute-done.1.left, ...), custom_call_target="tpu_custom_call" | custom-call | tf_op jit(solution)/shard_map/second/pallas_call | solution.py:55
  29.8 1.5 %collective-permute-start.2 = (f32[200,2176]{1,0:T(8,128)S(1)}, f32[200,2176]{1,0:T(8,128)S(1)}, u32[]{:S(2)}, u32[]{:S(2)}) collective-permute-start(f32[200,2176]{1,0:T(8,128)S(1)} %get-tuple-element.45), channel_id=1, source_target_pairs={{0,1},{1,0},{2,3},{3,2},{4,5},{5,4},{6,7},{7,6},{8,9},{9,8},{10,11... | collective-permute-start | bytes 5222408 | tf_op jit(solution)/shard_map/ppermute | solution.py:73
  31.3 3.8 %finish.1 = (f32[200,2176]{1,0:T(8,128)S(1)}, f32[400,512]{1,0:T(8,128)}, f32[1,512]{1,0:T(1,128)}) custom-call(s32[1]{0:T(128)} %bitcast.core, f32[400,512]{1,0:T(8,128)S(1)} %get-tuple-element.29.slab, f32[1,512]{1,0:T(1,128)S(1)} %get-tuple-element.30.state, s32[8,1024]{1,0:T(8,128)S(1)} %collective-permute-done.ids_next.ids, ...), custom_call_target="tpu_custom_call" | custom-call | tf_op jit(solution)/shard_map/finish/pallas_call | solution.py:55
  35.0 0.0 collective-permute-done.2.theirs
  35.0 0.5 send.1
  35.6 20.6 %all_to_all.15.parts = s16[32,112,128]{2,1,0:T(8,128)(2,1)S(1)} all-to-all(s16[32,112,128]{2,1,0:T(8,128)(2,1)S(1)} %send.1), channel_id=1, replica_groups=mesh['x'=4,'z_hi'=4,'z_lo'=2,'y_lo'=2,'y_hi'=2,'core'=2] {'x','z_lo','y_..., dimensions={0} | all-to-all | bytes 1835008 | tf_op jit(solution)/shard_map/all_to_all | solution.py:399
  56.2 0.3 gather.1
  56.6 10.8 %all_to_all.16.parts = s16[4,112,128]{2,1,0:T(8,128)(2,1)S(1)} all-to-all(s16[4,112,128]{2,1,0:T(8,128)(2,1)S(1)} %gather.1), channel_id=1, replica_groups=mesh['x'=4,'z_hi'=4,'z_lo'=2,'y_lo'=2,'y_hi'=2,'core'=2] {'z_hi'}, dimensions={0} | all-to-all | bytes 229376 | tf_op jit(solution)/shard_map/all_to_all | solution.py:402
  67.4 0.0 copy-start
  67.4 0.0 copy-start.1
  67.4 0.2 spread.1
  67.6 18.5 %all_to_all.17.codes = s16[32,112,128]{2,1,0:T(8,128)(2,1)S(1)} all-to-all(s16[32,112,128]{2,1,0:T(8,128)(2,1)S(1)} %spread.1), channel_id=1, replica_groups=mesh['x'=4,'z_hi'=4,'z_lo'=2,'y_lo'=2,'y_hi'=2,'core'=2] {'x','z_lo','y_..., dimensions={0} | all-to-all | bytes 1835008 | tf_op jit(solution)/shard_map/all_to_all | solution.py:404
  86.1 2.3 %collective-permute-start.3 = (s16[32,112,128]{2,1,0:T(8,128)(2,1)S(1)}, s16[32,112,128]{2,1,0:T(8,128)(2,1)S(1)}, u32[]{:S(2)}, u32[]{:S(2)}) collective-permute-start(s16[32,112,128]{2,1,0:T(8,128)(2,1)S(1)} %all_to_all.17.codes), channel_id=1, source_target_pairs={{0,1},{1,0},{2,3},{3,2},{4,5},{5,4},{6,7},{7,6},{8,9},{9,8},{10,11... | collective-permute-start | bytes 2752520 | tf_op jit(solution)/shard_map/ppermute | solution.py:73
  88.4 0.4 ours.1
  88.7 1.7 %collective-permute-done.3.codes = s16[32,112,128]{2,1,0:T(8,128)(2,1)S(1)} collective-permute-done((s16[32,112,128]{2,1,0:T(8,128)(2,1)S(1)}, s16[32,112,128]{2,1,0:T(8,128)(2,1)S(1)}, u32[]{:S(2)}, u32[]{:S(2)}) %collective-permute-start.3) | collective-permute-done | bytes 917536 | tf_op jit(solution)/shard_map/ppermute | solution.py:73
  90.5 0.0 copy-done
  90.5 0.0 copy-done.1
  90.5 2.9 %update.1 = (f32[400,2066]{1,0:T(8,128)}, f32[2066]{0:T(1024)}) custom-call(s32[1]{0:T(128)} %bitcast.core, f32[200,2176]{1,0:T(8,128)S(1)} %get-tuple-element.46.ours, f32[1,2176]{1,0:T(1,128)S(1)} %get-tuple-element.47.squares, s16[32,112,128]{2,1,0:T(8,128)(2,1)S(1)} %collective-permute-done.3.codes, f32[400,2066]{1,0:T(8,128)S(1)} %bitcast.17, ...), custom_call_target="tpu_custom_call" | custom-call | tf_op jit(solution)/shard_map/update/pallas_call | solution.py:55
Async XLA Ops:
  1.9 18.1 %collective-permute-start = (s32[8,1024]{1,0:T(8,128)S(1)}, s32[8,1024]{1,0:T(8,128)S(1)}, u32[]{:S(2)}, u32[]{:S(2)}) collective-permute-start(s32[8,1024]{1,0:T(8,128)S(1)} %get-tuple-element.31), channel_id=1, source_target_pairs={{4,0},{8,4},{12,8},{16,12},{20,16},{24,20},{28,24},{32,28},{36,32}... | collective-permute-start | bytes 98312 | tf_op jit(solution)/shard_map/ppermute | solution.py:69
  11.6 14.2 %collective-permute-start.1 = (bf16[400,512]{1,0:T(8,128)(2,1)S(1)}, bf16[400,512]{1,0:T(8,128)(2,1)S(1)}, u32[]{:S(2)}, u32[]{:S(2)}) collective-permute-start(bf16[400,512]{1,0:T(8,128)(2,1)S(1)} %get-tuple-element.27.left), channel_id=1, source_target_pairs={{4,0},{8,4},{12,8},{16,12},{20,16},{24,20},{28,24},{32,28},{36,32}... | collective-permute-start | bytes 1228808 | tf_op jit(solution)/shard_map/ppermute | solution.py:69
  19.1 0.9 copy-start.2
  20.0 1.1 %copy-start.3 = (bf16[400,1024]{1,0:T(8,128)(2,1)S(1)}, bf16[400,1024]{1,0:T(8,128)(2,1)}, u32[]{:S(2)}) copy-start(bf16[400,1024]{1,0:T(8,128)(2,1)} %copy-done.2) | copy-start | bytes 2457604
  29.8 5.3 %collective-permute-start.2 = (f32[200,2176]{1,0:T(8,128)S(1)}, f32[200,2176]{1,0:T(8,128)S(1)}, u32[]{:S(2)}, u32[]{:S(2)}) collective-permute-start(f32[200,2176]{1,0:T(8,128)S(1)} %get-tuple-element.45), channel_id=1, source_target_pairs={{0,1},{1,0},{2,3},{3,2},{4,5},{5,4},{6,7},{7,6},{8,9},{9,8},{10,11... | collective-permute-start | bytes 5222408 | tf_op jit(solution)/shard_map/ppermute | solution.py:73
  67.4 23.1 %copy-start = (f32[2066,400]{0,1:T(8,128)S(1)}, f32[2066,400]{0,1:T(8,128)}, u32[]{:S(2)}) copy-start(f32[2066,400]{0,1:T(8,128)} %param.12) | copy-start | bytes 9916804
  67.4 23.1 %copy-start.1 = (f32[2066]{0:T(1024)S(1)}, f32[2066]{0:T(1024)}, u32[]{:S(2)}) copy-start(f32[2066]{0:T(1024)} %state.1) | copy-start | bytes 24796
  86.1 4.4 %collective-permute-start.3 = (s16[32,112,128]{2,1,0:T(8,128)(2,1)S(1)}, s16[32,112,128]{2,1,0:T(8,128)(2,1)S(1)}, u32[]{:S(2)}, u32[]{:S(2)}) collective-permute-start(s16[32,112,128]{2,1,0:T(8,128)(2,1)S(1)} %all_to_all.17.codes), channel_id=1, source_target_pairs={{0,1},{1,0},{2,3},{3,2},{4,5},{5,4},{6,7},{7,6},{8,9},{9,8},{10,11... | collective-permute-start | bytes 2752520 | tf_op jit(solution)/shard_map/ppermute | solution.py:73

commit v8 on v7

--- a/solution.py
+++ b/solution.py
@@ -103,7 +103,7 @@
     d_prod = g_pos * pos_rows + dot(neg_rows, g_neg)
     p_re, p_im = d_prod[:HALF], d_prod[HALF:]
     d_rel = (p_re * h_re + p_im * h_im, p_im * h_re - p_re * h_im)
-    return prod, g_neg, d_pos, [part.astype(BF16) for part in d_rel]
+    return prod, g_neg, d_pos, d_rel
 
 
 def trained(slab, state, ids, prod, g_neg, d_pos):
@@ -136,7 +136,7 @@
 
 
 def first_kernel(
-    left, ids, slab_far, state_far, relation_far, slab_out, state_out, d_rel_out, table, slab, state, relation, sems
+    left, ids, slab_far, state_far, relation_far, slab_out, state_out, rel_grad, table, slab, state, relation, sems
 ):
     copies = [
         pltpu.make_async_copy(slab_far, slab, sems.at[0]),
@@ -158,16 +158,15 @@
     table[:, RMAIN:NREL] = relation[:, RMAIN:].astype(BF16)
     rel_rows = relation_rows_of(table[...], ids)
     prod, g_neg, d_pos, d_rel = edge_terms(heads, pos_rows, neg_rows, rel_rows)
-    d_rel_out[:HALF], d_rel_out[HALF:] = d_rel
     slab_out[...], state_out[...] = trained(slab[...], state[...], ids[...], prod, g_neg, d_pos)
-
-
-def between_kernel(slab, table, ids, ids_next, d_rel, pos_rows, neg_rows, rel_rows, rel_grad):
-    pos_rows[...], neg_rows[...] = target_rows_of(slab[...].astype(BF16), ids_next)
-    rel_rows[...] = relation_rows_of(table[...], ids_next)
-    whole = dot(d_rel[...], places(ids[2:3], RPAD), ((1,), (1,)))
+    whole = dot(jnp.concatenate(d_rel, 0).astype(BF16), places(ids[2:3], RPAD), ((1,), (1,)))
     for half in range(2):
         rel_grad[half] = whole[half * HALF : half * HALF + HALF]
+
+
+def between_kernel(slab, table, ids, pos_rows, neg_rows, rel_rows):
+    pos_rows[...], neg_rows[...] = target_rows_of(slab[...].astype(BF16), ids)
+    rel_rows[...] = relation_rows_of(table[...], ids)
 
 
 def rel_half(half, ids, d_rel, rel_grad):
@@ -182,7 +181,7 @@
         heads, pos_rows[...], neg_rows[...], rel_rows[...]
     )
     for half in range(2):
-        d_rel[half] = parts[half]
+        d_rel[half] = parts[half].astype(BF16)
     other[...] = rel_half(1 - core[0], ids, d_rel, rel_grad)
 
 
@@ -329,9 +328,14 @@
     slab_array, state_array = (D, ROWS), (1, ROWS)
     edge_array = kept((D, EPAD), BF16)
     half_array = kept((HALF, RPAD), F32)
-    slab, state, d_rel, table = call(
+    slab, state, rel_grad, table = call(
         first_kernel,
-        (kept(slab_array, F32), kept(state_array, F32), edge_array, kept((D, RPAD), BF16)),
+        (
+            kept(slab_array, F32),
+            kept(state_array, F32),
+            kept((2, HALF, RPAD), F32),
+            kept((D, RPAD), BF16),
+        ),
         left_low,
         ids,
         right_embed[0].T,
@@ -344,18 +348,16 @@
             pltpu.VMEM((D, NREL), F32),
             dma((6,)),
         ],
-        flops=1000,
+
         name="first",
     )
     wide_array = kept((D, EPAD), F32)
-    pos_rows, neg_rows, rel_rows, rel_grad = call(
+    pos_rows, neg_rows, rel_rows = call(
         between_kernel,
-        (wide_array, kept((D, NPAD), BF16), wide_array, kept((2, HALF, RPAD), F32)),
+        (wide_array, kept((D, NPAD), BF16), wide_array),
         slab,
         table,
-        ids,
         ids_next,
-        d_rel,
         flops=2 * 10**10,
         name="between",
     )

time: 93.8 us -> 92.1 us (0.982)
  local copies, waits for them, and re-layouts: 2.04 us -> 0.01 us
    unnamed x8 -> x4, local copies, waits for them, and re-layouts: 2.04 us -> 0.01 us
  transfers between devices with their start and end apart: 4 -> 4, of which waited for: 1 -> 1; matrix products, arithmetic and copies ran while one was open for 0% -> 0% of each run, Pallas kernels for 17% -> 18%
where the time goes in v8:
time: 92.1 us; the launch traced here: 91.9 us
  blocking collectives  50.3 us (55%)
  Pallas kernels  25.3 us (27%)
  starting transfers between devices  13.7 us (15%)
  waiting for transfers between devices  1.76 us (2%)
    pallas_call x10, Pallas kernels, call(): pl.pallas_call(kernel, out_shape=out_shape, in_specs=in_specs, out_specs=...  25.3 us
    all_to_all x1, blocking collectives, per_device(): got = lax.all_to_all(sent, CUBE, 0, 0, tiled=True)  20.6 us
    all_to_all x1, blocking collectives, per_device(): ours = lax.all_to_all(copies, CUBE, 0, 0, tiled=True)  18.5 us
    all_to_all x1, blocking collectives, per_device(): codes = lax.all_to_all(codes, 'z_hi', 0, 0, tiled=True)  11.1 us
    ppermute x2, starting transfers between devices, from_next(): lax.ppermute(block, BUCKET, [((i + 1) % count, i) for i in range(count)])  9.86 us
    ppermute x2, starting transfers between devices, swap_core(): return lax.ppermute(block, 'core', [(0, 1), (1, 0)])  3.79 us
  transfers between devices with their start and end apart: 4, of which 1 were waited for; matrix products, arithmetic and copies ran while one was open for 0% of the time, Pallas kernels for 18%

profile of v8, /device:TPU:1, one launch (start us, length us, event | category | flops | bytes accessed | tf_op | source)
XLA Modules:
  0.0 91.9 jit_solution(11774876672934258152)
XLA Ops:
  0.6 1.2 %prepare.1 = (s32[8,1024]{1,0:T(8,128)S(1)}, s32[8,1024]{1,0:T(8,128)S(1)}, bf16[400,512]{1,0:T(8,128)(2,1)S(1)}) custom-call(f32[400,512]{1,0:T(8,128)} %bitcast.18, s32[2,1000]{1,0:T(2,128)} %bitcast.20, s32[2,1000]{1,0:T(2,128)} %bitcast.21, s32[2,1000]{1,0:T(2,128)} %bitcast.22, s32[2,500]{1,0:T(2,128)} %bitcast.23), custom_call_target="tpu_custom_call" | custom-call | tf_op jit(solution)/shard_map/prepare/pallas_call | solution.py:55
  1.9 9.7 %collective-permute-start = (s32[8,1024]{1,0:T(8,128)S(1)}, s32[8,1024]{1,0:T(8,128)S(1)}, u32[]{:S(2)}, u32[]{:S(2)}) collective-permute-start(s32[8,1024]{1,0:T(8,128)S(1)} %get-tuple-element.30), channel_id=1, source_target_pairs={{4,0},{8,4},{12,8},{16,12},{20,16},{24,20},{28,24},{32,28},{36,32}... | collective-permute-start | bytes 98312 | tf_op jit(solution)/shard_map/ppermute | solution.py:69
  11.6 0.2 collective-permute-start.1
  11.7 9.3 %first.1 = (f32[400,512]{1,0:T(8,128)S(1)}, f32[1,512]{1,0:T(1,128)S(1)}, f32[2,200,2176]{2,1,0:T(8,128)S(1)}, bf16[400,2176]{1,0:T(8,128)(2,1)S(1)}) custom-call(bf16[400,512]{1,0:T(8,128)(2,1)S(1)} %get-tuple-element.26.left, s32[8,1024]{1,0:T(8,128)S(1)} %get-tuple-element.27.ids, f32[400,512]{1,0:T(8,128)} %bitcast.19, f32[1,512]{1,0:T(1,128)} %state_far.1, ...), custom_call_target="tpu_custom_call" | custom-call | tf_op jit(solution)/shard_map/first/pallas_call | solution.py:55
  21.1 0.0 collective-permute-done.ids
  21.1 2.7 %between.1 = (f32[400,1024]{1,0:T(8,128)S(1)}, bf16[400,512]{1,0:T(8,128)(2,1)S(1)}, f32[400,1024]{1,0:T(8,128)S(1)}) custom-call(f32[400,512]{1,0:T(8,128)S(1)} %get-tuple-element.28.slab, bf16[400,2176]{1,0:T(8,128)(2,1)S(1)} %get-tuple-element.32.table, s32[8,1024]{1,0:T(8,128)S(1)} %collective-permute-done.ids), custom_call_target="tpu_custom_call" | custom-call | flops 20000000000 | tf_op jit(solution)/shard_map/between/pallas_call | solution.py:55
  23.8 0.0 collective-permute-done.1.left
  23.8 4.0 %second.1 = (bf16[400,1024]{1,0:T(8,128)(2,1)S(1)}, bf16[512,1024]{1,0:T(8,128)(2,1)S(1)}, bf16[400,1024]{1,0:T(8,128)(2,1)S(1)}, bf16[2,200,1024]{2,1,0:T(8,128)(2,1)S(1)}, f32[200,2176]{1,0:T(8,128)S(1)}) custom-call(s32[1]{0:T(128)} %bitcast.core, bf16[400,512]{1,0:T(8,128)(2,1)S(1)} %collective-permute-done.1.left, ...), custom_call_target="tpu_custom_call" | custom-call | tf_op jit(solution)/shard_map/second/pallas_call | solution.py:55
  27.8 1.5 %collective-permute-start.2 = (f32[200,2176]{1,0:T(8,128)S(1)}, f32[200,2176]{1,0:T(8,128)S(1)}, u32[]{:S(2)}, u32[]{:S(2)}) collective-permute-start(f32[200,2176]{1,0:T(8,128)S(1)} %get-tuple-element.43), channel_id=1, source_target_pairs={{0,1},{1,0},{2,3},{3,2},{4,5},{5,4},{6,7},{7,6},{8,9},{9,8},{10,11... | collective-permute-start | bytes 5222408 | tf_op jit(solution)/shard_map/ppermute | solution.py:73
  29.3 3.8 %finish.1 = (f32[200,2176]{1,0:T(8,128)S(1)}, f32[400,512]{1,0:T(8,128)}, f32[1,512]{1,0:T(1,128)}) custom-call(s32[1]{0:T(128)} %bitcast.core, f32[400,512]{1,0:T(8,128)S(1)} %get-tuple-element.28.slab, f32[1,512]{1,0:T(1,128)S(1)} %get-tuple-element.29.state, s32[8,1024]{1,0:T(8,128)S(1)} %collective-permute-done.ids, ...), custom_call_target="tpu_custom_call" | custom-call | tf_op jit(solution)/shard_map/finish/pallas_call | solution.py:55
  33.1 0.0 collective-permute-done.2.theirs
  33.1 0.5 send.1
  33.6 20.6 %all_to_all.15.parts = s16[32,112,128]{2,1,0:T(8,128)(2,1)S(1)} all-to-all(s16[32,112,128]{2,1,0:T(8,128)(2,1)S(1)} %send.1), channel_id=1, replica_groups=mesh['x'=4,'z_hi'=4,'z_lo'=2,'y_lo'=2,'y_hi'=2,'core'=2] {'x','z_lo','y_..., dimensions={0} | all-to-all | bytes 1835008 | tf_op jit(solution)/shard_map/all_to_all | solution.py:401
  54.3 0.3 gather.1
  54.6 11.1 %all_to_all.16.parts = s16[4,112,128]{2,1,0:T(8,128)(2,1)S(1)} all-to-all(s16[4,112,128]{2,1,0:T(8,128)(2,1)S(1)} %gather.1), channel_id=1, replica_groups=mesh['x'=4,'z_hi'=4,'z_lo'=2,'y_lo'=2,'y_hi'=2,'core'=2] {'z_hi'}, dimensions={0} | all-to-all | bytes 229376 | tf_op jit(solution)/shard_map/all_to_all | solution.py:404
  65.7 0.0 copy-start
  65.7 0.0 copy-start.1
  65.7 0.2 spread.1
  66.0 18.5 %all_to_all.17.codes = s16[32,112,128]{2,1,0:T(8,128)(2,1)S(1)} all-to-all(s16[32,112,128]{2,1,0:T(8,128)(2,1)S(1)} %spread.1), channel_id=1, replica_groups=mesh['x'=4,'z_hi'=4,'z_lo'=2,'y_lo'=2,'y_hi'=2,'core'=2] {'x','z_lo','y_..., dimensions={0} | all-to-all | bytes 1835008 | tf_op jit(solution)/shard_map/all_to_all | solution.py:406
  84.4 2.3 %collective-permute-start.3 = (s16[32,112,128]{2,1,0:T(8,128)(2,1)S(1)}, s16[32,112,128]{2,1,0:T(8,128)(2,1)S(1)}, u32[]{:S(2)}, u32[]{:S(2)}) collective-permute-start(s16[32,112,128]{2,1,0:T(8,128)(2,1)S(1)} %all_to_all.17.codes), channel_id=1, source_target_pairs={{0,1},{1,0},{2,3},{3,2},{4,5},{5,4},{6,7},{7,6},{8,9},{9,8},{10,11... | collective-permute-start | bytes 2752520 | tf_op jit(solution)/shard_map/ppermute | solution.py:73
  86.7 0.4 ours.1
  87.1 1.7 %collective-permute-done.3.codes = s16[32,112,128]{2,1,0:T(8,128)(2,1)S(1)} collective-permute-done((s16[32,112,128]{2,1,0:T(8,128)(2,1)S(1)}, s16[32,112,128]{2,1,0:T(8,128)(2,1)S(1)}, u32[]{:S(2)}, u32[]{:S(2)}) %collective-permute-start.3) | collective-permute-done | bytes 917536 | tf_op jit(solution)/shard_map/ppermute | solution.py:73
  88.8 0.0 copy-done
  88.8 0.0 copy-done.1
  88.8 2.9 %update.1 = (f32[400,2066]{1,0:T(8,128)}, f32[2066]{0:T(1024)}) custom-call(s32[1]{0:T(128)} %bitcast.core, f32[200,2176]{1,0:T(8,128)S(1)} %get-tuple-element.44.ours, f32[1,2176]{1,0:T(1,128)S(1)} %get-tuple-element.45.squares, s16[32,112,128]{2,1,0:T(8,128)(2,1)S(1)} %collective-permute-done.3.codes, f32[400,2066]{1,0:T(8,128)S(1)} %bitcast.17, ...), custom_call_target="tpu_custom_call" | custom-call | tf_op jit(solution)/shard_map/update/pallas_call | solution.py:55
Async XLA Ops:
  1.9 19.2 %collective-permute-start = (s32[8,1024]{1,0:T(8,128)S(1)}, s32[8,1024]{1,0:T(8,128)S(1)}, u32[]{:S(2)}, u32[]{:S(2)}) collective-permute-start(s32[8,1024]{1,0:T(8,128)S(1)} %get-tuple-element.30), channel_id=1, source_target_pairs={{4,0},{8,4},{12,8},{16,12},{20,16},{24,20},{28,24},{32,28},{36,32}... | collective-permute-start | bytes 98312 | tf_op jit(solution)/shard_map/ppermute | solution.py:69
  11.6 12.3 %collective-permute-start.1 = (bf16[400,512]{1,0:T(8,128)(2,1)S(1)}, bf16[400,512]{1,0:T(8,128)(2,1)S(1)}, u32[]{:S(2)}, u32[]{:S(2)}) collective-permute-start(bf16[400,512]{1,0:T(8,128)(2,1)S(1)} %get-tuple-element.26.left), channel_id=1, source_target_pairs={{4,0},{8,4},{12,8},{16,12},{20,16},{24,20},{28,24},{32,28},{36,32}... | collective-permute-start | bytes 1228808 | tf_op jit(solution)/shard_map/ppermute | solution.py:69
  27.8 5.3 %collective-permute-start.2 = (f32[200,2176]{1,0:T(8,128)S(1)}, f32[200,2176]{1,0:T(8,128)S(1)}, u32[]{:S(2)}, u32[]{:S(2)}) collective-permute-start(f32[200,2176]{1,0:T(8,128)S(1)} %get-tuple-element.43), channel_id=1, source_target_pairs={{0,1},{1,0},{2,3},{3,2},{4,5},{5,4},{6,7},{7,6},{8,9},{9,8},{10,11... | collective-permute-start | bytes 5222408 | tf_op jit(solution)/shard_map/ppermute | solution.py:73
  65.7 23.1 %copy-start = (f32[2066,400]{0,1:T(8,128)S(1)}, f32[2066,400]{0,1:T(8,128)}, u32[]{:S(2)}) copy-start(f32[2066,400]{0,1:T(8,128)} %param.12) | copy-start | bytes 9916804
  65.7 23.1 %copy-start.1 = (f32[2066]{0:T(1024)S(1)}, f32[2066]{0:T(1024)}, u32[]{:S(2)}) copy-start(f32[2066]{0:T(1024)} %state.1) | copy-start | bytes 24796
  84.4 4.4 %collective-permute-start.3 = (s16[32,112,128]{2,1,0:T(8,128)(2,1)S(1)}, s16[32,112,128]{2,1,0:T(8,128)(2,1)S(1)}, u32[]{:S(2)}, u32[]{:S(2)}) collective-permute-start(s16[32,112,128]{2,1,0:T(8,128)(2,1)S(1)} %all_to_all.17.codes), channel_id=1, source_target_pairs={{0,1},{1,0},{2,3},{3,2},{4,5},{5,4},{6,7},{7,6},{8,9},{9,8},{10,11... | collective-permute-start | bytes 2752520 | tf_op jit(solution)/shard_map/ppermute | solution.py:73

commit v9 on v8

--- a/solution.py
+++ b/solution.py
@@ -174,7 +174,7 @@
 
 
 def second_kernel(
-    core, left, ids, pos_rows, neg_rows, rel_rows, rel_grad, prod, g_neg, d_pos, d_rel, other
+    core, left, ids, pos_rows, neg_rows, rel_rows, rel_grad, prod, g_neg, d_pos, d_rel, other, grads, last
 ):
     heads = dot(left[...], places(ids[0:1], ROWS))
     prod[...], g_neg[...], d_pos[...], parts = edge_terms(
@@ -182,16 +182,22 @@
     )
     for half in range(2):
         d_rel[half] = parts[half].astype(BF16)
-    other[...] = rel_half(1 - core[0], ids, d_rel, rel_grad)
-
-
-def finish_kernel(
-    core, slab, state, ids, rel_grad, prod, g_neg, d_pos, d_rel, mine, slab_out, state_out
-):
+    grads[...] = rel_half(1 - core[0], ids, d_rel, rel_grad)
+    last[HALF:] = jnp.zeros((last.shape[0] - HALF, 128), F32)
+    last[:HALF] = grads[:, RMAIN:]
+    for part in range(OWNERS):
+        other[part] = encode(grads[place_of(part)], last[7 * part : 7 * part + 8])
+
+
+def own_half_kernel(core, ids, rel_grad, d_rel, mine):
     mine[...] = rel_half(core[0], ids, d_rel, rel_grad)
+
+
+def target_kernel(after, slab, state, ids, prod, g_neg, d_pos, slab_out, state_out, done):
     slab_out[...], state_out[...] = trained(
         slab[...], state[...], ids[...], prod[...], g_neg[...], d_pos[...]
     )
+    done[...] = after[:, :128]
 
 
 def power_of(block):
@@ -232,10 +238,12 @@
 
 def send_kernel(mine, theirs, codes, last):
     last[HALF:] = jnp.zeros((last.shape[0] - HALF, 128), F32)
-    last[:HALF] = mine[:, RMAIN:] + theirs[:, RMAIN:]
+    last[:HALF] = mine[:, RMAIN:]
     for part in range(OWNERS):
-        at = place_of(part)
-        codes[part] = encode(mine[at] + theirs[at], last[7 * part : 7 * part + 8])
+        rows, lanes = place_of(part)
+        main, tail = decode(theirs[part])
+        main = mine[rows, lanes] + main[: rows.stop - rows.start]
+        codes[part] = encode(main, last[7 * part : 7 * part + 8] + tail)
 
 
 def gather_kernel(parts, codes):
@@ -273,7 +281,7 @@
 
 
 def update_kernel(
-    core, ours, squares, codes, relation, state, relation_out, state_out, theirs, last, wide, sems
+    core, ours, squares, codes, relation, state, done, relation_out, state_out, theirs, last, wide, sems
 ):
     total = squares[...] + decoded_into(codes, theirs, last)
     new_state = state[...].reshape(1, NREL) + total[:, :NREL] * (1.0 / D)
@@ -352,6 +360,9 @@
         name="first",
     )
     wide_array = kept((D, EPAD), F32)
+    part = (PART, 128)
+    last = pltpu.VMEM((232, 128), F32)
+    parts = kept((OWNERS, *part), jnp.int16)
     pos_rows, neg_rows, rel_rows = call(
         between_kernel,
         (wide_array, kept((D, NPAD), BF16), wide_array),
@@ -368,7 +379,7 @@
             kept((NPAD, EPAD), BF16),
             edge_array,
             kept((2, HALF, EPAD), BF16),
-            half_array,
+            parts,
         ),
         left_next,
         ids_next,
@@ -377,26 +388,13 @@
         rel_rows,
         rel_grad,
         core=core,
+        scratch=[pltpu.VMEM((HALF, RPAD), F32), last],
         name="second",
     )
     theirs = swap_core(other)
-    mine, slab_out, state_out = call(
-        finish_kernel,
-        (half_array, struct(slab_array, F32), struct(state_array, F32)),
-        slab,
-        state,
-        ids_next,
-        rel_grad,
-        prod,
-        g_neg,
-        d_pos,
-        d_rel,
-        core=core,
-        name="finish",
-    )
-    part = (PART, 128)
-    last = pltpu.VMEM((232, 128), F32)
-    parts = kept((OWNERS, *part), jnp.int16)
+    mine = call(
+        own_half_kernel, half_array, ids_next, rel_grad, d_rel, core=core, name="own_half"
+    )
     sent = call(send_kernel, parts, mine, theirs, scratch=[last], name="send")
     got = lax.all_to_all(sent, CUBE, 0, 0, tiled=True)
     count = lax.axis_size("z_hi")
@@ -408,6 +406,18 @@
     grads, squares = call(
         ours_kernel, (half_array, kept((1, RPAD), F32)), ours, scratch=[last], name="ours"
     )
+    slab_out, state_out, done = call(
+        target_kernel,
+        (struct(slab_array, F32), struct(state_array, F32), kept((1, 128), F32)),
+        squares,
+        slab,
+        state,
+        ids_next,
+        prod,
+        g_neg,
+        d_pos,
+        name="target",
+    )
     relation_out, relation_state_out = call(
         update_kernel,
         (struct((D, NREL), F32), struct((NREL,), F32)),
@@ -416,6 +426,7 @@
         theirs,
         relation,
         relation_state,
+        done,
         core=core,
         far_out=(0,),
         scratch=[

time: 92.1 us -> 90.8 us (0.986)
  waiting for transfers between devices: 1.76 us -> 0.53 us
    ppermute x2, waiting for transfers between devices: 1.75 us -> 0.52 us  [swap_core(): return lax.ppermute(block, 'core', [(0, 1), (1, 0)])]
    pallas_call x10 -> x11, Pallas kernels: 25.3 us -> 25.9 us  [call(): pl.pallas_call(kernel, out_shape=out_shape, in_specs=in_specs, out_specs=...]
where the time goes in v9:
time: 90.8 us; the launch traced here: 90.6 us
  blocking collectives  49.6 us (55%)
  Pallas kernels  25.9 us (29%)
  starting transfers between devices  13.7 us (15%)
    pallas_call x11, Pallas kernels, call(): pl.pallas_call(kernel, out_shape=out_shape, in_specs=in_specs, out_specs=...  25.9 us
    all_to_all x1, blocking collectives, per_device(): got = lax.all_to_all(sent, CUBE, 0, 0, tiled=True)  20.3 us
    all_to_all x1, blocking collectives, per_device(): ours = lax.all_to_all(copies, CUBE, 0, 0, tiled=True)  18.1 us
    all_to_all x1, blocking collectives, per_device(): codes = lax.all_to_all(codes, 'z_hi', 0, 0, tiled=True)  11.3 us
    ppermute x2, starting transfers between devices, from_next(): lax.ppermute(block, BUCKET, [((i + 1) % count, i) for i in range(count)])  9.86 us
    ppermute x2, starting transfers between devices, swap_core(): return lax.ppermute(block, 'core', [(0, 1), (1, 0)])  3.82 us
  transfers between devices with their start and end apart: 4, of which 1 were waited for; matrix products, arithmetic and copies ran while one was open for 0% of the time, Pallas kernels for 18%

profile of v9, /device:TPU:1, one launch (start us, length us, event | category | flops | bytes accessed | tf_op | source)
XLA Modules:
  0.0 90.6 jit_solution(4302812007259008668)
XLA Ops:
  0.6 1.2 %prepare.1 = (s32[8,1024]{1,0:T(8,128)S(1)}, s32[8,1024]{1,0:T(8,128)S(1)}, bf16[400,512]{1,0:T(8,128)(2,1)S(1)}) custom-call(f32[400,512]{1,0:T(8,128)} %bitcast.18, s32[2,1000]{1,0:T(2,128)} %bitcast.20, s32[2,1000]{1,0:T(2,128)} %bitcast.21, s32[2,1000]{1,0:T(2,128)} %bitcast.22, s32[2,500]{1,0:T(2,128)} %bitcast.23), custom_call_target="tpu_custom_call" | custom-call | tf_op jit(solution)/shard_map/prepare/pallas_call | solution.py:55
  1.9 9.7 %collective-permute-start = (s32[8,1024]{1,0:T(8,128)S(1)}, s32[8,1024]{1,0:T(8,128)S(1)}, u32[]{:S(2)}, u32[]{:S(2)}) collective-permute-start(s32[8,1024]{1,0:T(8,128)S(1)} %get-tuple-element.26), channel_id=1, source_target_pairs={{4,0},{8,4},{12,8},{16,12},{20,16},{24,20},{28,24},{32,28},{36,32}... | collective-permute-start | bytes 98312 | tf_op jit(solution)/shard_map/ppermute | solution.py:69
  11.6 0.2 collective-permute-start.1
  11.7 9.3 %first.1 = (f32[400,512]{1,0:T(8,128)S(1)}, f32[1,512]{1,0:T(1,128)S(1)}, f32[2,200,2176]{2,1,0:T(8,128)S(1)}, bf16[400,2176]{1,0:T(8,128)(2,1)S(1)}) custom-call(bf16[400,512]{1,0:T(8,128)(2,1)S(1)} %get-tuple-element.27.left, s32[8,1024]{1,0:T(8,128)S(1)} %get-tuple-element.28.ids, f32[400,512]{1,0:T(8,128)} %bitcast.19, f32[1,512]{1,0:T(1,128)} %state_far.1, ...), custom_call_target="tpu_custom_call" | custom-call | tf_op jit(solution)/shard_map/first/pallas_call | solution.py:55
  21.1 0.0 collective-permute-done.ids
  21.1 2.7 %between.1 = (f32[400,1024]{1,0:T(8,128)S(1)}, bf16[400,512]{1,0:T(8,128)(2,1)S(1)}, f32[400,1024]{1,0:T(8,128)S(1)}) custom-call(f32[400,512]{1,0:T(8,128)S(1)} %get-tuple-element.30.slab, bf16[400,2176]{1,0:T(8,128)(2,1)S(1)} %get-tuple-element.31.table, s32[8,1024]{1,0:T(8,128)S(1)} %collective-permute-done.ids), custom_call_target="tpu_custom_call" | custom-call | flops 20000000000 | tf_op jit(solution)/shard_map/between/pallas_call | solution.py:55
  23.8 0.0 collective-permute-done.1.left
  23.8 4.2 %second.1 = (bf16[400,1024]{1,0:T(8,128)(2,1)S(1)}, bf16[512,1024]{1,0:T(8,128)(2,1)S(1)}, bf16[400,1024]{1,0:T(8,128)(2,1)S(1)}, bf16[2,200,1024]{2,1,0:T(8,128)(2,1)S(1)}, s16[32,112,128]{2,1,0:T(8,128)(2,1)S(1)}) custom-call(s32[1]{0:T(128)} %bitcast.core, bf16[400,512]{1,0:T(8,128)(2,1)S(1)} %collective-permute-done.1.left, ...), custom_call_target="tpu_custom_call" | custom-call | tf_op jit(solution)/shard_map/second/pallas_call | solution.py:55
  28.0 1.5 %collective-permute-start.2 = (s16[32,112,128]{2,1,0:T(8,128)(2,1)S(1)}, s16[32,112,128]{2,1,0:T(8,128)(2,1)S(1)}, u32[]{:S(2)}, u32[]{:S(2)}) collective-permute-start(s16[32,112,128]{2,1,0:T(8,128)(2,1)S(1)} %get-tuple-element.36), channel_id=1, source_target_pairs={{0,1},{1,0},{2,3},{3,2},{4,5},{5,4},{6,7},{7,6},{8,9},{9,8},{10,11... | collective-permute-start | bytes 2752520 | tf_op jit(solution)/shard_map/ppermute | solution.py:73
  29.5 1.6 %own_half.1.mine = f32[200,2176]{1,0:T(8,128)S(1)} custom-call(s32[1]{0:T(128)} %bitcast.core, s32[8,1024]{1,0:T(8,128)S(1)} %collective-permute-done.ids, f32[2,200,2176]{2,1,0:T(8,128)S(1)} %get-tuple-element.29.rel_grad, bf16[2,200,1024]{2,1,0:T(8,128)(2,1)S(1)} %get-tuple-element.35.d_rel), custom_call_target="tpu_custom_call" | custom-call | tf_op jit(solution)/shard_map/own_half/pallas_call | solution.py:55
  31.1 0.5 collective-permute-done.2.theirs
  31.6 0.7 send.1
  32.3 20.3 %all_to_all.15.parts = s16[32,112,128]{2,1,0:T(8,128)(2,1)S(1)} all-to-all(s16[32,112,128]{2,1,0:T(8,128)(2,1)S(1)} %send.1), channel_id=1, replica_groups=mesh['x'=4,'z_hi'=4,'z_lo'=2,'y_lo'=2,'y_hi'=2,'core'=2] {'x','z_lo','y_..., dimensions={0} | all-to-all | bytes 1835008 | tf_op jit(solution)/shard_map/all_to_all | solution.py:399
  52.5 0.3 gather.1
  52.9 11.3 %all_to_all.16.parts = s16[4,112,128]{2,1,0:T(8,128)(2,1)S(1)} all-to-all(s16[4,112,128]{2,1,0:T(8,128)(2,1)S(1)} %gather.1), channel_id=1, replica_groups=mesh['x'=4,'z_hi'=4,'z_lo'=2,'y_lo'=2,'y_hi'=2,'core'=2] {'z_hi'}, dimensions={0} | all-to-all | bytes 229376 | tf_op jit(solution)/shard_map/all_to_all | solution.py:402
  64.2 0.2 spread.1
  64.4 18.1 %all_to_all.17.codes = s16[32,112,128]{2,1,0:T(8,128)(2,1)S(1)} all-to-all(s16[32,112,128]{2,1,0:T(8,128)(2,1)S(1)} %spread.1), channel_id=1, replica_groups=mesh['x'=4,'z_hi'=4,'z_lo'=2,'y_lo'=2,'y_hi'=2,'core'=2] {'x','z_lo','y_..., dimensions={0} | all-to-all | bytes 1835008 | tf_op jit(solution)/shard_map/all_to_all | solution.py:404
  82.5 2.3 %collective-permute-start.3 = (s16[32,112,128]{2,1,0:T(8,128)(2,1)S(1)}, s16[32,112,128]{2,1,0:T(8,128)(2,1)S(1)}, u32[]{:S(2)}, u32[]{:S(2)}) collective-permute-start(s16[32,112,128]{2,1,0:T(8,128)(2,1)S(1)} %all_to_all.17.codes), channel_id=1, source_target_pairs={{0,1},{1,0},{2,3},{3,2},{4,5},{5,4},{6,7},{7,6},{8,9},{9,8},{10,11... | collective-permute-start | bytes 2752520 | tf_op jit(solution)/shard_map/ppermute | solution.py:73
  84.8 0.4 ours.1
  85.2 0.0 copy-start
  85.2 0.0 copy-start.1
  85.2 2.4 %target.1 = (f32[400,512]{1,0:T(8,128)}, f32[1,512]{1,0:T(1,128)}, f32[1,128]{1,0:T(1,128)S(1)}) custom-call(f32[1,2176]{1,0:T(1,128)S(1)} %get-tuple-element.37.after.squares, f32[400,512]{1,0:T(8,128)S(1)} %get-tuple-element.30.slab, f32[1,512]{1,0:T(1,128)S(1)} %get-tuple-element.38.state, s32[8,1024]{1,0:T(8,128)S(1)} %collective-permute-done.ids, ...), custom_call_target="tpu_custom_call" | custom-call | tf_op jit(solution)/shard_map/target/pallas_call | solution.py:55
  87.5 0.0 collective-permute-done.3.codes
  87.5 0.0 copy-done
  87.5 0.0 copy-done.1
  87.5 2.9 %update.1 = (f32[400,2066]{1,0:T(8,128)}, f32[2066]{0:T(1024)}) custom-call(s32[1]{0:T(128)} %bitcast.core, f32[200,2176]{1,0:T(8,128)S(1)} %get-tuple-element.44.ours, f32[1,2176]{1,0:T(1,128)S(1)} %get-tuple-element.37.after.squares, s16[32,112,128]{2,1,0:T(8,128)(2,1)S(1)} %collective-permute-done.3.codes, f32[400,2066]{1,0:T(8,128)S(1)} %bitcast.17, ...), custom_call_target="tpu_custom_call" | custom-call | tf_op jit(solution)/shard_map/update/pallas_call | solution.py:55
Async XLA Ops:
  1.9 19.2 %collective-permute-start = (s32[8,1024]{1,0:T(8,128)S(1)}, s32[8,1024]{1,0:T(8,128)S(1)}, u32[]{:S(2)}, u32[]{:S(2)}) collective-permute-start(s32[8,1024]{1,0:T(8,128)S(1)} %get-tuple-element.26), channel_id=1, source_target_pairs={{4,0},{8,4},{12,8},{16,12},{20,16},{24,20},{28,24},{32,28},{36,32}... | collective-permute-start | bytes 98312 | tf_op jit(solution)/shard_map/ppermute | solution.py:69
  11.6 12.3 %collective-permute-start.1 = (bf16[400,512]{1,0:T(8,128)(2,1)S(1)}, bf16[400,512]{1,0:T(8,128)(2,1)S(1)}, u32[]{:S(2)}, u32[]{:S(2)}) collective-permute-start(bf16[400,512]{1,0:T(8,128)(2,1)S(1)} %get-tuple-element.27.left), channel_id=1, source_target_pairs={{4,0},{8,4},{12,8},{16,12},{20,16},{24,20},{28,24},{32,28},{36,32}... | collective-permute-start | bytes 1228808 | tf_op jit(solution)/shard_map/ppermute | solution.py:69
  28.0 3.6 %collective-permute-start.2 = (s16[32,112,128]{2,1,0:T(8,128)(2,1)S(1)}, s16[32,112,128]{2,1,0:T(8,128)(2,1)S(1)}, u32[]{:S(2)}, u32[]{:S(2)}) collective-permute-start(s16[32,112,128]{2,1,0:T(8,128)(2,1)S(1)} %get-tuple-element.36), channel_id=1, source_target_pairs={{0,1},{1,0},{2,3},{3,2},{4,5},{5,4},{6,7},{7,6},{8,9},{9,8},{10,11... | collective-permute-start | bytes 2752520 | tf_op jit(solution)/shard_map/ppermute | solution.py:73
  82.5 5.1 %collective-permute-start.3 = (s16[32,112,128]{2,1,0:T(8,128)(2,1)S(1)}, s16[32,112,128]{2,1,0:T(8,128)(2,1)S(1)}, u32[]{:S(2)}, u32[]{:S(2)}) collective-permute-start(s16[32,112,128]{2,1,0:T(8,128)(2,1)S(1)} %all_to_all.17.codes), channel_id=1, source_target_pairs={{0,1},{1,0},{2,3},{3,2},{4,5},{5,4},{6,7},{7,6},{8,9},{9,8},{10,11... | collective-permute-start | bytes 2752520 | tf_op jit(solution)/shard_map/ppermute | solution.py:73
  85.2 2.4 %copy-start = (f32[2066,400]{0,1:T(8,128)S(1)}, f32[2066,400]{0,1:T(8,128)}, u32[]{:S(2)}) copy-start(f32[2066,400]{0,1:T(8,128)} %param.12) | copy-start | bytes 9916804
  85.2 2.4 %copy-start.1 = (f32[2066]{0:T(1024)S(1)}, f32[2066]{0:T(1024)}, u32[]{:S(2)}) copy-start(f32[2066]{0:T(1024)} %state.1) | copy-start | bytes 24796

commit v10 on v9

--- a/solution.py
+++ b/solution.py
@@ -19,8 +19,9 @@
 NREL = 2066
 RMAIN = 2048
 RPAD = 2176
-CUT = 104
-PART = 112
+CUT = 100
+PART = 104
+EXTRA = NREL - RMAIN
 LEVELS = 32000.0
 F32 = jnp.float32
 BF16 = jnp.bfloat16
@@ -174,7 +175,7 @@
 
 
 def second_kernel(
-    core, left, ids, pos_rows, neg_rows, rel_rows, rel_grad, prod, g_neg, d_pos, d_rel, other, grads, last
+    core, left, ids, pos_rows, neg_rows, rel_rows, rel_grad, prod, g_neg, d_pos, d_rel, other, grads
 ):
     heads = dot(left[...], places(ids[0:1], ROWS))
     prod[...], g_neg[...], d_pos[...], parts = edge_terms(
@@ -183,10 +184,9 @@
     for half in range(2):
         d_rel[half] = parts[half].astype(BF16)
     grads[...] = rel_half(1 - core[0], ids, d_rel, rel_grad)
-    last[HALF:] = jnp.zeros((last.shape[0] - HALF, 128), F32)
-    last[:HALF] = grads[:, RMAIN:]
+    firsts, seconds = last_relations(grads)
     for part in range(OWNERS):
-        other[part] = encode(grads[place_of(part)], last[7 * part : 7 * part + 8])
+        other[part] = encode(block_of(grads, part), *picked(firsts, seconds, part))
 
 
 def own_half_kernel(core, ids, rel_grad, d_rel, mine):
@@ -200,79 +200,93 @@
     done[...] = after[:, :128]
 
 
-def power_of(block):
-    top = jnp.max(jnp.abs(block), axis=0, keepdims=True)
+def power_of(top):
     return jnp.ceil(jnp.log2(jnp.maximum(top, 1e-30)))
 
 
-def encode(main, last):
-    lane = lax.broadcasted_iota(jnp.int32, last.shape, 1)
-    row = lax.broadcasted_iota(jnp.int32, last.shape, 0)
-    last = jnp.where(row < 7, last, 0.0)
-    main_power, last_power = power_of(main), power_of(last)
-    main = jnp.round(main * (LEVELS * jnp.exp2(-main_power)))
-    last = jnp.round(last * (LEVELS * jnp.exp2(-last_power)))
-    last_power = pltpu.roll(jnp.broadcast_to(last_power, last.shape), 64, 1)
-    last = jnp.where(lane < 64, last, last_power)
-    last = jnp.where(row == 7, jnp.broadcast_to(main_power, last.shape), last)
-    fill = [jnp.zeros((CUT - main.shape[0], 128), F32)] if main.shape[0] < CUT else []
-    return jnp.concatenate([main, *fill, last], 0).astype(jnp.int32).astype(jnp.int16)
+def iota(shape, axis):
+    return lax.broadcasted_iota(jnp.int32, shape, axis)
+
+
+def encode(main, first, second):
+    row = iota(main.shape, 0)
+    main = jnp.where(row < CUT, main, 0.0)
+    power = power_of(jnp.max(jnp.abs(main), axis=0, keepdims=True))
+    top = jnp.maximum(jnp.abs(first), jnp.abs(second))
+    last_power = power_of(jnp.max(top, axis=1, keepdims=True))
+    scale = LEVELS * jnp.exp2(-last_power)
+    second = jnp.where(iota(second.shape, 1) == 127, last_power, jnp.round(second * scale))
+    codes = jnp.round(main * (LEVELS * jnp.exp2(-power)))
+    codes = jnp.where(row == CUT, jnp.round(first * scale), codes)
+    codes = jnp.where(row == CUT + 1, second, codes)
+    codes = jnp.where(row == CUT + 2, power, codes)
+    return codes.astype(jnp.int32).astype(jnp.int16)
 
 
 def decode(codes):
     wide = codes.astype(jnp.int32).astype(F32)
-    main, last = wide[:CUT], wide[CUT:]
-    lane = lax.broadcasted_iota(jnp.int32, last.shape, 1)
-    row = lax.broadcasted_iota(jnp.int32, last.shape, 0)
-    main = main * (jnp.exp2(last[7:8]) * (1.0 / LEVELS))
-    last_step = jnp.exp2(pltpu.roll(last, 64, 1)) * (1.0 / LEVELS)
-    valid = jnp.logical_and(lane < NREL - RMAIN, row < 7)
-    return main, jnp.where(valid, last * last_step, 0.0)
-
-
-def place_of(part):
+    first, second, power = (wide[CUT + i : CUT + i + 1] for i in range(3))
+    step = jnp.exp2(second[:, 127:]) * (1.0 / LEVELS)
+    second = jnp.where(iota(second.shape, 1) < HALF - 128, second * step, 0.0)
+    main = jnp.where(iota(wide.shape, 0) < CUT, wide, 0.0)
+    return main * (jnp.exp2(power) * (1.0 / LEVELS)), first * step, second
+
+
+def block_of(grads, part):
     tile, low = divmod(part, 2)
-    rows = slice(CUT, HALF) if low else slice(0, CUT)
-    return rows, slice(128 * tile, 128 * tile + 128)
-
-
-def send_kernel(mine, theirs, codes, last):
-    last[HALF:] = jnp.zeros((last.shape[0] - HALF, 128), F32)
-    last[:HALF] = mine[:, RMAIN:]
+    lanes = slice(128 * tile, 128 * tile + 128)
+    return pltpu.roll(grads[HALF - PART :, lanes], CUT, 0) if low else grads[:PART, lanes]
+
+
+def last_relations(grads):
+    gap = jnp.zeros((256 - HALF, 128), F32)
+    rows = jnp.transpose(jnp.concatenate([grads[:, RMAIN:], gap], 0))
+    return rows[:, :128], rows[:, 128:]
+
+
+def picked(firsts, seconds, part):
+    if part >= EXTRA:
+        return jnp.zeros((1, 128), F32), jnp.zeros((1, 128), F32)
+    return firsts[part : part + 1], seconds[part : part + 1]
+
+
+def send_kernel(mine, theirs, codes):
+    firsts, seconds = last_relations(mine)
     for part in range(OWNERS):
-        rows, lanes = place_of(part)
-        main, tail = decode(theirs[part])
-        main = mine[rows, lanes] + main[: rows.stop - rows.start]
-        codes[part] = encode(main, last[7 * part : 7 * part + 8] + tail)
+        main, first, second = decode(theirs[part])
+        own_first, own_second = picked(firsts, seconds, part)
+        codes[part] = encode(block_of(mine, part) + main, own_first + first, own_second + second)
+
+
+def summed(parts):
+    total = decode(parts[0])
+    for part in range(1, parts.shape[0]):
+        total = tuple(old + new for old, new in zip(total, decode(parts[part])))
+    return total
 
 
 def gather_kernel(parts, codes):
-    main, last = decode(parts[0])
-    for part in range(1, OWNERS):
-        more = decode(parts[part])
-        main, last = main + more[0], last + more[1]
-    code = encode(main, last)
+    code = encode(*summed(parts))
     for copy in range(codes.shape[0]):
         codes[copy] = code
 
 
-def spread_kernel(parts, copies):
-    main, last = decode(parts[0])
-    for part in range(1, parts.shape[0]):
-        more = decode(parts[part])
-        main, last = main + more[0], last + more[1]
-    code = encode(main, last)
-    for copy in range(OWNERS):
-        copies[copy] = code
-
-
 def decoded_into(codes, grads, last):
-    for part in range(OWNERS):
-        rows, lanes = place_of(part)
-        main, tail = decode(codes[part])
-        grads[rows, lanes] = main[: rows.stop - rows.start]
-        last[7 * part : 7 * part + 8] = tail
-    grads[:, RMAIN:] = last[:HALF]
+    last[...] = jnp.zeros(last.shape, F32)
+    for tile in range(OWNERS // 2):
+        lanes = slice(128 * tile, 128 * tile + 128)
+        blocks = []
+        for part in (2 * tile, 2 * tile + 1):
+            block, first, second = decode(codes[part])
+            blocks.append(block)
+            if part < EXTRA:
+                last[part : part + 1, :128] = first
+                last[part : part + 1, 128:] = second
+        upper, lower = blocks[0], pltpu.roll(blocks[1], PART - CUT, 0)
+        grads[: HALF - PART, lanes] = upper[: HALF - PART]
+        grads[HALF - PART : PART, lanes] = upper[HALF - PART :] + lower[: 2 * PART - HALF]
+        grads[PART:, lanes] = lower[2 * PART - HALF :]
+    grads[:, RMAIN:] = jnp.transpose(last[...])[:HALF]
     return jnp.sum(grads[...] * grads[...], 0, keepdims=True)
 
 
@@ -361,7 +375,7 @@
     )
     wide_array = kept((D, EPAD), F32)
     part = (PART, 128)
-    last = pltpu.VMEM((232, 128), F32)
+    last = pltpu.VMEM((128, 256), F32)
     parts = kept((OWNERS, *part), jnp.int16)
     pos_rows, neg_rows, rel_rows = call(
         between_kernel,
@@ -388,19 +402,19 @@
         rel_rows,
         rel_grad,
         core=core,
-        scratch=[pltpu.VMEM((HALF, RPAD), F32), last],
+        scratch=[pltpu.VMEM((HALF, RPAD), F32)],
         name="second",
     )
     theirs = swap_core(other)
     mine = call(
         own_half_kernel, half_array, ids_next, rel_grad, d_rel, core=core, name="own_half"
     )
-    sent = call(send_kernel, parts, mine, theirs, scratch=[last], name="send")
+    sent = call(send_kernel, parts, mine, theirs, name="send")
     got = lax.all_to_all(sent, CUBE, 0, 0, tiled=True)
     count = lax.axis_size("z_hi")
     codes = call(gather_kernel, kept((count, *part), jnp.int16), got, name="gather")
     codes = lax.all_to_all(codes, "z_hi", 0, 0, tiled=True)
-    copies = call(spread_kernel, parts, codes, name="spread")
+    copies = call(gather_kernel, parts, codes, name="spread")
     ours = lax.all_to_all(copies, CUBE, 0, 0, tiled=True)
     theirs = swap_core(ours)
     grads, squares = call(

time: 90.8 us -> 89.6 us (0.987)
  blocking collectives: 49.6 us -> 45.8 us
  starting transfers between devices: 13.7 us -> 15.9 us
    all_to_all x1, blocking collectives: 18.1 us -> 15.2 us  [per_device(): ours = lax.all_to_all(copies, CUBE, 0, 0, tiled=True)]
    ppermute x2, starting transfers between devices: 3.82 us -> 6.02 us  [swap_core(): return lax.ppermute(block, 'core', [(0, 1), (1, 0)])]
where the time goes in v10:
time: 89.6 us; the launch traced here: 89.4 us
  blocking collectives  45.8 us (51%)
  Pallas kernels  26.4 us (29%)
  starting transfers between devices  15.9 us (18%)
  between operations  0.9 us (1%)
    pallas_call x11, Pallas kernels, call(): pl.pallas_call(kernel, out_shape=out_shape, in_specs=in_specs, out_specs=...  26.4 us
    all_to_all x1, blocking collectives, per_device(): got = lax.all_to_all(sent, CUBE, 0, 0, tiled=True)  19.5 us
    all_to_all x1, blocking collectives, per_device(): ours = lax.all_to_all(copies, CUBE, 0, 0, tiled=True)  15.2 us
    all_to_all x1, blocking collectives, per_device(): codes = lax.all_to_all(codes, 'z_hi', 0, 0, tiled=True)  11 us
    ppermute x2, starting transfers between devices, from_next(): lax.ppermute(block, BUCKET, [((i + 1) % count, i) for i in range(count)])  9.86 us
    ppermute x2, starting transfers between devices, swap_core(): return lax.ppermute(block, 'core', [(0, 1), (1, 0)])  6.02 us
  transfers between devices with their start and end apart: 4, of which 1 were waited for; matrix products, arithmetic and copies ran while one was open for 0% of the time, Pallas kernels for 18%

profile of v10, /device:TPU:1, one launch (start us, length us, event | category | flops | bytes accessed | tf_op | source)
XLA Modules:
  0.0 89.4 jit_solution(11072867462775509576)
XLA Ops:
  0.6 1.2 %prepare.1 = (s32[8,1024]{1,0:T(8,128)S(1)}, s32[8,1024]{1,0:T(8,128)S(1)}, bf16[400,512]{1,0:T(8,128)(2,1)S(1)}) custom-call(f32[400,512]{1,0:T(8,128)} %bitcast.18, s32[2,1000]{1,0:T(2,128)} %bitcast.20, s32[2,1000]{1,0:T(2,128)} %bitcast.21, s32[2,1000]{1,0:T(2,128)} %bitcast.22, s32[2,500]{1,0:T(2,128)} %bitcast.23), custom_call_target="tpu_custom_call" | custom-call | tf_op jit(solution)/shard_map/prepare/pallas_call | solution.py:56
  1.9 9.7 %collective-permute-start = (s32[8,1024]{1,0:T(8,128)S(1)}, s32[8,1024]{1,0:T(8,128)S(1)}, u32[]{:S(2)}, u32[]{:S(2)}) collective-permute-start(s32[8,1024]{1,0:T(8,128)S(1)} %get-tuple-element.26), channel_id=1, source_target_pairs={{4,0},{8,4},{12,8},{16,12},{20,16},{24,20},{28,24},{32,28},{36,32}... | collective-permute-start | bytes 98312 | tf_op jit(solution)/shard_map/ppermute | solution.py:70
  11.6 0.2 collective-permute-start.1
  11.7 9.4 %first.1 = (f32[400,512]{1,0:T(8,128)S(1)}, f32[1,512]{1,0:T(1,128)S(1)}, f32[2,200,2176]{2,1,0:T(8,128)S(1)}, bf16[400,2176]{1,0:T(8,128)(2,1)S(1)}) custom-call(bf16[400,512]{1,0:T(8,128)(2,1)S(1)} %get-tuple-element.27.left, s32[8,1024]{1,0:T(8,128)S(1)} %get-tuple-element.28.ids, f32[400,512]{1,0:T(8,128)} %bitcast.19, f32[1,512]{1,0:T(1,128)} %state_far.1, ...), custom_call_target="tpu_custom_call" | custom-call | tf_op jit(solution)/shard_map/first/pallas_call | solution.py:56
  21.1 0.0 collective-permute-done.ids
  21.1 2.7 %between.1 = (f32[400,1024]{1,0:T(8,128)S(1)}, bf16[400,512]{1,0:T(8,128)(2,1)S(1)}, f32[400,1024]{1,0:T(8,128)S(1)}) custom-call(f32[400,512]{1,0:T(8,128)S(1)} %get-tuple-element.30.slab, bf16[400,2176]{1,0:T(8,128)(2,1)S(1)} %get-tuple-element.31.table, s32[8,1024]{1,0:T(8,128)S(1)} %collective-permute-done.ids), custom_call_target="tpu_custom_call" | custom-call | flops 20000000000 | tf_op jit(solution)/shard_map/between/pallas_call | solution.py:56
  23.8 0.0 collective-permute-done.1.left
  23.9 4.3 %second.1 = (bf16[400,1024]{1,0:T(8,128)(2,1)S(1)}, bf16[512,1024]{1,0:T(8,128)(2,1)S(1)}, bf16[400,1024]{1,0:T(8,128)(2,1)S(1)}, bf16[2,200,1024]{2,1,0:T(8,128)(2,1)S(1)}, s16[32,104,128]{2,1,0:T(8,128)(2,1)S(1)}) custom-call(s32[1]{0:T(128)} %bitcast.core, bf16[400,512]{1,0:T(8,128)(2,1)S(1)} %collective-permute-done.1.left, ...), custom_call_target="tpu_custom_call" | custom-call | tf_op jit(solution)/shard_map/second/pallas_call | solution.py:56
  28.1 1.5 %collective-permute-start.2 = (s16[32,104,128]{2,1,0:T(8,128)(2,1)S(1)}, s16[32,104,128]{2,1,0:T(8,128)(2,1)S(1)}, u32[]{:S(2)}, u32[]{:S(2)}) collective-permute-start(s16[32,104,128]{2,1,0:T(8,128)(2,1)S(1)} %get-tuple-element.36), channel_id=1, source_target_pairs={{0,1},{1,0},{2,3},{3,2},{4,5},{5,4},{6,7},{7,6},{8,9},{9,8},{10,11... | collective-permute-start | bytes 2555912 | tf_op jit(solution)/shard_map/ppermute | solution.py:74
  29.6 1.6 %own_half.1.mine = f32[200,2176]{1,0:T(8,128)S(1)} custom-call(s32[1]{0:T(128)} %bitcast.core, s32[8,1024]{1,0:T(8,128)S(1)} %collective-permute-done.ids, f32[2,200,2176]{2,1,0:T(8,128)S(1)} %get-tuple-element.29.rel_grad, bf16[2,200,1024]{2,1,0:T(8,128)(2,1)S(1)} %get-tuple-element.35.d_rel), custom_call_target="tpu_custom_call" | custom-call | tf_op jit(solution)/shard_map/own_half/pallas_call | solution.py:56
  31.2 0.4 collective-permute-done.2.theirs
  31.6 0.8 send.1
  32.5 19.5 %all_to_all.15.parts = s16[32,104,128]{2,1,0:T(8,128)(2,1)S(1)} all-to-all(s16[32,104,128]{2,1,0:T(8,128)(2,1)S(1)} %send.1), channel_id=1, replica_groups=mesh['x'=4,'z_hi'=4,'z_lo'=2,'y_lo'=2,'y_hi'=2,'core'=2] {'x','z_lo','y_..., dimensions={0} | all-to-all | bytes 1703936 | tf_op jit(solution)/shard_map/all_to_all | solution.py:413
  52.0 0.3 gather.1
  52.3 11.0 %all_to_all.16.parts = s16[4,104,128]{2,1,0:T(8,128)(2,1)S(1)} all-to-all(s16[4,104,128]{2,1,0:T(8,128)(2,1)S(1)} %gather.1), channel_id=1, replica_groups=mesh['x'=4,'z_hi'=4,'z_lo'=2,'y_lo'=2,'y_hi'=2,'core'=2] {'z_hi'}, dimensions={0} | all-to-all | bytes 212992 | tf_op jit(solution)/shard_map/all_to_all | solution.py:416
  63.3 0.2 spread.1
  63.5 15.2 %all_to_all.17.codes = s16[32,104,128]{2,1,0:T(8,128)(2,1)S(1)} all-to-all(s16[32,104,128]{2,1,0:T(8,128)(2,1)S(1)} %spread.1), channel_id=1, replica_groups=mesh['x'=4,'z_hi'=4,'z_lo'=2,'y_lo'=2,'y_hi'=2,'core'=2] {'x','z_lo','y_..., dimensions={0} | all-to-all | bytes 1703936 | tf_op jit(solution)/shard_map/all_to_all | solution.py:418
  78.8 4.5 %collective-permute-start.3 = (s16[32,104,128]{2,1,0:T(8,128)(2,1)S(1)}, s16[32,104,128]{2,1,0:T(8,128)(2,1)S(1)}, u32[]{:S(2)}, u32[]{:S(2)}) collective-permute-start(s16[32,104,128]{2,1,0:T(8,128)(2,1)S(1)} %all_to_all.17.codes), channel_id=1, source_target_pairs={{0,1},{1,0},{2,3},{3,2},{4,5},{5,4},{6,7},{7,6},{8,9},{9,8},{10,11... | collective-permute-start | bytes 2555912 | tf_op jit(solution)/shard_map/ppermute | solution.py:74
  83.3 0.5 ours.1
  83.8 0.0 copy-start
  83.8 0.0 copy-start.1
  83.8 2.4 %target.1 = (f32[400,512]{1,0:T(8,128)}, f32[1,512]{1,0:T(1,128)}, f32[1,128]{1,0:T(1,128)S(1)}) custom-call(f32[1,2176]{1,0:T(1,128)S(1)} %get-tuple-element.37.after.squares, f32[400,512]{1,0:T(8,128)S(1)} %get-tuple-element.30.slab, f32[1,512]{1,0:T(1,128)S(1)} %get-tuple-element.38.state, s32[8,1024]{1,0:T(8,128)S(1)} %collective-permute-done.ids, ...), custom_call_target="tpu_custom_call" | custom-call | tf_op jit(solution)/shard_map/target/pallas_call | solution.py:56
  86.2 0.0 collective-permute-done.3.codes
  86.2 0.0 copy-done
  86.2 0.0 copy-done.1
  86.2 3.0 %update.1 = (f32[400,2066]{1,0:T(8,128)}, f32[2066]{0:T(1024)}) custom-call(s32[1]{0:T(128)} %bitcast.core, f32[200,2176]{1,0:T(8,128)S(1)} %get-tuple-element.44.ours, f32[1,2176]{1,0:T(1,128)S(1)} %get-tuple-element.37.after.squares, s16[32,104,128]{2,1,0:T(8,128)(2,1)S(1)} %collective-permute-done.3.codes, f32[400,2066]{1,0:T(8,128)S(1)} %bitcast.17, ...), custom_call_target="tpu_custom_call" | custom-call | tf_op jit(solution)/shard_map/update/pallas_call | solution.py:56
Async XLA Ops:
  1.9 19.2 %collective-permute-start = (s32[8,1024]{1,0:T(8,128)S(1)}, s32[8,1024]{1,0:T(8,128)S(1)}, u32[]{:S(2)}, u32[]{:S(2)}) collective-permute-start(s32[8,1024]{1,0:T(8,128)S(1)} %get-tuple-element.26), channel_id=1, source_target_pairs={{4,0},{8,4},{12,8},{16,12},{20,16},{24,20},{28,24},{32,28},{36,32}... | collective-permute-start | bytes 98312 | tf_op jit(solution)/shard_map/ppermute | solution.py:70
  11.6 12.3 %collective-permute-start.1 = (bf16[400,512]{1,0:T(8,128)(2,1)S(1)}, bf16[400,512]{1,0:T(8,128)(2,1)S(1)}, u32[]{:S(2)}, u32[]{:S(2)}) collective-permute-start(bf16[400,512]{1,0:T(8,128)(2,1)S(1)} %get-tuple-element.27.left), channel_id=1, source_target_pairs={{4,0},{8,4},{12,8},{16,12},{20,16},{24,20},{28,24},{32,28},{36,32}... | collective-permute-start | bytes 1228808 | tf_op jit(solution)/shard_map/ppermute | solution.py:70
  28.1 3.5 %collective-permute-start.2 = (s16[32,104,128]{2,1,0:T(8,128)(2,1)S(1)}, s16[32,104,128]{2,1,0:T(8,128)(2,1)S(1)}, u32[]{:S(2)}, u32[]{:S(2)}) collective-permute-start(s16[32,104,128]{2,1,0:T(8,128)(2,1)S(1)} %get-tuple-element.36), channel_id=1, source_target_pairs={{0,1},{1,0},{2,3},{3,2},{4,5},{5,4},{6,7},{7,6},{8,9},{9,8},{10,11... | collective-permute-start | bytes 2555912 | tf_op jit(solution)/shard_map/ppermute | solution.py:74
  78.8 7.4 %collective-permute-start.3 = (s16[32,104,128]{2,1,0:T(8,128)(2,1)S(1)}, s16[32,104,128]{2,1,0:T(8,128)(2,1)S(1)}, u32[]{:S(2)}, u32[]{:S(2)}) collective-permute-start(s16[32,104,128]{2,1,0:T(8,128)(2,1)S(1)} %all_to_all.17.codes), channel_id=1, source_target_pairs={{0,1},{1,0},{2,3},{3,2},{4,5},{5,4},{6,7},{7,6},{8,9},{9,8},{10,11... | collective-permute-start | bytes 2555912 | tf_op jit(solution)/shard_map/ppermute | solution.py:74
  83.8 2.4 %copy-start = (f32[2066,400]{0,1:T(8,128)S(1)}, f32[2066,400]{0,1:T(8,128)}, u32[]{:S(2)}) copy-start(f32[2066,400]{0,1:T(8,128)} %param.12) | copy-start | bytes 9916804
  83.8 2.4 %copy-start.1 = (f32[2066]{0:T(1024)S(1)}, f32[2066]{0:T(1024)}, u32[]{:S(2)}) copy-start(f32[2066]{0:T(1024)} %state.1) | copy-start | bytes 24796

commit v11 on v10

--- a/solution.py
+++ b/solution.py
@@ -100,16 +100,19 @@
     pos = jnp.sum(prod_wide * pos_rows, 0, keepdims=True)
     g_pos = -jax.nn.sigmoid(-pos)
     g_neg = (jax.nn.sigmoid(dot(neg_rows, prod, ((0,), (0,)))) * (1.0 / NEG)).astype(BF16)
-    d_pos = (g_pos * prod_wide).astype(BF16)
     d_prod = g_pos * pos_rows + dot(neg_rows, g_neg)
     p_re, p_im = d_prod[:HALF], d_prod[HALF:]
     d_rel = (p_re * h_re + p_im * h_im, p_im * h_re - p_re * h_im)
-    return prod, g_neg, d_pos, d_rel
-
-
-def trained(slab, state, ids, prod, g_neg, d_pos):
+    return prod, g_neg, g_pos, d_rel
+
+
+def row_terms(prod, g_neg, g_pos):
+    d_pos = (g_pos * prod.astype(F32)).astype(BF16)
+    return d_pos, dot(prod, g_neg, ((1,), (1,))).astype(BF16)
+
+
+def trained(slab, state, ids, d_pos, d_neg):
     along = ((1,), (1,))
-    d_neg = dot(prod, g_neg, along).astype(BF16)
     grad = dot(d_pos, places(ids[1:2], ROWS), along)
     grad = grad + dot(d_neg, places(ids[3:4, :NPAD], ROWS), along)
     state = state + jnp.sum(grad * grad, 0, keepdims=True) * (1.0 / D)
@@ -158,8 +161,10 @@
     table[:, RMAIN:] = jnp.zeros((D, RPAD - RMAIN), BF16)
     table[:, RMAIN:NREL] = relation[:, RMAIN:].astype(BF16)
     rel_rows = relation_rows_of(table[...], ids)
-    prod, g_neg, d_pos, d_rel = edge_terms(heads, pos_rows, neg_rows, rel_rows)
-    slab_out[...], state_out[...] = trained(slab[...], state[...], ids[...], prod, g_neg, d_pos)
+    prod, g_neg, g_pos, d_rel = edge_terms(heads, pos_rows, neg_rows, rel_rows)
+    slab_out[...], state_out[...] = trained(
+        slab[...], state[...], ids[...], *row_terms(prod, g_neg, g_pos)
+    )
     whole = dot(jnp.concatenate(d_rel, 0).astype(BF16), places(ids[2:3], RPAD), ((1,), (1,)))
     for half in range(2):
         rel_grad[half] = whole[half * HALF : half * HALF + HALF]
@@ -175,10 +180,10 @@
 
 
 def second_kernel(
-    core, left, ids, pos_rows, neg_rows, rel_rows, rel_grad, prod, g_neg, d_pos, d_rel, other, grads
+    core, left, ids, pos_rows, neg_rows, rel_rows, rel_grad, prod, g_neg, g_pos, d_rel, other, grads
 ):
     heads = dot(left[...], places(ids[0:1], ROWS))
-    prod[...], g_neg[...], d_pos[...], parts = edge_terms(
+    prod[...], g_neg[...], g_pos[...], parts = edge_terms(
         heads, pos_rows[...], neg_rows[...], rel_rows[...]
     )
     for half in range(2):
@@ -189,13 +194,14 @@
         other[part] = encode(block_of(grads, part), *picked(firsts, seconds, part))
 
 
-def own_half_kernel(core, ids, rel_grad, d_rel, mine):
+def own_half_kernel(core, ids, rel_grad, d_rel, prod, g_neg, g_pos, mine, d_pos, d_neg):
     mine[...] = rel_half(core[0], ids, d_rel, rel_grad)
-
-
-def target_kernel(after, slab, state, ids, prod, g_neg, d_pos, slab_out, state_out, done):
+    d_pos[...], d_neg[...] = row_terms(prod[...], g_neg[...], g_pos[...])
+
+
+def target_kernel(after, slab, state, ids, d_pos, d_neg, slab_out, state_out, done):
     slab_out[...], state_out[...] = trained(
-        slab[...], state[...], ids[...], prod[...], g_neg[...], d_pos[...]
+        slab[...], state[...], ids[...], d_pos[...], d_neg[...]
     )
     done[...] = after[:, :128]
 
@@ -386,12 +392,12 @@
         flops=2 * 10**10,
         name="between",
     )
-    prod, g_neg, d_pos, d_rel, other = call(
+    prod, g_neg, g_pos, d_rel, other = call(
         second_kernel,
         (
             edge_array,
             kept((NPAD, EPAD), BF16),
-            edge_array,
+            kept((1, EPAD), F32),
             kept((2, HALF, EPAD), BF16),
             parts,
         ),
@@ -406,8 +412,17 @@
         name="second",
     )
     theirs = swap_core(other)
-    mine = call(
-        own_half_kernel, half_array, ids_next, rel_grad, d_rel, core=core, name="own_half"
+    mine, d_pos, d_neg = call(
+        own_half_kernel,
+        (half_array, edge_array, kept((D, NPAD), BF16)),
+        ids_next,
+        rel_grad,
+        d_rel,
+        prod,
+        g_neg,
+        g_pos,
+        core=core,
+        name="own_half",
     )
     sent = call(send_kernel, parts, mine, theirs, name="send")
     got = lax.all_to_all(sent, CUBE, 0, 0, tiled=True)
@@ -427,9 +442,8 @@
         slab,
         state,
         ids_next,
-        prod,
-        g_neg,
         d_pos,
+        d_neg,
         name="target",
     )
     relation_out, relation_state_out = call(

time: 89.6 us -> 89.4 us (level)
  blocking collectives: 45.8 us -> 48 us
  starting transfers between devices: 15.9 us -> 14.3 us
    all_to_all x1, blocking collectives: 15.2 us -> 17.1 us  [per_device(): ours = lax.all_to_all(copies, CUBE, 0, 0, tiled=True)]
    ppermute x2, starting transfers between devices: 6.02 us -> 4.41 us  [swap_core(): return lax.ppermute(block, 'core', [(0, 1), (1, 0)])]
  transfers between devices with their start and end apart: 4 -> 4, of which waited for: 1 -> 0; matrix products, arithmetic and copies ran while one was open for 0% -> 0% of each run, Pallas kernels for 18% -> 19%
where the time goes in v11:
time: 89.4 us; the launch traced here: 89.2 us
  blocking collectives  48 us (54%)
  Pallas kernels  26.1 us (29%)
  starting transfers between devices  14.3 us (16%)
  between operations  0.9 us (1%)
    pallas_call x11, Pallas kernels, call(): pl.pallas_call(kernel, out_shape=out_shape, in_specs=in_specs, out_specs=...  26.1 us
    all_to_all x1, blocking collectives, per_device(): got = lax.all_to_all(sent, CUBE, 0, 0, tiled=True)  19.7 us
    all_to_all x1, blocking collectives, per_device(): ours = lax.all_to_all(copies, CUBE, 0, 0, tiled=True)  17.1 us
    all_to_all x1, blocking collectives, per_device(): codes = lax.all_to_all(codes, 'z_hi', 0, 0, tiled=True)  11.2 us
    ppermute x2, starting transfers between devices, from_next(): lax.ppermute(block, BUCKET, [((i + 1) % count, i) for i in range(count)])  9.86 us
    ppermute x2, starting transfers between devices, swap_core(): return lax.ppermute(block, 'core', [(0, 1), (1, 0)])  4.41 us
  transfers between devices with their start and end apart: 4, of which 0 were waited for; matrix products, arithmetic and copies ran while one was open for 0% of the time, Pallas kernels for 19%

profile of v11, /device:TPU:1, one launch (start us, length us, event | category | flops | bytes accessed | tf_op | source)
XLA Modules:
  0.0 89.2 jit_solution(15762875393730492930)
XLA Ops:
  0.6 1.2 %prepare.1 = (s32[8,1024]{1,0:T(8,128)S(1)}, s32[8,1024]{1,0:T(8,128)S(1)}, bf16[400,512]{1,0:T(8,128)(2,1)S(1)}) custom-call(f32[400,512]{1,0:T(8,128)} %bitcast.18, s32[2,1000]{1,0:T(2,128)} %bitcast.20, s32[2,1000]{1,0:T(2,128)} %bitcast.21, s32[2,1000]{1,0:T(2,128)} %bitcast.22, s32[2,500]{1,0:T(2,128)} %bitcast.23), custom_call_target="tpu_custom_call" | custom-call | tf_op jit(solution)/shard_map/prepare/pallas_call | solution.py:56
  1.9 9.7 %collective-permute-start = (s32[8,1024]{1,0:T(8,128)S(1)}, s32[8,1024]{1,0:T(8,128)S(1)}, u32[]{:S(2)}, u32[]{:S(2)}) collective-permute-start(s32[8,1024]{1,0:T(8,128)S(1)} %get-tuple-element.29), channel_id=1, source_target_pairs={{4,0},{8,4},{12,8},{16,12},{20,16},{24,20},{28,24},{32,28},{36,32}... | collective-permute-start | bytes 98312 | tf_op jit(solution)/shard_map/ppermute | solution.py:70
  11.6 0.2 collective-permute-start.1
  11.7 9.4 %first.1 = (f32[400,512]{1,0:T(8,128)S(1)}, f32[1,512]{1,0:T(1,128)S(1)}, f32[2,200,2176]{2,1,0:T(8,128)S(1)}, bf16[400,2176]{1,0:T(8,128)(2,1)S(1)}) custom-call(bf16[400,512]{1,0:T(8,128)(2,1)S(1)} %get-tuple-element.30.left, s32[8,1024]{1,0:T(8,128)S(1)} %get-tuple-element.31.ids, f32[400,512]{1,0:T(8,128)} %bitcast.19, f32[1,512]{1,0:T(1,128)} %state_far.1, ...), custom_call_target="tpu_custom_call" | custom-call | tf_op jit(solution)/shard_map/first/pallas_call | solution.py:56
  21.1 0.0 collective-permute-done.ids
  21.1 2.7 %between.1 = (f32[400,1024]{1,0:T(8,128)S(1)}, bf16[400,512]{1,0:T(8,128)(2,1)S(1)}, f32[400,1024]{1,0:T(8,128)S(1)}) custom-call(f32[400,512]{1,0:T(8,128)S(1)} %get-tuple-element.33.slab, bf16[400,2176]{1,0:T(8,128)(2,1)S(1)} %get-tuple-element.34.table, s32[8,1024]{1,0:T(8,128)S(1)} %collective-permute-done.ids), custom_call_target="tpu_custom_call" | custom-call | flops 20000000000 | tf_op jit(solution)/shard_map/between/pallas_call | solution.py:56
  23.8 0.0 collective-permute-done.1.left
  23.8 4.0 %second.1 = (bf16[400,1024]{1,0:T(8,128)(2,1)S(1)}, bf16[512,1024]{1,0:T(8,128)(2,1)S(1)}, f32[1,1024]{1,0:T(1,128)S(1)}, bf16[2,200,1024]{2,1,0:T(8,128)(2,1)S(1)}, s16[32,104,128]{2,1,0:T(8,128)(2,1)S(1)}) custom-call(s32[1]{0:T(128)} %bitcast.core, bf16[400,512]{1,0:T(8,128)(2,1)S(1)} %collective-permute-done.1.left, ...), custom_call_target="tpu_custom_call" | custom-call | tf_op jit(solution)/shard_map/second/pallas_call | solution.py:56
  27.8 1.5 %collective-permute-start.2 = (s16[32,104,128]{2,1,0:T(8,128)(2,1)S(1)}, s16[32,104,128]{2,1,0:T(8,128)(2,1)S(1)}, u32[]{:S(2)}, u32[]{:S(2)}) collective-permute-start(s16[32,104,128]{2,1,0:T(8,128)(2,1)S(1)} %get-tuple-element.43), channel_id=1, source_target_pairs={{0,1},{1,0},{2,3},{3,2},{4,5},{5,4},{6,7},{7,6},{8,9},{9,8},{10,11... | collective-permute-start | bytes 2555912 | tf_op jit(solution)/shard_map/ppermute | solution.py:74
  29.3 2.1 %own_half.1 = (f32[200,2176]{1,0:T(8,128)S(1)}, bf16[400,1024]{1,0:T(8,128)(2,1)S(1)}, bf16[400,512]{1,0:T(8,128)(2,1)S(1)}) custom-call(s32[1]{0:T(128)} %bitcast.core, s32[8,1024]{1,0:T(8,128)S(1)} %collective-permute-done.ids, f32[2,200,2176]{2,1,0:T(8,128)S(1)} %get-tuple-element.32.rel_grad, bf16[2,200,1024]{2,1,0:T(8,128)(2,1)S(1)} %get-tuple-element.38.d_rel, ...), custom_call_target="tpu_custom_call" | custom-call | tf_op jit(solution)/shard_map/own_half/pallas_call | solution.py:56
  31.4 0.0 collective-permute-done.2.theirs
  31.4 0.8 send.1
  32.2 19.7 %all_to_all.15.parts = s16[32,104,128]{2,1,0:T(8,128)(2,1)S(1)} all-to-all(s16[32,104,128]{2,1,0:T(8,128)(2,1)S(1)} %send.1), channel_id=1, replica_groups=mesh['x'=4,'z_hi'=4,'z_lo'=2,'y_lo'=2,'y_hi'=2,'core'=2] {'x','z_lo','y_..., dimensions={0} | all-to-all | bytes 1703936 | tf_op jit(solution)/shard_map/all_to_all | solution.py:428
  51.9 0.3 gather.1
  52.2 11.2 %all_to_all.16.parts = s16[4,104,128]{2,1,0:T(8,128)(2,1)S(1)} all-to-all(s16[4,104,128]{2,1,0:T(8,128)(2,1)S(1)} %gather.1), channel_id=1, replica_groups=mesh['x'=4,'z_hi'=4,'z_lo'=2,'y_lo'=2,'y_hi'=2,'core'=2] {'z_hi'}, dimensions={0} | all-to-all | bytes 212992 | tf_op jit(solution)/shard_map/all_to_all | solution.py:431
  63.5 0.2 spread.1
  63.7 0.0 copy-start
  63.7 17.1 %all_to_all.17.codes = s16[32,104,128]{2,1,0:T(8,128)(2,1)S(1)} all-to-all(s16[32,104,128]{2,1,0:T(8,128)(2,1)S(1)} %spread.1), channel_id=1, replica_groups=mesh['x'=4,'z_hi'=4,'z_lo'=2,'y_lo'=2,'y_hi'=2,'core'=2] {'x','z_lo','y_..., dimensions={0} | all-to-all | bytes 1703936 | tf_op jit(solution)/shard_map/all_to_all | solution.py:433
  80.7 0.0 copy-start.1
  80.7 2.9 %collective-permute-start.3 = (s16[32,104,128]{2,1,0:T(8,128)(2,1)S(1)}, s16[32,104,128]{2,1,0:T(8,128)(2,1)S(1)}, u32[]{:S(2)}, u32[]{:S(2)}) collective-permute-start(s16[32,104,128]{2,1,0:T(8,128)(2,1)S(1)} %all_to_all.17.codes), channel_id=1, source_target_pairs={{0,1},{1,0},{2,3},{3,2},{4,5},{5,4},{6,7},{7,6},{8,9},{9,8},{10,11... | collective-permute-start | bytes 2555912 | tf_op jit(solution)/shard_map/ppermute | solution.py:74
  83.6 0.5 ours.1
  84.1 1.9 %target.1 = (f32[400,512]{1,0:T(8,128)}, f32[1,512]{1,0:T(1,128)}, f32[1,128]{1,0:T(1,128)S(1)}) custom-call(f32[1,2176]{1,0:T(1,128)S(1)} %get-tuple-element.44.after.squares, f32[400,512]{1,0:T(8,128)S(1)} %get-tuple-element.33.slab, f32[1,512]{1,0:T(1,128)S(1)} %get-tuple-element.45.state, s32[8,1024]{1,0:T(8,128)S(1)} %collective-permute-done.ids, ...), custom_call_target="tpu_custom_call" | custom-call | tf_op jit(solution)/shard_map/target/pallas_call | solution.py:56
  86.0 0.0 collective-permute-done.3.codes
  86.0 0.0 copy-done
  86.0 0.0 copy-done.1
  86.0 3.0 %update.1 = (f32[400,2066]{1,0:T(8,128)}, f32[2066]{0:T(1024)}) custom-call(s32[1]{0:T(128)} %bitcast.core, f32[200,2176]{1,0:T(8,128)S(1)} %get-tuple-element.50.ours, f32[1,2176]{1,0:T(1,128)S(1)} %get-tuple-element.44.after.squares, s16[32,104,128]{2,1,0:T(8,128)(2,1)S(1)} %collective-permute-done.3.codes, f32[400,2066]{1,0:T(8,128)S(1)} %bitcast.17, ...), custom_call_target="tpu_custom_call" | custom-call | tf_op jit(solution)/shard_map/update/pallas_call | solution.py:56
Async XLA Ops:
  1.9 19.2 %collective-permute-start = (s32[8,1024]{1,0:T(8,128)S(1)}, s32[8,1024]{1,0:T(8,128)S(1)}, u32[]{:S(2)}, u32[]{:S(2)}) collective-permute-start(s32[8,1024]{1,0:T(8,128)S(1)} %get-tuple-element.29), channel_id=1, source_target_pairs={{4,0},{8,4},{12,8},{16,12},{20,16},{24,20},{28,24},{32,28},{36,32}... | collective-permute-start | bytes 98312 | tf_op jit(solution)/shard_map/ppermute | solution.py:70
  11.6 12.3 %collective-permute-start.1 = (bf16[400,512]{1,0:T(8,128)(2,1)S(1)}, bf16[400,512]{1,0:T(8,128)(2,1)S(1)}, u32[]{:S(2)}, u32[]{:S(2)}) collective-permute-start(bf16[400,512]{1,0:T(8,128)(2,1)S(1)} %get-tuple-element.30.left), channel_id=1, source_target_pairs={{4,0},{8,4},{12,8},{16,12},{20,16},{24,20},{28,24},{32,28},{36,32}... | collective-permute-start | bytes 1228808 | tf_op jit(solution)/shard_map/ppermute | solution.py:70
  27.8 3.6 %collective-permute-start.2 = (s16[32,104,128]{2,1,0:T(8,128)(2,1)S(1)}, s16[32,104,128]{2,1,0:T(8,128)(2,1)S(1)}, u32[]{:S(2)}, u32[]{:S(2)}) collective-permute-start(s16[32,104,128]{2,1,0:T(8,128)(2,1)S(1)} %get-tuple-element.43), channel_id=1, source_target_pairs={{0,1},{1,0},{2,3},{3,2},{4,5},{5,4},{6,7},{7,6},{8,9},{9,8},{10,11... | collective-permute-start | bytes 2555912 | tf_op jit(solution)/shard_map/ppermute | solution.py:74
  63.7 22.3 %copy-start = (f32[2066,400]{0,1:T(8,128)S(1)}, f32[2066,400]{0,1:T(8,128)}, u32[]{:S(2)}) copy-start(f32[2066,400]{0,1:T(8,128)} %param.12) | copy-start | bytes 9916804
  80.7 5.3 %copy-start.1 = (f32[2066]{0:T(1024)S(1)}, f32[2066]{0:T(1024)}, u32[]{:S(2)}) copy-start(f32[2066]{0:T(1024)} %state.1) | copy-start | bytes 24796
  80.7 5.3 %collective-permute-start.3 = (s16[32,104,128]{2,1,0:T(8,128)(2,1)S(1)}, s16[32,104,128]{2,1,0:T(8,128)(2,1)S(1)}, u32[]{:S(2)}, u32[]{:S(2)}) collective-permute-start(s16[32,104,128]{2,1,0:T(8,128)(2,1)S(1)} %all_to_all.17.codes), channel_id=1, source_target_pairs={{0,1},{1,0},{2,3},{3,2},{4,5},{5,4},{6,7},{7,6},{8,9},{9,8},{10,11... | collective-permute-start | bytes 2555912 | tf_op jit(solution)/shard_map/ppermute | solution.py:74

commit v12 on v11

--- a/solution.py
+++ b/solution.py
@@ -199,11 +199,10 @@
     d_pos[...], d_neg[...] = row_terms(prod[...], g_neg[...], g_pos[...])
 
 
-def target_kernel(after, slab, state, ids, d_pos, d_neg, slab_out, state_out, done):
+def target_kernel(after, slab, state, ids, d_pos, d_neg, slab_out, state_out):
     slab_out[...], state_out[...] = trained(
         slab[...], state[...], ids[...], d_pos[...], d_neg[...]
     )
-    done[...] = after[:, :128]
 
 
 def power_of(top):
@@ -277,45 +276,75 @@
         codes[copy] = code
 
 
-def decoded_into(codes, grads, last):
+def decode_tile(codes, tile, grads, last):
+    lanes = slice(128 * tile, 128 * tile + 128)
+    blocks = []
+    for part in (2 * tile, 2 * tile + 1):
+        block, first, second = decode(codes[part])
+        blocks.append(block)
+        if part < EXTRA:
+            last[part : part + 1, :128] = first
+            last[part : part + 1, 128:] = second
+    upper, lower = blocks[0], pltpu.roll(blocks[1], PART - CUT, 0)
+    grads[: HALF - PART, lanes] = upper[: HALF - PART]
+    grads[HALF - PART : PART, lanes] = upper[HALF - PART :] + lower[: 2 * PART - HALF]
+    grads[PART:, lanes] = lower[2 * PART - HALF :]
+
+
+def squares_of(grads):
+    return jnp.sum(grads * grads, 0, keepdims=True)
+
+
+def ours_kernel(codes, grads, squares, last):
     last[...] = jnp.zeros(last.shape, F32)
     for tile in range(OWNERS // 2):
-        lanes = slice(128 * tile, 128 * tile + 128)
-        blocks = []
-        for part in (2 * tile, 2 * tile + 1):
-            block, first, second = decode(codes[part])
-            blocks.append(block)
-            if part < EXTRA:
-                last[part : part + 1, :128] = first
-                last[part : part + 1, 128:] = second
-        upper, lower = blocks[0], pltpu.roll(blocks[1], PART - CUT, 0)
-        grads[: HALF - PART, lanes] = upper[: HALF - PART]
-        grads[HALF - PART : PART, lanes] = upper[HALF - PART :] + lower[: 2 * PART - HALF]
-        grads[PART:, lanes] = lower[2 * PART - HALF :]
+        decode_tile(codes, tile, grads, last)
     grads[:, RMAIN:] = jnp.transpose(last[...])[:HALF]
-    return jnp.sum(grads[...] * grads[...], 0, keepdims=True)
-
-
-def ours_kernel(codes, grads, squares, last):
-    squares[...] = decoded_into(codes, grads, last)
+    squares[...] = squares_of(grads[...])
+
+
+GROUPS = ((0, 512), (512, 1024), (1024, 1536), (1536, RPAD))
 
 
 def update_kernel(
-    core, ours, squares, codes, relation, state, done, relation_out, state_out, theirs, last, wide, sems
+    core,
+    ours,
+    squares,
+    codes,
+    relation,
+    state,
+    slab,
+    relation_out,
+    slab_out,
+    state_out,
+    theirs,
+    last,
+    wide,
+    sems,
 ):
-    total = squares[...] + decoded_into(codes, theirs, last)
-    new_state = state[...].reshape(1, NREL) + total[:, :NREL] * (1.0 / D)
-    rate = 0.2 * lax.rsqrt(new_state)
-    state_out[...] = new_state.reshape(NREL)
-    copies = []
-    for grad, half in ((ours, core[0]), (theirs, 1 - core[0])):
-        for start, stop in ((0, 56), (56, 104), (104, 152), (152, 200)):
-            rows = pl.ds(pl.multiple_of(half * HALF + start, 8), stop - start)
-            wide[rows] = relation[rows] - grad[start:stop, :NREL] * rate
-            copies.append(
-                pltpu.make_async_copy(wide.at[rows], relation_out.at[rows], sems.at[len(copies)])
-            )
-            copies[-1].start()
+    copies = [pltpu.make_async_copy(slab, slab_out, sems.at[len(GROUPS)])]
+    copies[0].start()
+    last[...] = jnp.zeros(last.shape, F32)
+    old_state = state[...].reshape(1, NREL)
+    halves = [pl.ds(pl.multiple_of(half * HALF, 8), HALF) for half in (core[0], 1 - core[0])]
+    states = []
+    for place, (start, stop) in enumerate(GROUPS):
+        for tile in range(start // 128, min(stop, RMAIN) // 128):
+            decode_tile(codes, tile, theirs, last)
+        if stop == RPAD:
+            theirs[:, RMAIN:] = jnp.transpose(last[...])[:HALF]
+        total = squares[:, start:stop] + squares_of(theirs[:, start:stop])
+        end = min(stop, NREL)
+        lanes = slice(start, end)
+        states.append(old_state[:, lanes] + total[:, : end - start] * (1.0 / D))
+        rate = 0.2 * lax.rsqrt(states[-1])
+        for rows, grad in zip(halves, (ours, theirs)):
+            wide[rows, lanes] = relation[rows, lanes] - grad[:, lanes] * rate
+        copies.append(
+            pltpu.make_async_copy(wide.at[:, lanes], relation_out.at[:, lanes], sems.at[place])
+        )
+        copies[-1].start()
+    state_out[...] = jnp.concatenate(states, 1).reshape(NREL)
     for copy in copies:
         copy.wait()
 
@@ -435,9 +464,9 @@
     grads, squares = call(
         ours_kernel, (half_array, kept((1, RPAD), F32)), ours, scratch=[last], name="ours"
     )
-    slab_out, state_out, done = call(
+    slab, state_out = call(
         target_kernel,
-        (struct(slab_array, F32), struct(state_array, F32), kept((1, 128), F32)),
+        (kept(slab_array, F32), struct(state_array, F32)),
         squares,
         slab,
         state,
@@ -446,22 +475,22 @@
         d_neg,
         name="target",
     )
-    relation_out, relation_state_out = call(
+    relation_out, slab_out, relation_state_out = call(
         update_kernel,
-        (struct((D, NREL), F32), struct((NREL,), F32)),
+        (struct((D, NREL), F32), struct(slab_array, F32), struct((NREL,), F32)),
         grads,
         squares,
         theirs,
         relation,
         relation_state,
-        done,
+        slab,
         core=core,
-        far_out=(0,),
+        far_out=(0, 1),
         scratch=[
             pltpu.VMEM((HALF, RPAD), F32),
             last,
             pltpu.VMEM((D, NREL), F32),
-            dma((8,)),
+            dma((len(GROUPS) + 1,)),
         ],
         name="update",
     )

time: 89.4 us -> 88.8 us (level)
  transfers between devices with their start and end apart: 4 -> 4, of which waited for: 0 -> 1; matrix products, arithmetic and copies ran while one was open for 0% -> 0% of each run, Pallas kernels for 19% -> 18%
where the time goes in v12:
time: 88.8 us; the launch traced here: 88.6 us
  blocking collectives  48 us (54%)
  Pallas kernels  25.3 us (28%)
  starting transfers between devices  14.3 us (16%)
  between operations  0.89 us (1%)
    pallas_call x11, Pallas kernels, call(): pl.pallas_call(kernel, out_shape=out_shape, in_specs=in_specs, out_specs=...  25.3 us
    all_to_all x1, blocking collectives, per_device(): got = lax.all_to_all(sent, CUBE, 0, 0, tiled=True)  19.6 us
    all_to_all x1, blocking collectives, per_device(): ours = lax.all_to_all(copies, CUBE, 0, 0, tiled=True)  17.1 us
    all_to_all x1, blocking collectives, per_device(): codes = lax.all_to_all(codes, 'z_hi', 0, 0, tiled=True)  11.3 us
    ppermute x2, starting transfers between devices, from_next(): lax.ppermute(block, BUCKET, [((i + 1) % count, i) for i in range(count)])  9.86 us
    ppermute x2, starting transfers between devices, swap_core(): return lax.ppermute(block, 'core', [(0, 1), (1, 0)])  4.41 us
  transfers between devices with their start and end apart: 4, of which 1 were waited for; matrix products, arithmetic and copies ran while one was open for 0% of the time, Pallas kernels for 18%

profile of v12, /device:TPU:1, one launch (start us, length us, event | category | flops | bytes accessed | tf_op | source)
XLA Modules:
  0.0 88.6 jit_solution(4124360862628688672)
XLA Ops:
  0.6 1.2 %prepare.1 = (s32[8,1024]{1,0:T(8,128)S(1)}, s32[8,1024]{1,0:T(8,128)S(1)}, bf16[400,512]{1,0:T(8,128)(2,1)S(1)}) custom-call(f32[400,512]{1,0:T(8,128)} %bitcast.18, s32[2,1000]{1,0:T(2,128)} %bitcast.20, s32[2,1000]{1,0:T(2,128)} %bitcast.21, s32[2,1000]{1,0:T(2,128)} %bitcast.22, s32[2,500]{1,0:T(2,128)} %bitcast.23), custom_call_target="tpu_custom_call" | custom-call | tf_op jit(solution)/shard_map/prepare/pallas_call | solution.py:56
  1.9 9.7 %collective-permute-start = (s32[8,1024]{1,0:T(8,128)S(1)}, s32[8,1024]{1,0:T(8,128)S(1)}, u32[]{:S(2)}, u32[]{:S(2)}) collective-permute-start(s32[8,1024]{1,0:T(8,128)S(1)} %get-tuple-element.29), channel_id=1, source_target_pairs={{4,0},{8,4},{12,8},{16,12},{20,16},{24,20},{28,24},{32,28},{36,32}... | collective-permute-start | bytes 98312 | tf_op jit(solution)/shard_map/ppermute | solution.py:70
  11.6 0.2 collective-permute-start.1
  11.7 9.4 %first.1 = (f32[400,512]{1,0:T(8,128)S(1)}, f32[1,512]{1,0:T(1,128)S(1)}, f32[2,200,2176]{2,1,0:T(8,128)S(1)}, bf16[400,2176]{1,0:T(8,128)(2,1)S(1)}) custom-call(bf16[400,512]{1,0:T(8,128)(2,1)S(1)} %get-tuple-element.30.left, s32[8,1024]{1,0:T(8,128)S(1)} %get-tuple-element.31.ids, f32[400,512]{1,0:T(8,128)} %bitcast.19, f32[1,512]{1,0:T(1,128)} %state_far.1, ...), custom_call_target="tpu_custom_call" | custom-call | tf_op jit(solution)/shard_map/first/pallas_call | solution.py:56
  21.1 0.0 collective-permute-done.ids
  21.1 2.7 %between.1 = (f32[400,1024]{1,0:T(8,128)S(1)}, bf16[400,512]{1,0:T(8,128)(2,1)S(1)}, f32[400,1024]{1,0:T(8,128)S(1)}) custom-call(f32[400,512]{1,0:T(8,128)S(1)} %get-tuple-element.33.slab, bf16[400,2176]{1,0:T(8,128)(2,1)S(1)} %get-tuple-element.34.table, s32[8,1024]{1,0:T(8,128)S(1)} %collective-permute-done.ids), custom_call_target="tpu_custom_call" | custom-call | flops 20000000000 | tf_op jit(solution)/shard_map/between/pallas_call | solution.py:56
  23.8 0.0 collective-permute-done.1.left
  23.8 4.0 %second.1 = (bf16[400,1024]{1,0:T(8,128)(2,1)S(1)}, bf16[512,1024]{1,0:T(8,128)(2,1)S(1)}, f32[1,1024]{1,0:T(1,128)S(1)}, bf16[2,200,1024]{2,1,0:T(8,128)(2,1)S(1)}, s16[32,104,128]{2,1,0:T(8,128)(2,1)S(1)}) custom-call(s32[1]{0:T(128)} %bitcast.core, bf16[400,512]{1,0:T(8,128)(2,1)S(1)} %collective-permute-done.1.left, ...), custom_call_target="tpu_custom_call" | custom-call | tf_op jit(solution)/shard_map/second/pallas_call | solution.py:56
  27.8 1.5 %collective-permute-start.2 = (s16[32,104,128]{2,1,0:T(8,128)(2,1)S(1)}, s16[32,104,128]{2,1,0:T(8,128)(2,1)S(1)}, u32[]{:S(2)}, u32[]{:S(2)}) collective-permute-start(s16[32,104,128]{2,1,0:T(8,128)(2,1)S(1)} %get-tuple-element.43), channel_id=1, source_target_pairs={{0,1},{1,0},{2,3},{3,2},{4,5},{5,4},{6,7},{7,6},{8,9},{9,8},{10,11... | collective-permute-start | bytes 2555912 | tf_op jit(solution)/shard_map/ppermute | solution.py:74
  29.3 2.1 %own_half.1 = (f32[200,2176]{1,0:T(8,128)S(1)}, bf16[400,1024]{1,0:T(8,128)(2,1)S(1)}, bf16[400,512]{1,0:T(8,128)(2,1)S(1)}) custom-call(s32[1]{0:T(128)} %bitcast.core, s32[8,1024]{1,0:T(8,128)S(1)} %collective-permute-done.ids, f32[2,200,2176]{2,1,0:T(8,128)S(1)} %get-tuple-element.32.rel_grad, bf16[2,200,1024]{2,1,0:T(8,128)(2,1)S(1)} %get-tuple-element.38.d_rel, ...), custom_call_target="tpu_custom_call" | custom-call | tf_op jit(solution)/shard_map/own_half/pallas_call | solution.py:56
  31.4 0.0 collective-permute-done.2.theirs
  31.4 0.8 send.1
  32.2 19.6 %all_to_all.15.parts = s16[32,104,128]{2,1,0:T(8,128)(2,1)S(1)} all-to-all(s16[32,104,128]{2,1,0:T(8,128)(2,1)S(1)} %send.1), channel_id=1, replica_groups=mesh['x'=4,'z_hi'=4,'z_lo'=2,'y_lo'=2,'y_hi'=2,'core'=2] {'x','z_lo','y_..., dimensions={0} | all-to-all | bytes 1703936 | tf_op jit(solution)/shard_map/all_to_all | solution.py:457
  51.9 0.3 gather.1
  52.2 11.3 %all_to_all.16.parts = s16[4,104,128]{2,1,0:T(8,128)(2,1)S(1)} all-to-all(s16[4,104,128]{2,1,0:T(8,128)(2,1)S(1)} %gather.1), channel_id=1, replica_groups=mesh['x'=4,'z_hi'=4,'z_lo'=2,'y_lo'=2,'y_hi'=2,'core'=2] {'z_hi'}, dimensions={0} | all-to-all | bytes 212992 | tf_op jit(solution)/shard_map/all_to_all | solution.py:460
  63.5 0.2 spread.1
  63.7 0.0 copy-start
  63.7 17.1 %all_to_all.17.codes = s16[32,104,128]{2,1,0:T(8,128)(2,1)S(1)} all-to-all(s16[32,104,128]{2,1,0:T(8,128)(2,1)S(1)} %spread.1), channel_id=1, replica_groups=mesh['x'=4,'z_hi'=4,'z_lo'=2,'y_lo'=2,'y_hi'=2,'core'=2] {'x','z_lo','y_..., dimensions={0} | all-to-all | bytes 1703936 | tf_op jit(solution)/shard_map/all_to_all | solution.py:462
  80.7 0.0 copy-start.1
  80.7 2.9 %collective-permute-start.3 = (s16[32,104,128]{2,1,0:T(8,128)(2,1)S(1)}, s16[32,104,128]{2,1,0:T(8,128)(2,1)S(1)}, u32[]{:S(2)}, u32[]{:S(2)}) collective-permute-start(s16[32,104,128]{2,1,0:T(8,128)(2,1)S(1)} %all_to_all.17.codes), channel_id=1, source_target_pairs={{0,1},{1,0},{2,3},{3,2},{4,5},{5,4},{6,7},{7,6},{8,9},{9,8},{10,11... | collective-permute-start | bytes 2555912 | tf_op jit(solution)/shard_map/ppermute | solution.py:74
  83.6 0.5 ours.1
  84.1 1.4 %target.1 = (f32[400,512]{1,0:T(8,128)S(1)}, f32[1,512]{1,0:T(1,128)}) custom-call(f32[1,2176]{1,0:T(1,128)S(1)} %get-tuple-element.45.after.squares, f32[400,512]{1,0:T(8,128)S(1)} %get-tuple-element.33.slab, f32[1,512]{1,0:T(1,128)S(1)} %get-tuple-element.46.state, s32[8,1024]{1,0:T(8,128)S(1)} %collective-permute-done.ids, ...), custom_call_target="tpu_custom_call" | custom-call | tf_op jit(solution)/shard_map/target/pallas_call | solution.py:56
  85.5 0.1 collective-permute-done.3.codes
  85.6 0.0 copy-done
  85.6 0.0 copy-done.1
  85.6 2.8 %update.1 = (f32[400,2066]{1,0:T(8,128)}, f32[400,512]{1,0:T(8,128)}, f32[2066]{0:T(1024)}) custom-call(s32[1]{0:T(128)} %bitcast.core, f32[200,2176]{1,0:T(8,128)S(1)} %get-tuple-element.44.ours, f32[1,2176]{1,0:T(1,128)S(1)} %get-tuple-element.45.after.squares, s16[32,104,128]{2,1,0:T(8,128)(2,1)S(1)} %collective-permute-done.3.codes, ...), custom_call_target="tpu_custom_call" | custom-call | tf_op jit(solution)/shard_map/update/pallas_call | solution.py:56
Async XLA Ops:
  1.9 19.2 %collective-permute-start = (s32[8,1024]{1,0:T(8,128)S(1)}, s32[8,1024]{1,0:T(8,128)S(1)}, u32[]{:S(2)}, u32[]{:S(2)}) collective-permute-start(s32[8,1024]{1,0:T(8,128)S(1)} %get-tuple-element.29), channel_id=1, source_target_pairs={{4,0},{8,4},{12,8},{16,12},{20,16},{24,20},{28,24},{32,28},{36,32}... | collective-permute-start | bytes 98312 | tf_op jit(solution)/shard_map/ppermute | solution.py:70
  11.6 12.3 %collective-permute-start.1 = (bf16[400,512]{1,0:T(8,128)(2,1)S(1)}, bf16[400,512]{1,0:T(8,128)(2,1)S(1)}, u32[]{:S(2)}, u32[]{:S(2)}) collective-permute-start(bf16[400,512]{1,0:T(8,128)(2,1)S(1)} %get-tuple-element.30.left), channel_id=1, source_target_pairs={{4,0},{8,4},{12,8},{16,12},{20,16},{24,20},{28,24},{32,28},{36,32}... | collective-permute-start | bytes 1228808 | tf_op jit(solution)/shard_map/ppermute | solution.py:70
  27.8 3.6 %collective-permute-start.2 = (s16[32,104,128]{2,1,0:T(8,128)(2,1)S(1)}, s16[32,104,128]{2,1,0:T(8,128)(2,1)S(1)}, u32[]{:S(2)}, u32[]{:S(2)}) collective-permute-start(s16[32,104,128]{2,1,0:T(8,128)(2,1)S(1)} %get-tuple-element.43), channel_id=1, source_target_pairs={{0,1},{1,0},{2,3},{3,2},{4,5},{5,4},{6,7},{7,6},{8,9},{9,8},{10,11... | collective-permute-start | bytes 2555912 | tf_op jit(solution)/shard_map/ppermute | solution.py:74
  63.7 22.0 %copy-start = (f32[2066,400]{0,1:T(8,128)S(1)}, f32[2066,400]{0,1:T(8,128)}, u32[]{:S(2)}) copy-start(f32[2066,400]{0,1:T(8,128)} %param.12) | copy-start | bytes 9916804
  80.7 4.9 %copy-start.1 = (f32[2066]{0:T(1024)S(1)}, f32[2066]{0:T(1024)}, u32[]{:S(2)}) copy-start(f32[2066]{0:T(1024)} %state.1) | copy-start | bytes 24796
  80.7 4.9 %collective-permute-start.3 = (s16[32,104,128]{2,1,0:T(8,128)(2,1)S(1)}, s16[32,104,128]{2,1,0:T(8,128)(2,1)S(1)}, u32[]{:S(2)}, u32[]{:S(2)}) collective-permute-start(s16[32,104,128]{2,1,0:T(8,128)(2,1)S(1)} %all_to_all.17.codes), channel_id=1, source_target_pairs={{0,1},{1,0},{2,3},{3,2},{4,5},{5,4},{6,7},{7,6},{8,9},{9,8},{10,11... | collective-permute-start | bytes 2555912 | tf_op jit(solution)/shard_map/ppermute | solution.py:74

commit v13 on v12

--- a/solution.py
+++ b/solution.py
@@ -136,7 +136,7 @@
     left_low[...] = wide[...].astype(BF16)
 
 
-CHUNKS = ((0, 104), (104, 200), (200, 304), (304, 400))
+GROUPS = ((0, 512), (512, 1024), (1024, 1536), (1536, RPAD))
 
 
 def first_kernel(
@@ -146,21 +146,23 @@
         pltpu.make_async_copy(slab_far, slab, sems.at[0]),
         pltpu.make_async_copy(state_far, state, sems.at[1]),
     ]
-    for i, (start, stop) in enumerate(CHUNKS):
-        rows = slice(start, stop)
-        copies.append(pltpu.make_async_copy(relation_far.at[rows], relation.at[rows], sems.at[2 + i]))
+    for i, (start, stop) in enumerate(GROUPS):
+        at = (slice(None), slice(start, min(stop, NREL)))
+        copies.append(pltpu.make_async_copy(relation_far.at[at], relation.at[at], sems.at[2 + i]))
     for copy in copies:
         copy.start()
     heads = dot(left[...], places(ids[0:1], ROWS))
     for copy in copies[:2]:
         copy.wait()
     pos_rows, neg_rows = target_rows_of(slab[...].astype(BF16), ids)
-    for copy in copies[2:]:
+    table[:, RMAIN:] = jnp.zeros((D, RPAD - RMAIN), BF16)
+    rel_rows = 0.0
+    for copy, (start, stop) in zip(copies[2:], GROUPS):
         copy.wait()
-    table[:, :RMAIN] = relation[:, :RMAIN].astype(BF16)
-    table[:, RMAIN:] = jnp.zeros((D, RPAD - RMAIN), BF16)
-    table[:, RMAIN:NREL] = relation[:, RMAIN:].astype(BF16)
-    rel_rows = relation_rows_of(table[...], ids)
+        end = min(stop, NREL)
+        table[:, start:end] = relation[:, start:end].astype(BF16)
+        found = places(ids[2:3] - start, stop - start)
+        rel_rows = rel_rows + dot(table[:, start:stop], found)
     prod, g_neg, g_pos, d_rel = edge_terms(heads, pos_rows, neg_rows, rel_rows)
     slab_out[...], state_out[...] = trained(
         slab[...], state[...], ids[...], *row_terms(prod, g_neg, g_pos)
@@ -301,9 +303,6 @@
         decode_tile(codes, tile, grads, last)
     grads[:, RMAIN:] = jnp.transpose(last[...])[:HALF]
     squares[...] = squares_of(grads[...])
-
-
-GROUPS = ((0, 512), (512, 1024), (1024, 1536), (1536, RPAD))
 
 
 def update_kernel(
@@ -361,7 +360,7 @@
     negative_rows,
 ):
     core = lax.axis_index("core").astype(jnp.int32)[None]
-    id_array = kept((8, EPAD), jnp.int32)
+    id_array = kept((4, EPAD), jnp.int32)
     index_arrays = [
         array[0, 0] for array in (source_rows, target_rows, relation_ids, negative_rows)
     ]

time: 88.8 us -> 88.6 us (level)
  no operation moved by 1% of the time
where the time goes in v13:
time: 88.6 us; the launch traced here: 88.4 us
  blocking collectives  47.7 us (54%)
  Pallas kernels  25.4 us (29%)
  starting transfers between devices  14.3 us (16%)
  between operations  0.89 us (1%)
    pallas_call x11, Pallas kernels, call(): pl.pallas_call(kernel, out_shape=out_shape, in_specs=in_specs, out_specs=...  25.4 us
    all_to_all x1, blocking collectives, per_device(): got = lax.all_to_all(sent, CUBE, 0, 0, tiled=True)  19.6 us
    all_to_all x1, blocking collectives, per_device(): ours = lax.all_to_all(copies, CUBE, 0, 0, tiled=True)  17.1 us
    all_to_all x1, blocking collectives, per_device(): codes = lax.all_to_all(codes, 'z_hi', 0, 0, tiled=True)  11 us
    ppermute x2, starting transfers between devices, from_next(): lax.ppermute(block, BUCKET, [((i + 1) % count, i) for i in range(count)])  9.86 us
    ppermute x2, starting transfers between devices, swap_core(): return lax.ppermute(block, 'core', [(0, 1), (1, 0)])  4.4 us
  transfers between devices with their start and end apart: 4, of which 1 were waited for; matrix products, arithmetic and copies ran while one was open for 0% of the time, Pallas kernels for 18%

profile of v13, /device:TPU:1, one launch (start us, length us, event | category | flops | bytes accessed | tf_op | source)
XLA Modules:
  0.0 88.4 jit_solution(9799586910538643512)
XLA Ops:
  0.6 1.2 %prepare.1 = (s32[4,1024]{1,0:T(4,128)S(1)}, s32[4,1024]{1,0:T(4,128)S(1)}, bf16[400,512]{1,0:T(8,128)(2,1)S(1)}) custom-call(f32[400,512]{1,0:T(8,128)} %bitcast.18, s32[2,1000]{1,0:T(2,128)} %bitcast.20, s32[2,1000]{1,0:T(2,128)} %bitcast.21, s32[2,1000]{1,0:T(2,128)} %bitcast.22, s32[2,500]{1,0:T(2,128)} %bitcast.23), custom_call_target="tpu_custom_call" | custom-call | tf_op jit(solution)/shard_map/prepare/pallas_call | solution.py:56
  1.9 9.7 %collective-permute-start = (s32[4,1024]{1,0:T(4,128)S(1)}, s32[4,1024]{1,0:T(4,128)S(1)}, u32[]{:S(2)}, u32[]{:S(2)}) collective-permute-start(s32[4,1024]{1,0:T(4,128)S(1)} %get-tuple-element.29), channel_id=1, source_target_pairs={{4,0},{8,4},{12,8},{16,12},{20,16},{24,20},{28,24},{32,28},{36,32}... | collective-permute-start | bytes 49160 | tf_op jit(solution)/shard_map/ppermute | solution.py:70
  11.6 0.2 collective-permute-start.1
  11.7 9.4 %first.1 = (f32[400,512]{1,0:T(8,128)S(1)}, f32[1,512]{1,0:T(1,128)S(1)}, f32[2,200,2176]{2,1,0:T(8,128)S(1)}, bf16[400,2176]{1,0:T(8,128)(2,1)S(1)}) custom-call(bf16[400,512]{1,0:T(8,128)(2,1)S(1)} %get-tuple-element.30.left, s32[4,1024]{1,0:T(4,128)S(1)} %get-tuple-element.31.ids, f32[400,512]{1,0:T(8,128)} %bitcast.19, f32[1,512]{1,0:T(1,128)} %state_far.1, ...), custom_call_target="tpu_custom_call" | custom-call | tf_op jit(solution)/shard_map/first/pallas_call | solution.py:56
  21.2 0.0 collective-permute-done.ids
  21.2 2.7 %between.1 = (f32[400,1024]{1,0:T(8,128)S(1)}, bf16[400,512]{1,0:T(8,128)(2,1)S(1)}, f32[400,1024]{1,0:T(8,128)S(1)}) custom-call(f32[400,512]{1,0:T(8,128)S(1)} %get-tuple-element.33.slab, bf16[400,2176]{1,0:T(8,128)(2,1)S(1)} %get-tuple-element.34.table, s32[4,1024]{1,0:T(4,128)S(1)} %collective-permute-done.ids), custom_call_target="tpu_custom_call" | custom-call | flops 20000000000 | tf_op jit(solution)/shard_map/between/pallas_call | solution.py:56
  23.9 0.0 collective-permute-done.1.left
  23.9 4.0 %second.1 = (bf16[400,1024]{1,0:T(8,128)(2,1)S(1)}, bf16[512,1024]{1,0:T(8,128)(2,1)S(1)}, f32[1,1024]{1,0:T(1,128)S(1)}, bf16[2,200,1024]{2,1,0:T(8,128)(2,1)S(1)}, s16[32,104,128]{2,1,0:T(8,128)(2,1)S(1)}) custom-call(s32[1]{0:T(128)} %bitcast.core, bf16[400,512]{1,0:T(8,128)(2,1)S(1)} %collective-permute-done.1.left, ...), custom_call_target="tpu_custom_call" | custom-call | tf_op jit(solution)/shard_map/second/pallas_call | solution.py:56
  27.9 1.5 %collective-permute-start.2 = (s16[32,104,128]{2,1,0:T(8,128)(2,1)S(1)}, s16[32,104,128]{2,1,0:T(8,128)(2,1)S(1)}, u32[]{:S(2)}, u32[]{:S(2)}) collective-permute-start(s16[32,104,128]{2,1,0:T(8,128)(2,1)S(1)} %get-tuple-element.43), channel_id=1, source_target_pairs={{0,1},{1,0},{2,3},{3,2},{4,5},{5,4},{6,7},{7,6},{8,9},{9,8},{10,11... | collective-permute-start | bytes 2555912 | tf_op jit(solution)/shard_map/ppermute | solution.py:74
  29.4 2.1 %own_half.1 = (f32[200,2176]{1,0:T(8,128)S(1)}, bf16[400,1024]{1,0:T(8,128)(2,1)S(1)}, bf16[400,512]{1,0:T(8,128)(2,1)S(1)}) custom-call(s32[1]{0:T(128)} %bitcast.core, s32[4,1024]{1,0:T(4,128)S(1)} %collective-permute-done.ids, f32[2,200,2176]{2,1,0:T(8,128)S(1)} %get-tuple-element.32.rel_grad, bf16[2,200,1024]{2,1,0:T(8,128)(2,1)S(1)} %get-tuple-element.38.d_rel, ...), custom_call_target="tpu_custom_call" | custom-call | tf_op jit(solution)/shard_map/own_half/pallas_call | solution.py:56
  31.5 0.0 collective-permute-done.2.theirs
  31.5 0.8 send.1
  32.3 19.6 %all_to_all.15.parts = s16[32,104,128]{2,1,0:T(8,128)(2,1)S(1)} all-to-all(s16[32,104,128]{2,1,0:T(8,128)(2,1)S(1)} %send.1), channel_id=1, replica_groups=mesh['x'=4,'z_hi'=4,'z_lo'=2,'y_lo'=2,'y_hi'=2,'core'=2] {'x','z_lo','y_..., dimensions={0} | all-to-all | bytes 1703936 | tf_op jit(solution)/shard_map/all_to_all | solution.py:456
  51.9 0.3 gather.1
  52.3 11.0 %all_to_all.16.parts = s16[4,104,128]{2,1,0:T(8,128)(2,1)S(1)} all-to-all(s16[4,104,128]{2,1,0:T(8,128)(2,1)S(1)} %gather.1), channel_id=1, replica_groups=mesh['x'=4,'z_hi'=4,'z_lo'=2,'y_lo'=2,'y_hi'=2,'core'=2] {'z_hi'}, dimensions={0} | all-to-all | bytes 212992 | tf_op jit(solution)/shard_map/all_to_all | solution.py:459
  63.3 0.2 spread.1
  63.5 0.0 copy-start
  63.5 17.1 %all_to_all.17.codes = s16[32,104,128]{2,1,0:T(8,128)(2,1)S(1)} all-to-all(s16[32,104,128]{2,1,0:T(8,128)(2,1)S(1)} %spread.1), channel_id=1, replica_groups=mesh['x'=4,'z_hi'=4,'z_lo'=2,'y_lo'=2,'y_hi'=2,'core'=2] {'x','z_lo','y_..., dimensions={0} | all-to-all | bytes 1703936 | tf_op jit(solution)/shard_map/all_to_all | solution.py:461
  80.6 0.0 copy-start.1
  80.6 2.9 %collective-permute-start.3 = (s16[32,104,128]{2,1,0:T(8,128)(2,1)S(1)}, s16[32,104,128]{2,1,0:T(8,128)(2,1)S(1)}, u32[]{:S(2)}, u32[]{:S(2)}) collective-permute-start(s16[32,104,128]{2,1,0:T(8,128)(2,1)S(1)} %all_to_all.17.codes), channel_id=1, source_target_pairs={{0,1},{1,0},{2,3},{3,2},{4,5},{5,4},{6,7},{7,6},{8,9},{9,8},{10,11... | collective-permute-start | bytes 2555912 | tf_op jit(solution)/shard_map/ppermute | solution.py:74
  83.5 0.5 ours.1
  83.9 1.4 %target.1 = (f32[400,512]{1,0:T(8,128)S(1)}, f32[1,512]{1,0:T(1,128)}) custom-call(f32[1,2176]{1,0:T(1,128)S(1)} %get-tuple-element.45.after.squares, f32[400,512]{1,0:T(8,128)S(1)} %get-tuple-element.33.slab, f32[1,512]{1,0:T(1,128)S(1)} %get-tuple-element.46.state, s32[4,1024]{1,0:T(4,128)S(1)} %collective-permute-done.ids, ...), custom_call_target="tpu_custom_call" | custom-call | tf_op jit(solution)/shard_map/target/pallas_call | solution.py:56
  85.4 0.1 collective-permute-done.3.codes
  85.5 0.0 copy-done
  85.5 0.0 copy-done.1
  85.5 2.8 %update.1 = (f32[400,2066]{1,0:T(8,128)}, f32[400,512]{1,0:T(8,128)}, f32[2066]{0:T(1024)}) custom-call(s32[1]{0:T(128)} %bitcast.core, f32[200,2176]{1,0:T(8,128)S(1)} %get-tuple-element.44.ours, f32[1,2176]{1,0:T(1,128)S(1)} %get-tuple-element.45.after.squares, s16[32,104,128]{2,1,0:T(8,128)(2,1)S(1)} %collective-permute-done.3.codes, ...), custom_call_target="tpu_custom_call" | custom-call | tf_op jit(solution)/shard_map/update/pallas_call | solution.py:56
Async XLA Ops:
  1.9 19.3 %collective-permute-start = (s32[4,1024]{1,0:T(4,128)S(1)}, s32[4,1024]{1,0:T(4,128)S(1)}, u32[]{:S(2)}, u32[]{:S(2)}) collective-permute-start(s32[4,1024]{1,0:T(4,128)S(1)} %get-tuple-element.29), channel_id=1, source_target_pairs={{4,0},{8,4},{12,8},{16,12},{20,16},{24,20},{28,24},{32,28},{36,32}... | collective-permute-start | bytes 49160 | tf_op jit(solution)/shard_map/ppermute | solution.py:70
  11.6 12.3 %collective-permute-start.1 = (bf16[400,512]{1,0:T(8,128)(2,1)S(1)}, bf16[400,512]{1,0:T(8,128)(2,1)S(1)}, u32[]{:S(2)}, u32[]{:S(2)}) collective-permute-start(bf16[400,512]{1,0:T(8,128)(2,1)S(1)} %get-tuple-element.30.left), channel_id=1, source_target_pairs={{4,0},{8,4},{12,8},{16,12},{20,16},{24,20},{28,24},{32,28},{36,32}... | collective-permute-start | bytes 1228808 | tf_op jit(solution)/shard_map/ppermute | solution.py:70
  27.9 3.6 %collective-permute-start.2 = (s16[32,104,128]{2,1,0:T(8,128)(2,1)S(1)}, s16[32,104,128]{2,1,0:T(8,128)(2,1)S(1)}, u32[]{:S(2)}, u32[]{:S(2)}) collective-permute-start(s16[32,104,128]{2,1,0:T(8,128)(2,1)S(1)} %get-tuple-element.43), channel_id=1, source_target_pairs={{0,1},{1,0},{2,3},{3,2},{4,5},{5,4},{6,7},{7,6},{8,9},{9,8},{10,11... | collective-permute-start | bytes 2555912 | tf_op jit(solution)/shard_map/ppermute | solution.py:74
  63.5 22.0 %copy-start = (f32[2066,400]{0,1:T(8,128)S(1)}, f32[2066,400]{0,1:T(8,128)}, u32[]{:S(2)}) copy-start(f32[2066,400]{0,1:T(8,128)} %param.12) | copy-start | bytes 9916804
  80.6 4.9 %copy-start.1 = (f32[2066]{0:T(1024)S(1)}, f32[2066]{0:T(1024)}, u32[]{:S(2)}) copy-start(f32[2066]{0:T(1024)} %state.1) | copy-start | bytes 24796
  80.6 4.9 %collective-permute-start.3 = (s16[32,104,128]{2,1,0:T(8,128)(2,1)S(1)}, s16[32,104,128]{2,1,0:T(8,128)(2,1)S(1)}, u32[]{:S(2)}, u32[]{:S(2)}) collective-permute-start(s16[32,104,128]{2,1,0:T(8,128)(2,1)S(1)} %all_to_all.17.codes), channel_id=1, source_target_pairs={{0,1},{1,0},{2,3},{3,2},{4,5},{5,4},{6,7},{7,6},{8,9},{9,8},{10,11... | collective-permute-start | bytes 2555912 | tf_op jit(solution)/shard_map/ppermute | solution.py:74

commit v14 on v12

--- a/solution.py
+++ b/solution.py
@@ -270,10 +270,15 @@
     return total
 
 
-def gather_kernel(parts, codes):
-    code = encode(*summed(parts))
-    for copy in range(codes.shape[0]):
-        codes[copy] = code
+def gather_kernel(parts, code):
+    code[...] = encode(*summed(parts))
+
+
+def spread_kernel(a, b, c, d, copies):
+    rows = zip(*(decode(part[...]) for part in (a, b, c, d)))
+    code = encode(*((w + y) + (x + z) for w, x, y, z in rows))
+    for copy in range(OWNERS):
+        copies[copy] = code
 
 
 def decode_tile(codes, tile, grads, last):
@@ -456,9 +461,12 @@
     sent = call(send_kernel, parts, mine, theirs, name="send")
     got = lax.all_to_all(sent, CUBE, 0, 0, tiled=True)
     count = lax.axis_size("z_hi")
-    codes = call(gather_kernel, kept((count, *part), jnp.int16), got, name="gather")
-    codes = lax.all_to_all(codes, "z_hi", 0, 0, tiled=True)
-    copies = call(gather_kernel, parts, codes, name="spread")
+    codes = call(gather_kernel, kept(part, jnp.int16), got, name="gather")
+    ring = [
+        lax.ppermute(codes, "z_hi", [((i + k) % count, i) for i in range(count)])
+        for k in range(1, count)
+    ]
+    copies = call(spread_kernel, parts, codes, *ring, name="spread")
     ours = lax.all_to_all(copies, CUBE, 0, 0, tiled=True)
     theirs = swap_core(ours)
     grads, squares = call(

time: 88.8 us -> 86.9 us (0.979)
  blocking collectives: 48 us -> 37.8 us
  starting transfers between devices: 14.3 us -> 19.9 us
  waiting for transfers between devices: 0.13 us -> 2.83 us
    all_to_all x1 -> x0, blocking collectives: 11.3 us -> none  [per_device(): codes = lax.all_to_all(codes, 'z_hi', 0, 0, tiled=True)]
    ppermute x0 -> x3, starting transfers between devices: none -> 6.17 us  [per_device(): lax.ppermute(codes, 'z_hi', [((i + k) % count, i) for i in range(count)])]
    ppermute x0 -> x3, waiting for transfers between devices: none -> 2.71 us  [per_device(): lax.ppermute(codes, 'z_hi', [((i + k) % count, i) for i in range(count)])]
    all_to_all x1, blocking collectives: 17.1 us -> 18.1 us  [per_device(): ours = lax.all_to_all(copies, CUBE, 0, 0, tiled=True)]
  transfers between devices with their start and end apart: 4 -> 7, of which waited for: 1 -> 3; matrix products, arithmetic and copies ran while one was open for 0% -> 0% of each run, Pallas kernels for 18% -> 18%
where the time goes in v14:
time: 86.9 us; the launch traced here: 86.7 us
  blocking collectives  37.8 us (43%)
  Pallas kernels  25.3 us (29%)
  starting transfers between devices  19.9 us (23%)
  waiting for transfers between devices  2.83 us (3%)
  between operations  0.9 us (1%)
    pallas_call x11, Pallas kernels, call(): pl.pallas_call(kernel, out_shape=out_shape, in_specs=in_specs, out_specs=...  25.3 us
    all_to_all x1, blocking collectives, per_device(): got = lax.all_to_all(sent, CUBE, 0, 0, tiled=True)  19.6 us
    all_to_all x1, blocking collectives, per_device(): ours = lax.all_to_all(copies, CUBE, 0, 0, tiled=True)  18.1 us
    ppermute x2, starting transfers between devices, from_next(): lax.ppermute(block, BUCKET, [((i + 1) % count, i) for i in range(count)])  9.86 us
    ppermute x3, starting transfers between devices, per_device(): lax.ppermute(codes, 'z_hi', [((i + k) % count, i) for i in range(count)])  6.17 us
    ppermute x2, starting transfers between devices, swap_core(): return lax.ppermute(block, 'core', [(0, 1), (1, 0)])  3.82 us
    ppermute x3, waiting for transfers between devices, per_device(): lax.ppermute(codes, 'z_hi', [((i + k) % count, i) for i in range(count)])  2.71 us
  transfers between devices with their start and end apart: 7, of which 3 were waited for; matrix products, arithmetic and copies ran while one was open for 0% of the time, Pallas kernels for 18%

profile of v14, /device:TPU:1, one launch (start us, length us, event | category | flops | bytes accessed | tf_op | source)
XLA Modules:
  0.0 86.7 jit_solution(8169332567775186296)
XLA Ops:
  0.6 1.2 %prepare.1 = (s32[8,1024]{1,0:T(8,128)S(1)}, s32[8,1024]{1,0:T(8,128)S(1)}, bf16[400,512]{1,0:T(8,128)(2,1)S(1)}) custom-call(f32[400,512]{1,0:T(8,128)} %bitcast.18, s32[2,1000]{1,0:T(2,128)} %bitcast.20, s32[2,1000]{1,0:T(2,128)} %bitcast.21, s32[2,1000]{1,0:T(2,128)} %bitcast.22, s32[2,500]{1,0:T(2,128)} %bitcast.23), custom_call_target="tpu_custom_call" | custom-call | tf_op jit(solution)/shard_map/prepare/pallas_call | solution.py:56
  1.9 9.7 %collective-permute-start = (s32[8,1024]{1,0:T(8,128)S(1)}, s32[8,1024]{1,0:T(8,128)S(1)}, u32[]{:S(2)}, u32[]{:S(2)}) collective-permute-start(s32[8,1024]{1,0:T(8,128)S(1)} %get-tuple-element.29), channel_id=1, source_target_pairs={{4,0},{8,4},{12,8},{16,12},{20,16},{24,20},{28,24},{32,28},{36,32}... | collective-permute-start | bytes 98312 | tf_op jit(solution)/shard_map/ppermute | solution.py:70
  11.6 0.2 collective-permute-start.1
  11.7 9.4 %first.1 = (f32[400,512]{1,0:T(8,128)S(1)}, f32[1,512]{1,0:T(1,128)S(1)}, f32[2,200,2176]{2,1,0:T(8,128)S(1)}, bf16[400,2176]{1,0:T(8,128)(2,1)S(1)}) custom-call(bf16[400,512]{1,0:T(8,128)(2,1)S(1)} %get-tuple-element.30.left, s32[8,1024]{1,0:T(8,128)S(1)} %get-tuple-element.31.ids, f32[400,512]{1,0:T(8,128)} %bitcast.19, f32[1,512]{1,0:T(1,128)} %state_far.1, ...), custom_call_target="tpu_custom_call" | custom-call | tf_op jit(solution)/shard_map/first/pallas_call | solution.py:56
  21.1 0.0 collective-permute-done.ids
  21.1 2.7 %between.1 = (f32[400,1024]{1,0:T(8,128)S(1)}, bf16[400,512]{1,0:T(8,128)(2,1)S(1)}, f32[400,1024]{1,0:T(8,128)S(1)}) custom-call(f32[400,512]{1,0:T(8,128)S(1)} %get-tuple-element.33.slab, bf16[400,2176]{1,0:T(8,128)(2,1)S(1)} %get-tuple-element.34.table, s32[8,1024]{1,0:T(8,128)S(1)} %collective-permute-done.ids), custom_call_target="tpu_custom_call" | custom-call | flops 20000000000 | tf_op jit(solution)/shard_map/between/pallas_call | solution.py:56
  23.8 0.0 collective-permute-done.1.left
  23.8 4.0 %second.1 = (bf16[400,1024]{1,0:T(8,128)(2,1)S(1)}, bf16[512,1024]{1,0:T(8,128)(2,1)S(1)}, f32[1,1024]{1,0:T(1,128)S(1)}, bf16[2,200,1024]{2,1,0:T(8,128)(2,1)S(1)}, s16[32,104,128]{2,1,0:T(8,128)(2,1)S(1)}) custom-call(s32[1]{0:T(128)} %bitcast.core, bf16[400,512]{1,0:T(8,128)(2,1)S(1)} %collective-permute-done.1.left, ...), custom_call_target="tpu_custom_call" | custom-call | tf_op jit(solution)/shard_map/second/pallas_call | solution.py:56
  27.8 1.5 %collective-permute-start.2 = (s16[32,104,128]{2,1,0:T(8,128)(2,1)S(1)}, s16[32,104,128]{2,1,0:T(8,128)(2,1)S(1)}, u32[]{:S(2)}, u32[]{:S(2)}) collective-permute-start(s16[32,104,128]{2,1,0:T(8,128)(2,1)S(1)} %get-tuple-element.43), channel_id=1, source_target_pairs={{0,1},{1,0},{2,3},{3,2},{4,5},{5,4},{6,7},{7,6},{8,9},{9,8},{10,11... | collective-permute-start | bytes 2555912 | tf_op jit(solution)/shard_map/ppermute | solution.py:74
  29.3 2.1 %own_half.1 = (f32[200,2176]{1,0:T(8,128)S(1)}, bf16[400,1024]{1,0:T(8,128)(2,1)S(1)}, bf16[400,512]{1,0:T(8,128)(2,1)S(1)}) custom-call(s32[1]{0:T(128)} %bitcast.core, s32[8,1024]{1,0:T(8,128)S(1)} %collective-permute-done.ids, f32[2,200,2176]{2,1,0:T(8,128)S(1)} %get-tuple-element.32.rel_grad, bf16[2,200,1024]{2,1,0:T(8,128)(2,1)S(1)} %get-tuple-element.38.d_rel, ...), custom_call_target="tpu_custom_call" | custom-call | tf_op jit(solution)/shard_map/own_half/pallas_call | solution.py:56
  31.4 0.0 collective-permute-done.2.theirs
  31.4 0.8 send.1
  32.2 19.6 %all_to_all.10.parts = s16[32,104,128]{2,1,0:T(8,128)(2,1)S(1)} all-to-all(s16[32,104,128]{2,1,0:T(8,128)(2,1)S(1)} %send.1), channel_id=1, replica_groups=mesh['x'=4,'z_hi'=4,'z_lo'=2,'y_lo'=2,'y_hi'=2,'core'=2] {'x','z_lo','y_..., dimensions={0} | all-to-all | bytes 1703936 | tf_op jit(solution)/shard_map/all_to_all | solution.py:462
  51.9 0.3 gather.1.a
  52.2 0.1 collective-permute-start.5
  52.3 4.9 %collective-permute-start.4 = (s16[104,128]{1,0:T(8,128)(2,1)S(1)}, s16[104,128]{1,0:T(8,128)(2,1)S(1)}, u32[]{:S(2)}, u32[]{:S(2)}) collective-permute-start(s16[104,128]{1,0:T(8,128)(2,1)S(1)} %gather.1.a), channel_id=1, source_target_pairs={{32,0},{48,16},{0,32},{16,48},{33,1},{49,17},{1,33},{17,49},{34,2}... | collective-permute-start | bytes 79880 | tf_op jit(solution)/shard_map/ppermute | solution.py:466
  57.2 1.2 %collective-permute-start.3 = (s16[104,128]{1,0:T(8,128)(2,1)S(1)}, s16[104,128]{1,0:T(8,128)(2,1)S(1)}, u32[]{:S(2)}, u32[]{:S(2)}) collective-permute-start(s16[104,128]{1,0:T(8,128)(2,1)S(1)} %gather.1.a), channel_id=1, source_target_pairs={{16,0},{32,16},{48,32},{0,48},{17,1},{33,17},{49,33},{1,49},{18,2}... | collective-permute-start | bytes 79880 | tf_op jit(solution)/shard_map/ppermute | solution.py:466
  58.4 0.0 collective-permute-done.5.d
  58.4 0.6 collective-permute-done.4.c
  59.0 2.1 %collective-permute-done.3.b = s16[104,128]{1,0:T(8,128)(2,1)S(1)} collective-permute-done((s16[104,128]{1,0:T(8,128)(2,1)S(1)}, s16[104,128]{1,0:T(8,128)(2,1)S(1)}, u32[]{:S(2)}, u32[]{:S(2)}) %collective-permute-start.3) | collective-permute-done | bytes 26656 | tf_op jit(solution)/shard_map/ppermute | solution.py:466
  61.1 0.2 spread.1
  61.3 0.0 copy-start
  61.3 18.1 %all_to_all.11.codes = s16[32,104,128]{2,1,0:T(8,128)(2,1)S(1)} all-to-all(s16[32,104,128]{2,1,0:T(8,128)(2,1)S(1)} %spread.1), channel_id=1, replica_groups=mesh['x'=4,'z_hi'=4,'z_lo'=2,'y_lo'=2,'y_hi'=2,'core'=2] {'x','z_lo','y_..., dimensions={0} | all-to-all | bytes 1703936 | tf_op jit(solution)/shard_map/all_to_all | solution.py:470
  79.4 0.0 copy-start.1
  79.5 2.3 %collective-permute-start.6 = (s16[32,104,128]{2,1,0:T(8,128)(2,1)S(1)}, s16[32,104,128]{2,1,0:T(8,128)(2,1)S(1)}, u32[]{:S(2)}, u32[]{:S(2)}) collective-permute-start(s16[32,104,128]{2,1,0:T(8,128)(2,1)S(1)} %all_to_all.11.codes), channel_id=1, source_target_pairs={{0,1},{1,0},{2,3},{3,2},{4,5},{5,4},{6,7},{7,6},{8,9},{9,8},{10,11... | collective-permute-start | bytes 2555912 | tf_op jit(solution)/shard_map/ppermute | solution.py:74
  81.7 0.5 ours.1
  82.2 1.4 %target.1 = (f32[400,512]{1,0:T(8,128)S(1)}, f32[1,512]{1,0:T(1,128)}) custom-call(f32[1,2176]{1,0:T(1,128)S(1)} %get-tuple-element.45.after.squares, f32[400,512]{1,0:T(8,128)S(1)} %get-tuple-element.33.slab, f32[1,512]{1,0:T(1,128)S(1)} %get-tuple-element.46.state, s32[8,1024]{1,0:T(8,128)S(1)} %collective-permute-done.ids, ...), custom_call_target="tpu_custom_call" | custom-call | tf_op jit(solution)/shard_map/target/pallas_call | solution.py:56
  83.6 0.1 collective-permute-done.6.codes
  83.8 0.0 copy-done
  83.8 0.0 copy-done.1
  83.8 2.8 %update.1 = (f32[400,2066]{1,0:T(8,128)}, f32[400,512]{1,0:T(8,128)}, f32[2066]{0:T(1024)}) custom-call(s32[1]{0:T(128)} %bitcast.core, f32[200,2176]{1,0:T(8,128)S(1)} %get-tuple-element.44.ours, f32[1,2176]{1,0:T(1,128)S(1)} %get-tuple-element.45.after.squares, s16[32,104,128]{2,1,0:T(8,128)(2,1)S(1)} %collective-permute-done.6.codes, ...), custom_call_target="tpu_custom_call" | custom-call | tf_op jit(solution)/shard_map/update/pallas_call | solution.py:56
Async XLA Ops:
  1.9 19.2 %collective-permute-start = (s32[8,1024]{1,0:T(8,128)S(1)}, s32[8,1024]{1,0:T(8,128)S(1)}, u32[]{:S(2)}, u32[]{:S(2)}) collective-permute-start(s32[8,1024]{1,0:T(8,128)S(1)} %get-tuple-element.29), channel_id=1, source_target_pairs={{4,0},{8,4},{12,8},{16,12},{20,16},{24,20},{28,24},{32,28},{36,32}... | collective-permute-start | bytes 98312 | tf_op jit(solution)/shard_map/ppermute | solution.py:70
  11.6 12.3 %collective-permute-start.1 = (bf16[400,512]{1,0:T(8,128)(2,1)S(1)}, bf16[400,512]{1,0:T(8,128)(2,1)S(1)}, u32[]{:S(2)}, u32[]{:S(2)}) collective-permute-start(bf16[400,512]{1,0:T(8,128)(2,1)S(1)} %get-tuple-element.30.left), channel_id=1, source_target_pairs={{4,0},{8,4},{12,8},{16,12},{20,16},{24,20},{28,24},{32,28},{36,32}... | collective-permute-start | bytes 1228808 | tf_op jit(solution)/shard_map/ppermute | solution.py:70
  27.8 3.6 %collective-permute-start.2 = (s16[32,104,128]{2,1,0:T(8,128)(2,1)S(1)}, s16[32,104,128]{2,1,0:T(8,128)(2,1)S(1)}, u32[]{:S(2)}, u32[]{:S(2)}) collective-permute-start(s16[32,104,128]{2,1,0:T(8,128)(2,1)S(1)} %get-tuple-element.43), channel_id=1, source_target_pairs={{0,1},{1,0},{2,3},{3,2},{4,5},{5,4},{6,7},{7,6},{8,9},{9,8},{10,11... | collective-permute-start | bytes 2555912 | tf_op jit(solution)/shard_map/ppermute | solution.py:74
  52.2 6.2 %collective-permute-start.5 = (s16[104,128]{1,0:T(8,128)(2,1)S(1)}, s16[104,128]{1,0:T(8,128)(2,1)S(1)}, u32[]{:S(2)}, u32[]{:S(2)}) collective-permute-start(s16[104,128]{1,0:T(8,128)(2,1)S(1)} %gather.1.a), channel_id=1, source_target_pairs={{48,0},{0,16},{16,32},{32,48},{49,1},{1,17},{17,33},{33,49},{50,2}... | collective-permute-start | bytes 79880 | tf_op jit(solution)/shard_map/ppermute | solution.py:466
  52.3 6.7 %collective-permute-start.4 = (s16[104,128]{1,0:T(8,128)(2,1)S(1)}, s16[104,128]{1,0:T(8,128)(2,1)S(1)}, u32[]{:S(2)}, u32[]{:S(2)}) collective-permute-start(s16[104,128]{1,0:T(8,128)(2,1)S(1)} %gather.1.a), channel_id=1, source_target_pairs={{32,0},{48,16},{0,32},{16,48},{33,1},{49,17},{1,33},{17,49},{34,2}... | collective-permute-start | bytes 79880 | tf_op jit(solution)/shard_map/ppermute | solution.py:466
  57.2 3.9 %collective-permute-start.3 = (s16[104,128]{1,0:T(8,128)(2,1)S(1)}, s16[104,128]{1,0:T(8,128)(2,1)S(1)}, u32[]{:S(2)}, u32[]{:S(2)}) collective-permute-start(s16[104,128]{1,0:T(8,128)(2,1)S(1)} %gather.1.a), channel_id=1, source_target_pairs={{16,0},{32,16},{48,32},{0,48},{17,1},{33,17},{49,33},{1,49},{18,2}... | collective-permute-start | bytes 79880 | tf_op jit(solution)/shard_map/ppermute | solution.py:466
  61.3 22.5 %copy-start = (f32[2066,400]{0,1:T(8,128)S(1)}, f32[2066,400]{0,1:T(8,128)}, u32[]{:S(2)}) copy-start(f32[2066,400]{0,1:T(8,128)} %param.12) | copy-start | bytes 9916804
  79.4 4.3 %copy-start.1 = (f32[2066]{0:T(1024)S(1)}, f32[2066]{0:T(1024)}, u32[]{:S(2)}) copy-start(f32[2066]{0:T(1024)} %state.1) | copy-start | bytes 24796
  79.5 4.3 %collective-permute-start.6 = (s16[32,104,128]{2,1,0:T(8,128)(2,1)S(1)}, s16[32,104,128]{2,1,0:T(8,128)(2,1)S(1)}, u32[]{:S(2)}, u32[]{:S(2)}) collective-permute-start(s16[32,104,128]{2,1,0:T(8,128)(2,1)S(1)} %all_to_all.11.codes), channel_id=1, source_target_pairs={{0,1},{1,0},{2,3},{3,2},{4,5},{5,4},{6,7},{7,6},{8,9},{9,8},{10,11... | collective-permute-start | bytes 2555912 | tf_op jit(solution)/shard_map/ppermute | solution.py:74
